TPU v7x, 32 devices: a whole 2x2x4 slice. The times are simulated.
32 devices in a mesh: groups: 2 (over x), dev: 8 (over z, y), side: 2 (over core).
Axes of the slice: x: 2, y: 2, z: 4, core: 2. Of those that a mesh axis runs over, the one named last changes fastest.
Arguments:
- states: float32 [64, 16, 128, 128], P(('groups', 'dev', 'side')), parts along dimension 0, may hold values from -6 to 6
- swap_pairs: int32 [4, 2], P('groups'), parts along dimension 0, may hold values from 0 to 31, as said below
- token_counts: int32 [64], P(('groups', 'dev', 'side')), parts along dimension 0, may hold values from 1 to 16, 256 in all
- query_vectors: bfloat16 [64, 16, 2048], P(('groups', 'dev', 'side')), parts along dimension 0, may hold values from -6 to 6
- key_vectors: bfloat16 [64, 16, 2048], P(('groups', 'dev', 'side')), parts along dimension 0, may hold values from -6 to 6
- value_vectors: bfloat16 [64, 16, 2048], P(('groups', 'dev', 'side')), parts along dimension 0, may hold values from -6 to 6
- decay_log: float32 [64, 16, 2048], P(('groups', 'dev', 'side')), parts along dimension 0, may hold values from 0.003 to 0.4
- write_rate: float32 [64, 16, 16], P(('groups', 'dev', 'side')), parts along dimension 0, may hold values from 0.1 to 1
- hidden_rows: bfloat16 [64, 16, 2304], P(('groups', 'dev', 'side')), parts along dimension 0, may hold values from -6 to 6
- expert_ids: int32 [64, 16, 8], P(('groups', 'dev', 'side')), parts along dimension 0, may hold values from 0 to 15, all different within a row; in each aligned block of 16 rows (0 to 15, 16 to 31, ..., all dimensions but the last counted through in order) at most 16 rows name the same one
- route_weights: float32 [64, 16, 8], P(('groups', 'dev', 'side')), parts along dimension 0, may hold values from 0.05 to 0.3
- gate_up_weight: bfloat16 [16, 2304, 1024], P(('dev', 'side')), may hold values from -0.125 to 0.125
- down_weight: bfloat16 [16, 512, 2304], P(('dev', 'side')), may hold values from -0.25 to 0.25
Outputs:
- new_states: float32 [64, 16, 128, 128], P(('groups', 'dev', 'side')), parts along dimension 0
- attention_out: bfloat16 [64, 16, 2048], P(('groups', 'dev', 'side')), parts along dimension 0
- expert_out: bfloat16 [64, 16, 2304], P(('groups', 'dev', 'side')), parts along dimension 0
There are 2 independent parts, one for each index of `groups`. A program takes and returns all parts, laid end to end along the dimension named above; an argument that names none is the same for every part. Nothing has to cross between parts.
Inputs may be any that keep to these rules, and one draw needn't show every extreme that they name: `swap_pairs`: the 4 entries are distinct request slots; slots 0 and 31 are always among them. `token_counts`: the counts of all 32 slots sum to 256, and some slot has exactly 16. `expert_ids`: A token names 8 different experts. In each aligned block of 16 rows (tokens in slot order), no expert is named by more than 16 rows, a bound that some block reaches.
All inputs are finite; a program needn't handle non-finite values. No bound on the sum of `token_counts` on one device may be relied on, other than what follows from the above.
Results may differ from a plain program's by a relative error of at most 0.006.
Values may be sent and summed in bfloat16 or wider, within the bound.
No kernel may reach another device: no remote copies, remote signals or barrier semaphores. Data moves between devices by JAX's collectives and lax.ppermute only.
A program may use at most 64 MiB of HBM per device.

v0:
```python
import jax
import jax.numpy as jnp
from jax import lax
from jax.sharding import PartitionSpec as P

D = 2304
FF = 512
H = 16
DK = 128
DV = 128
TOP = 8
T_MAX = 16
MICRO = 2


def normalize(vectors, local_reqs):
    widened = vectors.astype(jnp.float32).reshape(local_reqs, T_MAX, H, DK)
    return widened / jnp.sqrt(jnp.sum(widened * widened, axis=-1, keepdims=True) + 1e-06)


def advance(carried, inputs):
    query_now, key_now, value_now, retention_now, rate_now, active = inputs
    decayed = carried * retention_now[..., None]
    predicted = jnp.einsum("rhkv,rhk->rhv", decayed, key_now, precision=lax.Precision.HIGHEST)
    updated = (
        decayed
        + rate_now[..., None, None] * key_now[..., None] * (value_now - predicted)[:, :, None, :]
    )
    output = jnp.einsum("rhkv,rhk->rhv", updated, query_now, precision=lax.Precision.HIGHEST)
    carried = jnp.where(active[:, None, None, None], updated, carried)
    output = jnp.where(active[:, None, None], output, jnp.zeros_like(output))
    return (carried, output)


def slot_layout(route_ids, weights, expert_count, capacity, block_rows):
    flat_ids = route_ids.reshape(-1)
    onehot = (flat_ids[:, None] == jnp.arange(expert_count, dtype=jnp.int32)[None, :]).astype(
        jnp.int32
    )
    before = jnp.cumsum(onehot, axis=0) - onehot
    order_in = jnp.sum(before * onehot, axis=1)
    slot_ids = flat_ids * capacity + order_in
    slot_table = (
        slot_ids[:, None] == jnp.arange(expert_count * capacity, dtype=jnp.int32)[None, :]
    ).astype(jnp.float32)
    slot_table = slot_table.reshape(block_rows, TOP, expert_count * capacity)
    placing = jnp.sum(slot_table, axis=1)
    mixing = jnp.sum(slot_table * weights[:, :, None], axis=1)
    return (placing, mixing)


def per_device(
    states,
    swap_pairs,
    token_counts,
    query_vectors,
    key_vectors,
    value_vectors,
    decay_log,
    write_rate,
    hidden_rows,
    expert_ids,
    route_weights,
    gate_up_weight,
    down_weight,
):
    local_reqs = states.shape[0]
    dev_count = lax.axis_size("dev")
    side_count = lax.axis_size("side")
    peer_count = dev_count * side_count
    position = lax.axis_index(("dev", "side"))
    first_slot = position * local_reqs
    wanted = swap_pairs.reshape(-1)
    partner = swap_pairs[:, ::-1].reshape(-1)
    offsets = wanted - first_slot
    is_owned = (offsets >= 0) & (offsets < local_reqs)
    picked = states[jnp.clip(offsets, 0, local_reqs - 1)]
    outgoing = jnp.where(is_owned[:, None, None, None], picked, jnp.zeros_like(picked))
    moved_states = lax.psum(outgoing, ("dev", "side"))
    my_slots = first_slot + jnp.arange(local_reqs, dtype=jnp.int32)
    matches = my_slots[:, None] == partner[None, :]
    has_match = jnp.any(matches, axis=1)
    source_pick = jnp.sum(
        jnp.where(matches, jnp.arange(partner.shape[0], dtype=jnp.int32)[None, :], 0), axis=1
    )
    migrated = jnp.where(has_match[:, None, None, None], moved_states[source_pick], states)
    queries = normalize(query_vectors, local_reqs)
    unit_keys = normalize(key_vectors, local_reqs)
    value_rows = value_vectors.astype(jnp.float32).reshape(local_reqs, T_MAX, H, DV)
    retention = jnp.exp(-decay_log).reshape(local_reqs, T_MAX, H, DK)
    times_now = jnp.arange(T_MAX, dtype=jnp.int32)
    active = times_now[:, None] < token_counts[None, :]
    inputs = (
        jnp.moveaxis(queries, 1, 0),
        jnp.moveaxis(unit_keys, 1, 0),
        jnp.moveaxis(value_rows, 1, 0),
        jnp.moveaxis(retention, 1, 0),
        jnp.moveaxis(write_rate, 1, 0),
        active,
    )
    final_states, outputs = lax.scan(advance, migrated, inputs)
    attention_out = (
        jnp.moveaxis(outputs, 0, 1).reshape(local_reqs, T_MAX, H * DV).astype(jnp.bfloat16)
    )
    row_total = local_reqs * T_MAX
    block_rows = row_total // MICRO
    capacity = max(2, 2 * block_rows * TOP // peer_count)
    rows_flat = hidden_rows.reshape(row_total, D)
    route_flat = expert_ids.reshape(row_total, TOP)
    weight_flat = route_weights.reshape(row_total, TOP)

    def compute_rows(arrived):
        width_now = arrived.shape[1]
        stacked = arrived.reshape(-1, D)
        gate_up = jnp.dot(stacked, gate_up_weight[0], preferred_element_type=jnp.float32)
        activated = (jax.nn.silu(gate_up[:, :FF]) * gate_up[:, FF:]).astype(jnp.bfloat16)
        produced = jnp.dot(activated, down_weight[0], preferred_element_type=jnp.float32).astype(
            jnp.bfloat16
        )
        return produced.reshape(peer_count, width_now, D)

    def through_experts(outbound):
        width_now = outbound.shape[1]
        return lax.all_to_all(
            compute_rows(
                lax.all_to_all(outbound, ("dev", "side"), split_axis=0, concat_axis=0, tiled=True)
            ),
            ("dev", "side"),
            split_axis=0,
            concat_axis=0,
            tiled=True,
        )

    outbound_list = []
    mixing_list = []
    for batch_index in range(MICRO):
        lower = batch_index * block_rows
        placing, mixing = slot_layout(
            route_flat[lower : lower + block_rows],
            weight_flat[lower : lower + block_rows],
            peer_count,
            capacity,
            block_rows,
        )
        outbound = jnp.dot(
            placing.T.astype(jnp.bfloat16),
            rows_flat[lower : lower + block_rows],
            preferred_element_type=jnp.float32,
        ).astype(jnp.bfloat16)
        outbound_list.append(outbound.reshape(peer_count, capacity, D))
        mixing_list.append(mixing)
    returned_list = [through_experts(outbound) for outbound in outbound_list]
    combined = []
    for batch_index in range(MICRO):
        produced_rows = (
            returned_list[batch_index].reshape(peer_count * capacity, D).astype(jnp.float32)
        )
        combined.append(
            jnp.dot(mixing_list[batch_index], produced_rows, precision=lax.Precision.HIGHEST)
        )
    expert_out = (
        jnp.concatenate(combined, axis=0).reshape(local_reqs, T_MAX, D).astype(jnp.bfloat16)
    )
    return (final_states, attention_out, expert_out)


def solution(mesh):
    in_specs = (
        P(("groups", "dev", "side"), None, None, None),
        P("groups", None),
        P(("groups", "dev", "side")),
        P(("groups", "dev", "side"), None, None),
        P(("groups", "dev", "side"), None, None),
        P(("groups", "dev", "side"), None, None),
        P(("groups", "dev", "side"), None, None),
        P(("groups", "dev", "side"), None, None),
        P(("groups", "dev", "side"), None, None),
        P(("groups", "dev", "side"), None, None),
        P(("groups", "dev", "side"), None, None),
        P(("dev", "side"), None, None),
        P(("dev", "side"), None, None),
    )
    out_specs = (
        P(("groups", "dev", "side"), None, None, None),
        P(("groups", "dev", "side"), None, None),
        P(("groups", "dev", "side"), None, None),
    )
    return jax.shard_map(
        per_device, mesh=mesh, in_specs=in_specs, out_specs=out_specs, check_vma=False
    )
```

profile of v0, /device:TPU:0, one launch (start us, length us, event | category | flops | bytes accessed | tf_op | source)
XLA Modules:
  0.0 442.1 jit_solution(3409283563657411826)
XLA Ops:
  14.9 7.4 %all-to-all-start.2 = ((bf16[16,16,2304]{2,1,0:T(8,128)(2,1)}), bf16[16,16,2304]{2,1,0:T(8,128)(2,1)S(1)}, u32[]{:S(2)}, u32[]{:S(2)}) async-start(bf16[16,16,2304]{2,1,0:T(8,128)(2,1)} %bitcast.36), calls=%async_computation.2 | async-start | bytes 2359296 | tf_op jit(solution)/shard_map/all_to_all | solution.py:126
  28.6 4.5 %gather_fusion = f32[4,16,128,128]{3,2,1,0:T(8,128)} fusion(f32[2,16,128,128]{3,2,1,0:T(8,128)} %param.15, s32[1024]{0:T(1024)} %pad_clamp_fusion.1), kind=kCustom, calls=%fused_computation | custom fusion | bytes 8388624 | tf_op jit(solution)/shard_map/gather | solution.py:77
  33.1 4.9 %broadcast_select_fusion = f32[4,16,128,128]{3,2,1,0:T(8,128)} fusion(f32[4,16,128,128]{3,2,1,0:T(8,128)} %gather_fusion, pred[4]{0:T(512)(128)(4,1)} %and.13), kind=kLoop, calls=%fused_computation.33 | loop fusion | flops 1048576 | bytes 8388612 | tf_op jit(solution)/shard_map/jit(_where)/select_n | solution.py:78
  44.6 2.9 all-to-all-done.2
  47.5 11.5 %all-to-all-start = ((bf16[16,16,2304]{2,1,0:T(8,128)(2,1)}), bf16[16,16,2304]{2,1,0:T(8,128)(2,1)}, u32[]{:S(2)}, u32[]{:S(2)}) async-start(bf16[16,16,2304]{2,1,0:T(8,128)(2,1)} %bitcast.27), calls=%async_computation | async-start | bytes 2359296 | tf_op jit(solution)/shard_map/all_to_all | solution.py:126
  75.9 3.7 fusion.10
  81.6 14.9 %all-to-all-done = bf16[16,16,2304]{2,1,0:T(8,128)(2,1)} async-done(((bf16[16,16,2304]{2,1,0:T(8,128)(2,1)}), bf16[16,16,2304]{2,1,0:T(8,128)(2,1)}, u32[]{:S(2)}, u32[]{:S(2)}) %all-to-all-start) | async-done | bytes 1179680 | tf_op jit(solution)/shard_map/all_to_all | solution.py:126
  96.4 8.1 %all-to-all-start.3 = ((bf16[16,16,2304]{2,1,0:T(8,128)(2,1)}), bf16[16,16,2304]{2,1,0:T(8,128)(2,1)S(1)}, u32[]{:S(2)}, u32[]{:S(2)}) async-start(bf16[16,16,2304]{2,1,0:T(8,128)(2,1)} %bitcast.168), calls=%async_computation.3 | async-start | bytes 2359296 | tf_op jit(solution)/shard_map/all_to_all | solution.py:124
  111.2 78.0 %all-reduce.2.cloned.1.call-done = f32[4,16,128,128]{3,2,1,0:T(8,128)} async-done(((f32[4,16,128,128]{3,2,1,0:T(8,128)}), f32[4,16,128,128]{3,2,1,0:T(8,128)}) %all-reduce.2.cloned.1.call-update) | async-done | bytes 4194320 | tf_op jit(solution)/shard_map/psum | solution.py:79
  189.2 4.3 gather_fusion.1
  193.5 3.9 broadcast_select_fusion.1
  197.4 4.1 fusion.12
  203.4 4.6 %all-to-all-start.1 = ((bf16[16,16,2304]{2,1,0:T(8,128)(2,1)}), bf16[16,16,2304]{2,1,0:T(8,128)(2,1)}, u32[]{:S(2)}, u32[]{:S(2)}) async-start(bf16[16,16,2304]{2,1,0:T(8,128)(2,1)} %bitcast.167), calls=%async_computation.1 | async-start | bytes 2359296 | tf_op jit(solution)/shard_map/all_to_all | solution.py:124
  208.0 219.4 %while.12 = (s32[]{:T(128)}, f32[2,16,128,128]{3,2,1,0:T(8,128)}, bf16[16,2,16,128]{3,2,1,0:T(8,128)(2,1)}, pred[16,2]{1,0:T(8,128)(4,1)}, f32[16,2,16,128]{3,2,...) while((s32[]{:T(128)}, f32[2,16,128,128]{3,2,1,0:T(8,128)}, ...), condition=%wide.region_6.7_spmd, body=%wide.region_5.6_spmd.sunk | while | flops 16789504 | bytes 25535048 | solution.py:101
  211.1 3.7 fusion.64
  215.5 2.8 fusion.67
  224.8 3.7 fusion.64
  238.5 3.7 fusion.64
  242.9 2.8 fusion.67
  252.2 3.7 fusion.64
  265.9 3.7 fusion.64
  279.7 3.7 fusion.64
  293.4 3.7 fusion.64
  307.1 3.7 fusion.64
  320.8 3.7 fusion.64
  334.5 3.7 fusion.64
  348.2 3.7 fusion.64
  361.9 3.7 fusion.64
  375.6 3.7 fusion.64
  389.4 3.7 fusion.64
  403.1 3.7 fusion.64
  416.8 3.7 fusion.64
  (275 shorter events, 210.5 us)
Async XLA Ops:
  7.2 72.5 %copy-start = (bf16[1,512,2304]{2,1,0:T(8,128)(2,1)S(1)}, bf16[1,512,2304]{2,1,0:T(8,128)(2,1)}, u32[]{:S(2)}) copy-start(bf16[1,512,2304]{2,1,0:T(8,128)(2,1)} %param.27) | copy-start | bytes 7077892
  14.9 32.6 %all-to-all-start.2 = ((bf16[16,16,2304]{2,1,0:T(8,128)(2,1)}), bf16[16,16,2304]{2,1,0:T(8,128)(2,1)S(1)}, u32[]{:S(2)}, u32[]{:S(2)}) async-start(bf16[16,16,2304]{2,1,0:T(8,128)(2,1)} %bitcast.36), calls=%async_computation.2 | async-start | bytes 2359296 | tf_op jit(solution)/shard_map/all_to_all | solution.py:126
  22.3 166.9 %all-reduce.2.cloned.1.call-start = ((), (), s32[]{:S(2)}) async-start(), calls=%async_computation.4 | async-start | bytes 8388608 | tf_op jit(solution)/shard_map/psum | solution.py:79
  47.5 49.0 %all-to-all-start = ((bf16[16,16,2304]{2,1,0:T(8,128)(2,1)}), bf16[16,16,2304]{2,1,0:T(8,128)(2,1)}, u32[]{:S(2)}, u32[]{:S(2)}) async-start(bf16[16,16,2304]{2,1,0:T(8,128)(2,1)} %bitcast.27), calls=%async_computation | async-start | bytes 2359296 | tf_op jit(solution)/shard_map/all_to_all | solution.py:126
  63.0 1.9 copy-start.3
  64.0 1.7 copy-start.4
  96.4 107.0 %all-to-all-start.3 = ((bf16[16,16,2304]{2,1,0:T(8,128)(2,1)}), bf16[16,16,2304]{2,1,0:T(8,128)(2,1)S(1)}, u32[]{:S(2)}, u32[]{:S(2)}) async-start(bf16[16,16,2304]{2,1,0:T(8,128)(2,1)} %bitcast.168), calls=%async_computation.3 | async-start | bytes 2359296 | tf_op jit(solution)/shard_map/all_to_all | solution.py:124
  203.4 228.4 %all-to-all-start.1 = ((bf16[16,16,2304]{2,1,0:T(8,128)(2,1)}), bf16[16,16,2304]{2,1,0:T(8,128)(2,1)}, u32[]{:S(2)}, u32[]{:S(2)}) async-start(bf16[16,16,2304]{2,1,0:T(8,128)(2,1)} %bitcast.167), calls=%async_computation.1 | async-start | bytes 2359296 | tf_op jit(solution)/shard_map/all_to_all | solution.py:124
  208.0 7.5 %copy-start.1 = (f32[2,16,128,128]{3,2,1,0:T(8,128)S(1)}, f32[2,16,128,128]{3,2,1,0:T(8,128)}, u32[]{:S(2)}) copy-start(f32[2,16,128,128]{3,2,1,0:T(8,128)} %get-tuple-element.157) | copy-start | bytes 6291460 | tf_op jit(solution)/shard_map/while
  220.4 1.3 copy-start.2
  221.8 7.5 %copy-start.1 = (f32[2,16,128,128]{3,2,1,0:T(8,128)S(1)}, f32[2,16,128,128]{3,2,1,0:T(8,128)}, u32[]{:S(2)}) copy-start(f32[2,16,128,128]{3,2,1,0:T(8,128)} %get-tuple-element.157) | copy-start | bytes 6291460 | tf_op jit(solution)/shard_map/while
  234.1 1.3 copy-start.2
  235.5 7.5 %copy-start.1 = (f32[2,16,128,128]{3,2,1,0:T(8,128)S(1)}, f32[2,16,128,128]{3,2,1,0:T(8,128)}, u32[]{:S(2)}) copy-start(f32[2,16,128,128]{3,2,1,0:T(8,128)} %get-tuple-element.157) | copy-start | bytes 6291460 | tf_op jit(solution)/shard_map/while
  247.8 1.3 copy-start.2
  249.2 7.5 %copy-start.1 = (f32[2,16,128,128]{3,2,1,0:T(8,128)S(1)}, f32[2,16,128,128]{3,2,1,0:T(8,128)}, u32[]{:S(2)}) copy-start(f32[2,16,128,128]{3,2,1,0:T(8,128)} %get-tuple-element.157) | copy-start | bytes 6291460 | tf_op jit(solution)/shard_map/while
  261.6 1.3 copy-start.2
  262.9 7.5 %copy-start.1 = (f32[2,16,128,128]{3,2,1,0:T(8,128)S(1)}, f32[2,16,128,128]{3,2,1,0:T(8,128)}, u32[]{:S(2)}) copy-start(f32[2,16,128,128]{3,2,1,0:T(8,128)} %get-tuple-element.157) | copy-start | bytes 6291460 | tf_op jit(solution)/shard_map/while
  275.3 1.3 copy-start.2
  276.6 7.5 %copy-start.1 = (f32[2,16,128,128]{3,2,1,0:T(8,128)S(1)}, f32[2,16,128,128]{3,2,1,0:T(8,128)}, u32[]{:S(2)}) copy-start(f32[2,16,128,128]{3,2,1,0:T(8,128)} %get-tuple-element.157) | copy-start | bytes 6291460 | tf_op jit(solution)/shard_map/while
  289.0 1.3 copy-start.2
  290.3 7.5 %copy-start.1 = (f32[2,16,128,128]{3,2,1,0:T(8,128)S(1)}, f32[2,16,128,128]{3,2,1,0:T(8,128)}, u32[]{:S(2)}) copy-start(f32[2,16,128,128]{3,2,1,0:T(8,128)} %get-tuple-element.157) | copy-start | bytes 6291460 | tf_op jit(solution)/shard_map/while
  304.0 7.5 %copy-start.1 = (f32[2,16,128,128]{3,2,1,0:T(8,128)S(1)}, f32[2,16,128,128]{3,2,1,0:T(8,128)}, u32[]{:S(2)}) copy-start(f32[2,16,128,128]{3,2,1,0:T(8,128)} %get-tuple-element.157) | copy-start | bytes 6291460 | tf_op jit(solution)/shard_map/while
  317.7 7.5 %copy-start.1 = (f32[2,16,128,128]{3,2,1,0:T(8,128)S(1)}, f32[2,16,128,128]{3,2,1,0:T(8,128)}, u32[]{:S(2)}) copy-start(f32[2,16,128,128]{3,2,1,0:T(8,128)} %get-tuple-element.157) | copy-start | bytes 6291460 | tf_op jit(solution)/shard_map/while
  331.4 7.5 %copy-start.1 = (f32[2,16,128,128]{3,2,1,0:T(8,128)S(1)}, f32[2,16,128,128]{3,2,1,0:T(8,128)}, u32[]{:S(2)}) copy-start(f32[2,16,128,128]{3,2,1,0:T(8,128)} %get-tuple-element.157) | copy-start | bytes 6291460 | tf_op jit(solution)/shard_map/while
  345.2 7.5 %copy-start.1 = (f32[2,16,128,128]{3,2,1,0:T(8,128)S(1)}, f32[2,16,128,128]{3,2,1,0:T(8,128)}, u32[]{:S(2)}) copy-start(f32[2,16,128,128]{3,2,1,0:T(8,128)} %get-tuple-element.157) | copy-start | bytes 6291460 | tf_op jit(solution)/shard_map/while
  358.9 7.5 %copy-start.1 = (f32[2,16,128,128]{3,2,1,0:T(8,128)S(1)}, f32[2,16,128,128]{3,2,1,0:T(8,128)}, u32[]{:S(2)}) copy-start(f32[2,16,128,128]{3,2,1,0:T(8,128)} %get-tuple-element.157) | copy-start | bytes 6291460 | tf_op jit(solution)/shard_map/while
  372.6 7.5 %copy-start.1 = (f32[2,16,128,128]{3,2,1,0:T(8,128)S(1)}, f32[2,16,128,128]{3,2,1,0:T(8,128)}, u32[]{:S(2)}) copy-start(f32[2,16,128,128]{3,2,1,0:T(8,128)} %get-tuple-element.157) | copy-start | bytes 6291460 | tf_op jit(solution)/shard_map/while
  386.3 7.5 %copy-start.1 = (f32[2,16,128,128]{3,2,1,0:T(8,128)S(1)}, f32[2,16,128,128]{3,2,1,0:T(8,128)}, u32[]{:S(2)}) copy-start(f32[2,16,128,128]{3,2,1,0:T(8,128)} %get-tuple-element.157) | copy-start | bytes 6291460 | tf_op jit(solution)/shard_map/while
  398.7 1.3 copy-start.2
  400.0 7.5 %copy-start.1 = (f32[2,16,128,128]{3,2,1,0:T(8,128)S(1)}, f32[2,16,128,128]{3,2,1,0:T(8,128)}, u32[]{:S(2)}) copy-start(f32[2,16,128,128]{3,2,1,0:T(8,128)} %get-tuple-element.157) | copy-start | bytes 6291460 | tf_op jit(solution)/shard_map/while
  413.7 7.5 %copy-start.1 = (f32[2,16,128,128]{3,2,1,0:T(8,128)S(1)}, f32[2,16,128,128]{3,2,1,0:T(8,128)}, u32[]{:S(2)}) copy-start(f32[2,16,128,128]{3,2,1,0:T(8,128)} %get-tuple-element.157) | copy-start | bytes 6291460 | tf_op jit(solution)/shard_map/while
  426.1 1.3 copy-start.2
  (8 other events, 10.6 us)
Sparse Core Ops, SparseCore 0:
  38.1 151.0 all-reduce.1
where the time goes:
time: 450 us; the launch traced here: 442 us
  matrix products  123 us (27%)
  waiting for transfers between devices  95.7 us (21%)
  other arithmetic  90.6 us (20%)
  local copies, waits for them, and re-layouts  86.6 us (19%)
  starting transfers between devices  31.6 us (7%)
  between operations  14.2 us (3%)
    psum x1, waiting for transfers between devices, per_device(): moved_states = lax.psum(outgoing, ('dev', 'side'))  78 us
    dot_general x16, matrix products, advance(): jnp.einsum('rhkv,rhk->rhv', decayed, key_now, precision=lax.Precision.HIG...  58.7 us
    dot_general x16, matrix products, advance(): jnp.einsum('rhkv,rhk->rhv', updated, query_now, precision=lax.Precision.H...  44.8 us
    select_n x16, other arithmetic, advance(): carried = jnp.where(active[:, None, None, None], updated, carried)  23.7 us
    all_to_all x2, starting transfers between devices, through_experts(): lax.all_to_all(outbound, ('dev', 'side'), split_axis=0, concat_axis=0, ti...  18.9 us
    all_to_all x2, waiting for transfers between devices, through_experts(): lax.all_to_all(outbound, ('dev', 'side'), split_axis=0, concat_axis=0, ti...  17.8 us
    dynamic_slice x16, local copies, waits for them, and re-layouts, per_device(): final_states, outputs = lax.scan(advance, migrated, inputs)  13.9 us
    all_to_all x2, starting transfers between devices, through_experts(): lax.all_to_all(compute_rows(lax.all_to_all(outbound, ('dev', 'side'), spl...  12.6 us
  transfers between devices with their start and end apart: 5, of which 3 were waited for; matrix products, arithmetic and copies ran while one was open for 63% of the time, Pallas kernels for 0%

commit v1 on v0

v1 whole, which is shorter than its diff:
```python
import functools

import jax
import jax.numpy as jnp
from jax import lax
from jax.experimental import pallas as pl
from jax.experimental.pallas import tpu as pltpu
from jax.sharding import PartitionSpec as P

D = 2304
FF = 512
H = 16
DK = 128
DV = 128
TOP = 8
T_MAX = 16
AXES = ("dev", "side")
HIGHEST = lax.Precision.HIGHEST
VMEM_LIMIT = 48 * 1024 * 1024


def dot_nt(a, b):
    return lax.dot_general(
        a, b, (((1,), (1,)), ((), ())), precision=HIGHEST, preferred_element_type=jnp.float32
    )


def dot_nn(a, b):
    return lax.dot_general(
        a, b, (((1,), (0,)), ((), ())), precision=HIGHEST, preferred_element_type=jnp.float32
    )


def dot_tn(a, b):
    return lax.dot_general(
        a, b, (((0,), (0,)), ((), ())), precision=HIGHEST, preferred_element_type=jnp.float32
    )


def pack_kernel(scalars, states_ref, send_ref, keep_ref):
    for out_ref, base in ((send_ref, 1), (keep_ref, 3)):
        for member in range(2):
            slot = scalars[base + member]
            value = jnp.zeros(states_ref.shape[2:], jnp.float32)
            for r in range(states_ref.shape[0]):
                value = jnp.where(slot == r, states_ref[r, 0], value)
            out_ref[0, member] = value.astype(jnp.bfloat16)


def unit(vectors):
    return vectors * lax.rsqrt(jnp.sum(vectors * vectors, axis=-1, keepdims=True) + 1e-06)


def prep_kernel(counts, q_ref, k_ref, v_ref, decay_ref, rate_ref, z_ref, uo_ref, dg_ref):
    r = pl.program_id(0)
    count = counts[r]
    times = lax.broadcasted_iota(jnp.int32, (T_MAX, 1), 0)
    live = (times < count).astype(jnp.float32)
    rows = lax.broadcasted_iota(jnp.int32, (T_MAX, T_MAX), 0)
    cols = lax.broadcasted_iota(jnp.int32, (T_MAX, T_MAX), 1)
    lower = (cols <= rows).astype(jnp.float32)
    decay = decay_ref[0] * live
    total = dot_nn(lower, decay)
    rates = rate_ref[0] * live
    for h in range(q_ref.shape[2] // DK):
        lanes = slice(h * DK, (h + 1) * DK)
        cum = total[:, lanes]
        grown = jnp.exp(-cum)
        key = unit(k_ref[0, :, lanes].astype(jnp.float32))
        query = unit(q_ref[0, :, lanes].astype(jnp.float32)) * live
        value = v_ref[0, :, lanes].astype(jnp.float32)
        rate = rates[:, h : h + 1]
        key_in = key * grown
        query_in = query * grown
        key_out = key * jnp.exp(cum)
        gram = dot_nt(jnp.concatenate([key_in, query_in], axis=0), key_out)
        mix = jnp.where(cols < rows, gram[:T_MAX], 0.0) * rate
        read = jnp.where(cols <= rows, gram[T_MAX:], 0.0)
        solved = jnp.concatenate([value, key_in], axis=1) * rate
        for s in range(T_MAX - 1):
            solved = solved - mix[:, s : s + 1] * solved[s : s + 1, :]
        seen = dot_nn(read, solved)
        z_ref[0, h, :T_MAX] = solved[:, DV:]
        z_ref[0, h, T_MAX:] = query_in - seen[:, DV:]
        uo_ref[0, h, :T_MAX] = solved[:, :DV]
        uo_ref[0, h, T_MAX:] = seen[:, :DV]
        last = cum[T_MAX - 1 : T_MAX]
        dg_ref[0, h, :T_MAX] = key * jnp.exp(cum - last)
        dg_ref[0, h, T_MAX:] = jnp.broadcast_to(jnp.exp(-last), (8, DK))


def finish_kernel(pieces, heads, scalars, states_ref, *refs):
    mine = refs[:pieces]
    other = refs[pieces : 2 * pieces]
    z_ref, uo_ref, dg_ref, new_ref, out_ref = refs[2 * pieces :]
    r = pl.program_id(0)
    base = 1 + 3 * r
    moved = scalars[base] > 0
    is_other = scalars[base + 1] > 0

    def whole(parts):
        parts = [part[0, 0] for part in parts]
        return parts[0] if pieces == 1 else jnp.concatenate(parts, axis=0)

    arrived = jnp.where(is_other, whole(other).astype(jnp.float32), whole(mine).astype(jnp.float32))
    for h in range(heads):
        state = jnp.where(moved, arrived[h * DK : (h + 1) * DK], states_ref[0, h])
        both = dot_nn(z_ref[0, h], state)
        writes = uo_ref[0, h, :T_MAX] - both[:T_MAX]
        read = uo_ref[0, h, T_MAX:] + both[T_MAX:]
        out_ref[0, :, h * DV : (h + 1) * DV] = read.astype(out_ref.dtype)
        turned = jnp.transpose(dg_ref[0, h, T_MAX:])
        new_ref[0, h] = turned[:, :1] * state + dot_tn(dg_ref[0, h, :T_MAX], writes)


def per_device(
    states,
    swap_pairs,
    token_counts,
    query_vectors,
    key_vectors,
    value_vectors,
    decay_log,
    write_rate,
    hidden_rows,
    expert_ids,
    route_weights,
    gate_up_weight,
    down_weight,
):
    local_reqs = states.shape[0]
    dev_count = lax.axis_size("dev")
    side_count = lax.axis_size("side")
    peer_count = dev_count * side_count
    position = lax.axis_index(AXES)
    side = lax.axis_index("side")
    dev = lax.axis_index("dev")
    inner = 2
    outer = dev_count // inner
    f32, bf16 = jnp.float32, jnp.bfloat16

    def flip(x, dz=0, dy=0, ds=0):
        pairs = []
        for d in range(dev_count):
            for s in range(side_count):
                to = (((d // inner) ^ dz) * inner + ((d % inner) ^ dy)) * side_count + (s ^ ds)
                pairs.append((d * side_count + s, to))
        return lax.ppermute(x, AXES, pairs)

    row_total = local_reqs * T_MAX
    rows_flat = hidden_rows.reshape(row_total, D)
    ids = expert_ids.reshape(row_total, TOP)
    gates = route_weights.reshape(row_total, TOP)
    experts = jnp.arange(peer_count, dtype=jnp.int32)
    table = jnp.sum(jnp.where(ids[:, :, None] == experts, gates[:, :, None], 0.0), axis=1)
    high = lax.reduce_precision(table, 8, 7)
    low = (table - high).astype(bf16)
    pad = -2 * peer_count % 128
    row = jnp.concatenate(
        [rows_flat, high.astype(bf16), low, jnp.zeros((row_total, pad), bf16)], axis=1
    )
    line = [row] + [flip(row, dz=k) for k in range(1, outer)]
    across = [flip(x, dy=1) for x in line]

    first_slot = position * local_reqs
    blocks = inner * outer
    block_rows = H * DK // blocks
    chip = (dev % inner) * outer + dev // inner
    own_pair = lax.dynamic_index_in_dim(swap_pairs, side, 0, keepdims=False)
    other_pair = lax.dynamic_index_in_dim(swap_pairs, 1 - side, 0, keepdims=False)
    pack_scalars = jnp.concatenate(
        [chip[None], other_pair - first_slot, own_pair - first_slot]
    ).astype(jnp.int32)
    packed = jax.ShapeDtypeStruct((blocks, 2, block_rows, DV), bf16)
    out_spec = pl.BlockSpec((1, 2, block_rows, DV), lambda g, s: (g, 0, 0, 0))
    send, keep = pl.pallas_call(
        pack_kernel,
        out_shape=(packed, packed),
        grid_spec=pltpu.PrefetchScalarGridSpec(
            num_scalar_prefetch=1,
            grid=(blocks,),
            in_specs=[
                pl.BlockSpec(
                    (local_reqs, 1, block_rows, DV), lambda g, s: (0, jnp.bitwise_xor(g, s[0]), 0, 0)
                )
            ],
            out_specs=[out_spec, out_spec],
        ),
        name="pack",
    )(pack_scalars, states.reshape(local_reqs, blocks, block_rows, DV))
    chip_part = keep + flip(send, ds=1)
    line_part = chip_part[:outer] + flip(chip_part[outer:], dy=1)
    piece = line_part[0]
    for k in range(1, outer):
        piece = piece + flip(line_part[k], dz=k)
    half = jnp.stack([piece] + [flip(piece, dz=k) for k in range(1, outer)])
    mine = jnp.concatenate([half, flip(half, dy=1)])
    other = flip(mine, ds=1)

    lanes = H * DK
    vec_spec = pl.BlockSpec((1, T_MAX, lanes), lambda r, c: (r, 0, 0))

    def per_head(n):
        return (
            jax.ShapeDtypeStruct((local_reqs, H, n, DK), f32),
            pl.BlockSpec((1, H, n, DK), lambda r, c: (r, 0, 0, 0)),
        )

    shapes, specs = zip(per_head(2 * T_MAX), per_head(2 * T_MAX), per_head(T_MAX + 8))
    z, uo, dg = pl.pallas_call(
        prep_kernel,
        out_shape=shapes,
        grid_spec=pltpu.PrefetchScalarGridSpec(
            num_scalar_prefetch=1,
            grid=(local_reqs,),
            in_specs=[vec_spec] * 4 + [pl.BlockSpec((1, T_MAX, H), lambda r, c: (r, 0, 0))],
            out_specs=list(specs),
        ),
        compiler_params=pltpu.CompilerParams(vmem_limit_bytes=VMEM_LIMIT),
        name="prep",
    )(token_counts, query_vectors, key_vectors, value_vectors, decay_log, write_rate)

    def feed(x):
        gate = x[:, D:].astype(f32)
        picked = (experts == position).astype(f32)
        weight = jnp.sum(
            (gate[:, :peer_count] + gate[:, peer_count : 2 * peer_count]) * picked, axis=1
        )
        gate_up = jnp.dot(x[:, :D], gate_up_weight[0], preferred_element_type=f32)
        activated = (jax.nn.silu(gate_up[:, :FF]) * gate_up[:, FF:]).astype(bf16)
        produced = jnp.dot(activated, down_weight[0], preferred_element_type=f32)
        return (produced * weight[:, None]).astype(bf16)

    def chip_sum(group):
        n = group.shape[0]
        fed = feed(jnp.concatenate([group, flip(group, ds=1)]))
        return fed[:n].astype(f32) + flip(fed[n:], ds=1).astype(f32)

    near = chip_sum(jnp.concatenate(line))
    far = chip_sum(jnp.concatenate(across)).astype(bf16)

    def chunk(x, k):
        return x[k * row_total : (k + 1) * row_total]

    result = None
    for k in range(outer - 1, -1, -1):
        part = chunk(near, k) + flip(chunk(far, k), dy=1).astype(f32)
        if k:
            part = flip(part.astype(bf16), dz=k).astype(f32)
        result = part if result is None else result + part
    expert_out = result.astype(bf16).reshape(local_reqs, T_MAX, D)

    flat_pairs = jnp.concatenate([own_pair, other_pair])
    my_slots = first_slot + jnp.arange(local_reqs, dtype=jnp.int32)
    match = (my_slots[:, None] == flat_pairs[None, :]).astype(jnp.int32)
    moved = jnp.sum(match, axis=1)
    is_other = jnp.sum(match * jnp.array([0, 0, 1, 1], jnp.int32), axis=1)
    member = jnp.sum(match * jnp.array([1, 0, 1, 0], jnp.int32), axis=1)
    scalars = jnp.concatenate(
        [chip[None], jnp.stack([moved, is_other, member], axis=1).reshape(-1)]
    ).astype(jnp.int32)
    heads = max(1, block_rows // DK)
    pieces = max(1, DK // block_rows)

    def piece_spec(which, j):
        def index(r, g, s):
            used = (s[1 + 3 * r] > 0) & (s[2 + 3 * r] == which)
            at = jnp.bitwise_xor(g * pieces + j, s[0])
            return (jnp.where(used, at, 0), jnp.where(used, s[3 + 3 * r], 0), 0, 0)

        return pl.BlockSpec((1, 1, block_rows, DV), index)

    def head_spec(n):
        return pl.BlockSpec((1, heads, n, DK), lambda r, g, s: (r, g, 0, 0))

    new_states, attention_out = pl.pallas_call(
        functools.partial(finish_kernel, pieces, heads),
        out_shape=(
            jax.ShapeDtypeStruct(states.shape, f32),
            jax.ShapeDtypeStruct(query_vectors.shape, bf16),
        ),
        grid_spec=pltpu.PrefetchScalarGridSpec(
            num_scalar_prefetch=1,
            grid=(local_reqs, H // heads),
            in_specs=[head_spec(DK)]
            + [piece_spec(which, j) for which in range(2) for j in range(pieces)]
            + [head_spec(2 * T_MAX), head_spec(2 * T_MAX), head_spec(T_MAX + 8)],
            out_specs=[
                head_spec(DK),
                pl.BlockSpec((1, T_MAX, heads * DV), lambda r, g, s: (r, 0, g)),
            ],
        ),
        name="finish",
    )(scalars, states, *[mine] * pieces, *[other] * pieces, z, uo, dg)
    return (new_states, attention_out, expert_out)


def solution(mesh):
    slots = P(("groups", "dev", "side"))
    experts = P(("dev", "side"))
    in_specs = (slots, P("groups")) + (slots,) * 9 + (experts, experts)
    return jax.shard_map(
        per_device, mesh=mesh, in_specs=in_specs, out_specs=(slots, slots, slots), check_vma=False
    )
```

time: 450 us -> 141 us (0.31); the launches traced: 442 us -> 140 us
  matrix products: 123 us -> 4.52 us
  other arithmetic: 90.6 us -> 6.77 us
  local copies, waits for them, and re-layouts: 86.6 us -> 9.53 us
  waiting for transfers between devices: 95.7 us -> 62.4 us
  Pallas kernels: 0 us -> 28.6 us
  between operations: 14.2 us -> 0.98 us
    dot_general x40 -> x4, matrix products: 123 us -> 4.52 us  [the longest x2 2.83 us: feed(): gate_up = jnp.dot(x[:, :D], gate_up_weight[0], preferred_element_type=f32)]
    psum x1 -> x0, waiting for transfers between devices: 78 us -> none  [per_device(): moved_states = lax.psum(outgoing, ('dev', 'side'))]
    ppermute x0 -> x28, waiting for transfers between devices: none -> 62.4 us  [flip(): return lax.ppermute(x, AXES, pairs)]
    select_n x20 -> x0, other arithmetic: 33.6 us -> none  [the longest x16 23.7 us: advance(): carried = jnp.where(active[:, None, None, None], updated, carried)]
    all_to_all x4 -> x0, starting transfers between devices: 31.5 us -> none  [the longest x2 18.9 us: through_experts(): lax.all_to_all(outbound, ('dev', 'side'), split_axis=0, concat_axis=0, ti...]
    pallas_call x0 -> x3, Pallas kernels: none -> 28.6 us  [the longest x1 16.6 us: per_device(): pl.pallas_call(functools.partial(finish_kernel, pieces, heads), out_shape...]
    ppermute x0 -> x28, starting transfers between devices: none -> 27.5 us  [flip(): return lax.ppermute(x, AXES, pairs)]
    mul x35 -> x0, local copies, waits for them, and re-layouts: 25.1 us -> none  [the longest x16 11.5 us: advance(): decayed = carried * retention_now[..., None]]
  transfers between devices with their start and end apart: 5 -> 28, of which waited for: 3 -> 14; matrix products, arithmetic and copies ran while one was open for 63% -> 10% of each run, Pallas kernels for 0% -> 9%
where the time goes in v1:
time: 141 us; the launch traced here: 140 us
  waiting for transfers between devices  62.4 us (44%)
  Pallas kernels  28.6 us (20%)
  starting transfers between devices  27.5 us (20%)
  local copies, waits for them, and re-layouts  9.53 us (7%)
  other arithmetic  6.77 us (5%)
  matrix products  4.52 us (3%)
    ppermute x28, waiting for transfers between devices, flip(): return lax.ppermute(x, AXES, pairs)  62.4 us
    ppermute x28, starting transfers between devices, flip(): return lax.ppermute(x, AXES, pairs)  27.5 us
    pallas_call x1, Pallas kernels, per_device(): pl.pallas_call(functools.partial(finish_kernel, pieces, heads), out_shape...  16.6 us
    unnamed x43, local copies, waits for them, and re-layouts  6.86 us
    pallas_call x1, Pallas kernels, per_device(): pl.pallas_call(pack_kernel, out_shape=(packed, packed), grid_spec=pltpu.P...  6.33 us
    pallas_call x1, Pallas kernels, per_device(): pl.pallas_call(prep_kernel, out_shape=shapes, grid_spec=pltpu.PrefetchSca...  5.68 us
    dot_general x2, matrix products, feed(): gate_up = jnp.dot(x[:, :D], gate_up_weight[0], preferred_element_type=f32)  2.83 us
  transfers between devices with their start and end apart: 28, of which 14 were waited for; matrix products, arithmetic and copies ran while one was open for 10% of the time, Pallas kernels for 9%

profile of v1, /device:TPU:0, one launch (start us, length us, event | category | flops | bytes accessed | tf_op | source)
XLA Modules:
  0.0 140.3 jit_solution(8728985940691609648)
XLA Ops:
  0.6 0.9 copy.25
  2.6 1.0 concatenate.34
  3.6 3.0 %collective-permute-start.15 = (bf16[32,2432]{1,0:T(8,128)(2,1)S(1)}, bf16[32,2432]{1,0:T(8,128)(2,1)S(1)}, u32[]{:S(2)}, u32[]{:S(2)}) collective-permute-start(bf16[32,2432]{1,0:T(8,128)(2,1)S(1)} %concatenate.34), channel_id=1, source_target_pairs={{0,2},{1,3},{2,0},{3,1},{4,6},{5,7},{6,4},{7,5},{8,10},{9,11},{10,... | collective-permute-start | bytes 466952 | tf_op jit(solution)/shard_map/ppermute | solution.py:148
  6.6 3.6 %collective-permute-start.12 = (bf16[32,2432]{1,0:T(8,128)(2,1)S(1)}, bf16[32,2432]{1,0:T(8,128)(2,1)S(1)}, u32[]{:S(2)}, u32[]{:S(2)}) collective-permute-start(bf16[32,2432]{1,0:T(8,128)(2,1)S(1)} %concatenate.34), channel_id=1, source_target_pairs={{0,12},{1,13},{2,14},{3,15},{4,8},{5,9},{6,10},{7,11},{8,4},{9,5},... | collective-permute-start | bytes 466952 | tf_op jit(solution)/shard_map/ppermute | solution.py:148
  12.4 6.3 %pack.1 = (bf16[8,2,256,128]{3,2,1,0:T(8,128)(2,1)}, bf16[8,2,256,128]{3,2,1,0:T(8,128)(2,1)}) custom-call(s32[5]{0:T(128)} %pad_add_fusion.3.scalars, f32[2,8,256,128]{3,2,1,0:T(8,128)} %bitcast.50), custom_call_target="tpu_custom_call" | custom-call | tf_op jit(solution)/shard_map/pack/pallas_call | solution.py:176
  19.0 4.1 %collective-permute-done.11 = bf16[32,2432]{1,0:T(8,128)(2,1)S(1)} collective-permute-done((bf16[32,2432]{1,0:T(8,128)(2,1)S(1)}, bf16[32,2432]{1,0:T(8,128)(2,1)S(1)}, u32[]{:S(2)}, u32[]{:S(2)}) %collective-permute-start.11) | collective-permute-done | bytes 155680 | tf_op jit(solution)/shard_map/ppermute | solution.py:148
  23.8 1.5 %collective-permute-start.17 = (bf16[32,2432]{1,0:T(8,128)(2,1)S(1)}, bf16[32,2432]{1,0:T(8,128)(2,1)S(1)}, u32[]{:S(2)}, u32[]{:S(2)}) collective-permute-start(bf16[32,2432]{1,0:T(8,128)(2,1)S(1)} %collective-permute-done.11), channel_id=1, source_target_pairs={{0,2},{1,3},{2,0},{3,1},{4,6},{5,7},{6,4},{7,5},{8,10},{9,11},{10,... | collective-permute-start | bytes 466952 | tf_op jit(solution)/shard_map/ppermute | solution.py:148
  26.0 4.1 %collective-permute-done.18 = bf16[32,2432]{1,0:T(8,128)(2,1)S(1)} collective-permute-done((bf16[32,2432]{1,0:T(8,128)(2,1)S(1)}, bf16[32,2432]{1,0:T(8,128)(2,1)S(1)}, u32[]{:S(2)}, u32[]{:S(2)}) %collective-permute-start.18) | collective-permute-done | bytes 155680 | tf_op jit(solution)/shard_map/ppermute | solution.py:148
  30.1 3.3 %collective-permute-done.17 = bf16[32,2432]{1,0:T(8,128)(2,1)S(1)} collective-permute-done((bf16[32,2432]{1,0:T(8,128)(2,1)S(1)}, bf16[32,2432]{1,0:T(8,128)(2,1)S(1)}, u32[]{:S(2)}, u32[]{:S(2)}) %collective-permute-start.17) | collective-permute-done | bytes 155680 | tf_op jit(solution)/shard_map/ppermute | solution.py:148
  33.5 2.9 %collective-permute-done.16 = bf16[32,2432]{1,0:T(8,128)(2,1)S(1)} collective-permute-done((bf16[32,2432]{1,0:T(8,128)(2,1)S(1)}, bf16[32,2432]{1,0:T(8,128)(2,1)S(1)}, u32[]{:S(2)}, u32[]{:S(2)}) %collective-permute-start.16) | collective-permute-done | bytes 155680 | tf_op jit(solution)/shard_map/ppermute | solution.py:148
  36.7 1.9 %collective-permute-done.19 = bf16[128,2432]{1,0:T(8,128)(2,1)S(1)} collective-permute-done((bf16[128,2432]{1,0:T(8,128)(2,1)S(1)}, bf16[128,2432]{1,0:T(8,128)(2,1)S(1)}, u32[]{:S(2)}, u32[]{:S(2)}) %collective-permute-start.19) | collective-permute-done | bytes 622624 | tf_op jit(solution)/shard_map/ppermute | solution.py:148
  38.7 1.4 fusion
  40.3 0.8 fusion.5
  41.4 1.5 %fusion.2 = f32[256,1024]{1,0:T(8,128)S(1)} fusion(bf16[1,2304,1024]{2,1,0:T(8,128)(2,1)S(1)} %copy-done.14, bf16[256,2432]{1,0:T(8,128)(2,1)S(1)} %constant_dynamic-update-slice_fusion.5), kind=kOutput, calls=%fused_computation.2 | convolution fusion | flops 1207959552 | bytes 6946816 | tf_op jit(solution)/shard_map/dot_general | solution.py:229
  46.0 13.6 %collective-permute-done.1 = bf16[4,2,256,128]{3,2,1,0:T(8,128)(2,1)S(1)} collective-permute-done((bf16[4,2,256,128]{3,2,1,0:T(8,128)(2,1)S(1)}, bf16[4,2,256,128]{3,2,1,0:T(8,128)(2,1)S(1)}, u32[]{:S(2)}, u32[]{:S(2)}) %collective-permute-start.1) | collective-permute-done | bytes 524320 | tf_op jit(solution)/shard_map/ppermute | solution.py:148
  59.8 2.6 %collective-permute-start.4 = (bf16[2,256,128]{2,1,0:T(8,128)(2,1)S(1)}, bf16[2,256,128]{2,1,0:T(8,128)(2,1)S(1)}, u32[]{:S(2)}, u32[]{:S(2)}) collective-permute-start(bf16[2,256,128]{2,1,0:T(8,128)(2,1)S(1)} %get-tuple-element.36), channel_id=1, source_target_pairs={{0,12},{1,13},{2,14},{3,15},{4,8},{5,9},{6,10},{7,11},{8,4},{9,5},... | collective-permute-start | bytes 393224 | tf_op jit(solution)/shard_map/ppermute | solution.py:148
  62.3 0.9 collective-permute-start.3
  63.9 1.2 collective-permute-done.2
  65.6 3.9 %collective-permute-done.4 = bf16[2,256,128]{2,1,0:T(8,128)(2,1)S(1)} collective-permute-done((bf16[2,256,128]{2,1,0:T(8,128)(2,1)S(1)}, bf16[2,256,128]{2,1,0:T(8,128)(2,1)S(1)}, u32[]{:S(2)}, u32[]{:S(2)}) %collective-permute-start.4) | collective-permute-done | bytes 131104 | tf_op jit(solution)/shard_map/ppermute | solution.py:148
  69.5 5.0 %collective-permute-done.3 = bf16[2,256,128]{2,1,0:T(8,128)(2,1)S(1)} collective-permute-done((bf16[2,256,128]{2,1,0:T(8,128)(2,1)S(1)}, bf16[2,256,128]{2,1,0:T(8,128)(2,1)S(1)}, u32[]{:S(2)}, u32[]{:S(2)}) %collective-permute-start.3) | collective-permute-done | bytes 131104 | tf_op jit(solution)/shard_map/ppermute | solution.py:148
  75.2 2.4 %collective-permute-start.7 = (bf16[2,256,128]{2,1,0:T(8,128)(2,1)S(1)}, bf16[2,256,128]{2,1,0:T(8,128)(2,1)S(1)}, u32[]{:S(2)}, u32[]{:S(2)}) collective-permute-start(bf16[2,256,128]{2,1,0:T(8,128)(2,1)S(1)} %get-tuple-element.23), channel_id=1, source_target_pairs={{0,12},{1,13},{2,14},{3,15},{4,8},{5,9},{6,10},{7,11},{8,4},{9,5},... | collective-permute-start | bytes 393224 | tf_op jit(solution)/shard_map/ppermute | solution.py:148
  77.7 1.9 %collective-permute-start.5 = (bf16[2,256,128]{2,1,0:T(8,128)(2,1)S(1)}, bf16[2,256,128]{2,1,0:T(8,128)(2,1)S(1)}, u32[]{:S(2)}, u32[]{:S(2)}) collective-permute-start(bf16[2,256,128]{2,1,0:T(8,128)(2,1)S(1)} %get-tuple-element.23), channel_id=1, source_target_pairs={{0,4},{1,5},{2,6},{3,7},{4,0},{5,1},{6,2},{7,3},{8,12},{9,13},{10,... | collective-permute-start | bytes 393224 | tf_op jit(solution)/shard_map/ppermute | solution.py:148
  79.7 3.7 %collective-permute-done.7 = bf16[2,256,128]{2,1,0:T(8,128)(2,1)S(1)} collective-permute-done((bf16[2,256,128]{2,1,0:T(8,128)(2,1)S(1)}, bf16[2,256,128]{2,1,0:T(8,128)(2,1)S(1)}, u32[]{:S(2)}, u32[]{:S(2)}) %collective-permute-start.7) | collective-permute-done | bytes 131104 | tf_op jit(solution)/shard_map/ppermute | solution.py:148
  84.0 3.7 %collective-permute-done.6 = bf16[2,256,128]{2,1,0:T(8,128)(2,1)S(1)} collective-permute-done((bf16[2,256,128]{2,1,0:T(8,128)(2,1)S(1)}, bf16[2,256,128]{2,1,0:T(8,128)(2,1)S(1)}, u32[]{:S(2)}, u32[]{:S(2)}) %collective-permute-start.6) | collective-permute-done | bytes 131104 | tf_op jit(solution)/shard_map/ppermute | solution.py:148
  88.2 1.6 %collective-permute-start.8 = (bf16[4,2,256,128]{3,2,1,0:T(8,128)(2,1)S(1)}, bf16[4,2,256,128]{3,2,1,0:T(8,128)(2,1)S(1)}, u32[]{:S(2)}, u32[]{:S(2)}) collective-permute-start(bf16[4,2,256,128]{3,2,1,0:T(8,128)(2,1)S(1)} %pad_maximum_fusion.2), channel_id=1, source_target_pairs={{0,2},{1,3},{2,0},{3,1},{4,6},{5,7},{6,4},{7,5},{8,10},{9,11},{10,... | collective-permute-start | bytes 1572872 | tf_op jit(solution)/shard_map/ppermute | solution.py:148
  91.9 12.3 %collective-permute-done.8 = bf16[4,2,256,128]{3,2,1,0:T(8,128)(2,1)S(1)} collective-permute-done((bf16[4,2,256,128]{3,2,1,0:T(8,128)(2,1)S(1)}, bf16[4,2,256,128]{3,2,1,0:T(8,128)(2,1)S(1)}, u32[]{:S(2)}, u32[]{:S(2)}) %collective-permute-start.8) | collective-permute-done | bytes 524320 | tf_op jit(solution)/shard_map/ppermute | solution.py:148
  105.8 2.3 %collective-permute-start.22 = (bf16[32,2304]{1,0:T(8,128)(2,1)}, bf16[32,2304]{1,0:T(8,128)(2,1)}, u32[]{:S(2)}, u32[]{:S(2)}) collective-permute-start(bf16[32,2304]{1,0:T(8,128)(2,1)} %get-tuple-element.28), channel_id=1, source_target_pairs={{0,12},{1,13},{2,14},{3,15},{4,8},{5,9},{6,10},{7,11},{8,4},{9,5},... | collective-permute-start | bytes 442376 | tf_op jit(solution)/shard_map/ppermute | solution.py:148
  108.1 2.1 %collective-permute-start.24 = (bf16[32,2304]{1,0:T(8,128)(2,1)S(1)}, bf16[32,2304]{1,0:T(8,128)(2,1)}, u32[]{:S(2)}, u32[]{:S(2)}) collective-permute-start(bf16[32,2304]{1,0:T(8,128)(2,1)S(1)} %get-tuple-element.30), channel_id=1, source_target_pairs={{0,8},{1,9},{2,10},{3,11},{4,12},{5,13},{6,14},{7,15},{8,0},{9,1},... | collective-permute-start | bytes 442376 | tf_op jit(solution)/shard_map/ppermute | solution.py:148
  110.4 5.7 %prep.1 = (f32[2,16,32,128]{3,2,1,0:T(8,128)S(1)}, f32[2,16,32,128]{3,2,1,0:T(8,128)S(1)}, f32[2,16,24,128]{3,2,1,0:T(8,128)S(1)}) custom-call(s32[2]{0:T(128)S(1)} %copy-done.9, bf16[2,16,2048]{2,1,0:T(8,128)(2,1)S(1)} %copy-done.5, bf16[2,16,2048]{2,1,0:T(8,128)(2,1)S(1)} %copy-done.6, bf16[2,16,2048]{2,1,0:T(8,128)(2,1)S(1)} %copy-done.7, ...), custom_call_target="tpu_custom_call" | custom-call | tf_op jit(solution)/shard_map/prep/pallas_call | solution.py:210
  119.5 2.2 %collective-permute-done.24 = bf16[32,2304]{1,0:T(8,128)(2,1)} collective-permute-done((bf16[32,2304]{1,0:T(8,128)(2,1)S(1)}, bf16[32,2304]{1,0:T(8,128)(2,1)}, u32[]{:S(2)}, u32[]{:S(2)}) %collective-permute-start.24) | collective-permute-done | bytes 147488 | tf_op jit(solution)/shard_map/ppermute | solution.py:148
  121.7 1.9 %fusion.13 = bf16[32,2304]{1,0:T(8,128)(2,1)} fusion(f32[128,2304]{1,0:T(8,128)} %copy-done.10, bf16[32,2304]{1,0:T(8,128)(2,1)} %collective-permute-done.27, bf16[32,2304]{1,0:T(8,128)(2,1)} %collective-permute-done.26, bf16[32,2304]{1,0:T(8,128)(2,1)} %collective-permute-done.24, bf16[32,2304]{1,0:T(8,128)(2,1)} %collective-permute-done.22), kind=kLoop, calls=%fused_computation.24 | loop fusion | flops 663552 | bytes 1032192 | tf_op jit(solution)/shard_map/convert_element_type | solution.py:251
  123.7 16.6 %finish.1 = (f32[2,16,128,128]{3,2,1,0:T(8,128)}, bf16[2,16,2048]{2,1,0:T(8,128)(2,1)}) custom-call(s32[7]{0:T(128)} %pad_add_fusion.2.scalars, f32[2,16,128,128]{3,2,1,0:T(8,128)} %states_ref.1, bf16[8,2,256,128]{3,2,1,0:T(8,128)(2,1)} %constant_dynamic-update-slice_fusion.refs_0_, bf16[8,2,256,128]{3,2,1,0:T(8,128)(2,1)} %collective-permute-done.9.refs_1_, ...), custom_call_target="tpu_custom_call" | custom-call | tf_op jit(solution)/shard_map/finish/pallas_call | solution.py:276
  (112 shorter events, 19.2 us)
Async XLA Ops:
  0.6 39.7 %copy-start = (bf16[1,512,2304]{2,1,0:T(8,128)(2,1)S(1)}, bf16[1,512,2304]{2,1,0:T(8,128)(2,1)}, u32[]{:S(2)}) copy-start(bf16[1,512,2304]{2,1,0:T(8,128)(2,1)} %param.27) | copy-start | bytes 7077892
  3.6 21.8 %collective-permute-start.15 = (bf16[32,2432]{1,0:T(8,128)(2,1)S(1)}, bf16[32,2432]{1,0:T(8,128)(2,1)S(1)}, u32[]{:S(2)}, u32[]{:S(2)}) collective-permute-start(bf16[32,2432]{1,0:T(8,128)(2,1)S(1)} %concatenate.34), channel_id=1, source_target_pairs={{0,2},{1,3},{2,0},{3,1},{4,6},{5,7},{6,4},{7,5},{8,10},{9,11},{10,... | collective-permute-start | bytes 466952 | tf_op jit(solution)/shard_map/ppermute | solution.py:148
  6.6 12.4 %collective-permute-start.12 = (bf16[32,2432]{1,0:T(8,128)(2,1)S(1)}, bf16[32,2432]{1,0:T(8,128)(2,1)S(1)}, u32[]{:S(2)}, u32[]{:S(2)}) collective-permute-start(bf16[32,2432]{1,0:T(8,128)(2,1)S(1)} %concatenate.34), channel_id=1, source_target_pairs={{0,12},{1,13},{2,14},{3,15},{4,8},{5,9},{6,10},{7,11},{8,4},{9,5},... | collective-permute-start | bytes 466952 | tf_op jit(solution)/shard_map/ppermute | solution.py:148
  10.2 12.9 %collective-permute-start.11 = (bf16[32,2432]{1,0:T(8,128)(2,1)S(1)}, bf16[32,2432]{1,0:T(8,128)(2,1)S(1)}, u32[]{:S(2)}, u32[]{:S(2)}) collective-permute-start(bf16[32,2432]{1,0:T(8,128)(2,1)S(1)} %concatenate.34), channel_id=1, source_target_pairs={{0,8},{1,9},{2,10},{3,11},{4,12},{5,13},{6,14},{7,15},{8,0},{9,1},... | collective-permute-start | bytes 466952 | tf_op jit(solution)/shard_map/ppermute | solution.py:148
  10.2 12.9 %collective-permute-start.10 = (bf16[32,2432]{1,0:T(8,128)(2,1)S(1)}, bf16[32,2432]{1,0:T(8,128)(2,1)S(1)}, u32[]{:S(2)}, u32[]{:S(2)}) collective-permute-start(bf16[32,2432]{1,0:T(8,128)(2,1)S(1)} %concatenate.34), channel_id=1, source_target_pairs={{0,4},{1,5},{2,6},{3,7},{4,0},{5,1},{6,2},{7,3},{8,12},{9,13},{10,... | collective-permute-start | bytes 466952 | tf_op jit(solution)/shard_map/ppermute | solution.py:148
  18.7 25.6 %collective-permute-start = (bf16[8,2,256,128]{3,2,1,0:T(8,128)(2,1)}, bf16[8,2,256,128]{3,2,1,0:T(8,128)(2,1)S(1)}, u32[]{:S(2)}, u32[]{:S(2)}) collective-permute-start(bf16[8,2,256,128]{3,2,1,0:T(8,128)(2,1)} %get-tuple-element.11), channel_id=1, source_target_pairs={{0,1},{1,0},{2,3},{3,2},{4,5},{5,4},{6,7},{7,6},{8,9},{9,8},{10,11... | collective-permute-start | bytes 3145736 | tf_op jit(solution)/shard_map/ppermute | solution.py:148
  23.2 13.4 %collective-permute-start.13 = (bf16[128,2432]{1,0:T(8,128)(2,1)S(1)}, bf16[128,2432]{1,0:T(8,128)(2,1)S(1)}, u32[]{:S(2)}, u32[]{:S(2)}) collective-permute-start(bf16[128,2432]{1,0:T(8,128)(2,1)S(1)} %pad_maximum_fusion), channel_id=1, source_target_pairs={{0,1},{1,0},{2,3},{3,2},{4,5},{5,4},{6,7},{7,6},{8,9},{9,8},{10,11... | collective-permute-start | bytes 1867784 | tf_op jit(solution)/shard_map/ppermute | solution.py:148
  23.3 6.9 %collective-permute-start.18 = (bf16[32,2432]{1,0:T(8,128)(2,1)S(1)}, bf16[32,2432]{1,0:T(8,128)(2,1)S(1)}, u32[]{:S(2)}, u32[]{:S(2)}) collective-permute-start(bf16[32,2432]{1,0:T(8,128)(2,1)S(1)} %collective-permute-done.12), channel_id=1, source_target_pairs={{0,2},{1,3},{2,0},{3,1},{4,6},{5,7},{6,4},{7,5},{8,10},{9,11},{10,... | collective-permute-start | bytes 466952 | tf_op jit(solution)/shard_map/ppermute | solution.py:148
  23.8 9.7 %collective-permute-start.17 = (bf16[32,2432]{1,0:T(8,128)(2,1)S(1)}, bf16[32,2432]{1,0:T(8,128)(2,1)S(1)}, u32[]{:S(2)}, u32[]{:S(2)}) collective-permute-start(bf16[32,2432]{1,0:T(8,128)(2,1)S(1)} %collective-permute-done.11), channel_id=1, source_target_pairs={{0,2},{1,3},{2,0},{3,1},{4,6},{5,7},{6,4},{7,5},{8,10},{9,11},{10,... | collective-permute-start | bytes 466952 | tf_op jit(solution)/shard_map/ppermute | solution.py:148
  25.4 10.9 %collective-permute-start.16 = (bf16[32,2432]{1,0:T(8,128)(2,1)S(1)}, bf16[32,2432]{1,0:T(8,128)(2,1)S(1)}, u32[]{:S(2)}, u32[]{:S(2)}) collective-permute-start(bf16[32,2432]{1,0:T(8,128)(2,1)S(1)} %collective-permute-done.10), channel_id=1, source_target_pairs={{0,2},{1,3},{2,0},{3,1},{4,6},{5,7},{6,4},{7,5},{8,10},{9,11},{10,... | collective-permute-start | bytes 466952 | tf_op jit(solution)/shard_map/ppermute | solution.py:148
  36.4 2.1 %collective-permute-start.19 = (bf16[128,2432]{1,0:T(8,128)(2,1)S(1)}, bf16[128,2432]{1,0:T(8,128)(2,1)S(1)}, u32[]{:S(2)}, u32[]{:S(2)}) collective-permute-start(bf16[128,2432]{1,0:T(8,128)(2,1)S(1)} %pad_maximum_fusion.1), channel_id=1, source_target_pairs={{0,1},{1,0},{2,3},{3,2},{4,5},{5,4},{6,7},{7,6},{8,9},{9,8},{10,11... | collective-permute-start | bytes 1867784 | tf_op jit(solution)/shard_map/ppermute | solution.py:148
  41.2 4.6 %collective-permute-start.20 = (bf16[128,2304]{1,0:T(8,128)(2,1)S(1)}, bf16[128,2304]{1,0:T(8,128)(2,1)S(1)}, u32[]{:S(2)}, u32[]{:S(2)}) collective-permute-start(bf16[128,2304]{1,0:T(8,128)(2,1)S(1)} %slice.142), channel_id=1, source_target_pairs={{0,1},{1,0},{2,3},{3,2},{4,5},{5,4},{6,7},{7,6},{8,9},{9,8},{10,11... | collective-permute-start | bytes 1769480 | tf_op jit(solution)/shard_map/ppermute | solution.py:148
  43.7 33.9 %collective-permute-start.14 = (bf16[128,2304]{1,0:T(8,128)(2,1)S(1)}, bf16[128,2304]{1,0:T(8,128)(2,1)S(1)}, u32[]{:S(2)}, u32[]{:S(2)}) collective-permute-start(bf16[128,2304]{1,0:T(8,128)(2,1)S(1)} %slice.133), channel_id=1, source_target_pairs={{0,1},{1,0},{2,3},{3,2},{4,5},{5,4},{6,7},{7,6},{8,9},{9,8},{10,11... | collective-permute-start | bytes 1769480 | tf_op jit(solution)/shard_map/ppermute | solution.py:148
  45.2 14.3 %collective-permute-start.1 = (bf16[4,2,256,128]{3,2,1,0:T(8,128)(2,1)S(1)}, bf16[4,2,256,128]{3,2,1,0:T(8,128)(2,1)S(1)}, u32[]{:S(2)}, u32[]{:S(2)}) collective-permute-start(bf16[4,2,256,128]{3,2,1,0:T(8,128)(2,1)S(1)} %slice.121), channel_id=1, source_target_pairs={{0,2},{1,3},{2,0},{3,1},{4,6},{5,7},{6,4},{7,5},{8,10},{9,11},{10,... | collective-permute-start | bytes 1572872 | tf_op jit(solution)/shard_map/ppermute | solution.py:148
  59.7 5.4 %collective-permute-start.2 = (bf16[2,256,128]{2,1,0:T(8,128)(2,1)S(1)}, bf16[2,256,128]{2,1,0:T(8,128)(2,1)S(1)}, u32[]{:S(2)}, u32[]{:S(2)}) collective-permute-start(bf16[2,256,128]{2,1,0:T(8,128)(2,1)S(1)} %get-tuple-element.35), channel_id=1, source_target_pairs={{0,4},{1,5},{2,6},{3,7},{4,0},{5,1},{6,2},{7,3},{8,12},{9,13},{10,... | collective-permute-start | bytes 393224 | tf_op jit(solution)/shard_map/ppermute | solution.py:148
  59.8 9.8 %collective-permute-start.4 = (bf16[2,256,128]{2,1,0:T(8,128)(2,1)S(1)}, bf16[2,256,128]{2,1,0:T(8,128)(2,1)S(1)}, u32[]{:S(2)}, u32[]{:S(2)}) collective-permute-start(bf16[2,256,128]{2,1,0:T(8,128)(2,1)S(1)} %get-tuple-element.36), channel_id=1, source_target_pairs={{0,12},{1,13},{2,14},{3,15},{4,8},{5,9},{6,10},{7,11},{8,4},{9,5},... | collective-permute-start | bytes 393224 | tf_op jit(solution)/shard_map/ppermute | solution.py:148
  62.3 12.1 %collective-permute-start.3 = (bf16[2,256,128]{2,1,0:T(8,128)(2,1)S(1)}, bf16[2,256,128]{2,1,0:T(8,128)(2,1)S(1)}, u32[]{:S(2)}, u32[]{:S(2)}) collective-permute-start(bf16[2,256,128]{2,1,0:T(8,128)(2,1)S(1)} %get-tuple-element.37), channel_id=1, source_target_pairs={{0,8},{1,9},{2,10},{3,11},{4,12},{5,13},{6,14},{7,15},{8,0},{9,1},... | collective-permute-start | bytes 393224 | tf_op jit(solution)/shard_map/ppermute | solution.py:148
  63.3 41.8 %collective-permute-start.21 = (bf16[32,2304]{1,0:T(8,128)(2,1)S(1)}, bf16[32,2304]{1,0:T(8,128)(2,1)S(1)}, u32[]{:S(2)}, u32[]{:S(2)}) collective-permute-start(bf16[32,2304]{1,0:T(8,128)(2,1)S(1)} %get-tuple-element.31), channel_id=1, source_target_pairs={{0,2},{1,3},{2,0},{3,1},{4,6},{5,7},{6,4},{7,5},{8,10},{9,11},{10,... | collective-permute-start | bytes 442376 | tf_op jit(solution)/shard_map/ppermute | solution.py:148
  65.1 54.1 %collective-permute-start.27 = (bf16[32,2304]{1,0:T(8,128)(2,1)S(1)}, bf16[32,2304]{1,0:T(8,128)(2,1)}, u32[]{:S(2)}, u32[]{:S(2)}) collective-permute-start(bf16[32,2304]{1,0:T(8,128)(2,1)S(1)} %get-tuple-element.32), channel_id=1, source_target_pairs={{0,2},{1,3},{2,0},{3,1},{4,6},{5,7},{6,4},{7,5},{8,10},{9,11},{10,... | collective-permute-start | bytes 442376 | tf_op jit(solution)/shard_map/ppermute | solution.py:148
  75.2 8.2 %collective-permute-start.7 = (bf16[2,256,128]{2,1,0:T(8,128)(2,1)S(1)}, bf16[2,256,128]{2,1,0:T(8,128)(2,1)S(1)}, u32[]{:S(2)}, u32[]{:S(2)}) collective-permute-start(bf16[2,256,128]{2,1,0:T(8,128)(2,1)S(1)} %get-tuple-element.23), channel_id=1, source_target_pairs={{0,12},{1,13},{2,14},{3,15},{4,8},{5,9},{6,10},{7,11},{8,4},{9,5},... | collective-permute-start | bytes 393224 | tf_op jit(solution)/shard_map/ppermute | solution.py:148
  77.6 10.0 %collective-permute-start.6 = (bf16[2,256,128]{2,1,0:T(8,128)(2,1)S(1)}, bf16[2,256,128]{2,1,0:T(8,128)(2,1)S(1)}, u32[]{:S(2)}, u32[]{:S(2)}) collective-permute-start(bf16[2,256,128]{2,1,0:T(8,128)(2,1)S(1)} %get-tuple-element.23), channel_id=1, source_target_pairs={{0,8},{1,9},{2,10},{3,11},{4,12},{5,13},{6,14},{7,15},{8,0},{9,1},... | collective-permute-start | bytes 393224 | tf_op jit(solution)/shard_map/ppermute | solution.py:148
  77.7 10.5 %collective-permute-start.5 = (bf16[2,256,128]{2,1,0:T(8,128)(2,1)S(1)}, bf16[2,256,128]{2,1,0:T(8,128)(2,1)S(1)}, u32[]{:S(2)}, u32[]{:S(2)}) collective-permute-start(bf16[2,256,128]{2,1,0:T(8,128)(2,1)S(1)} %get-tuple-element.23), channel_id=1, source_target_pairs={{0,4},{1,5},{2,6},{3,7},{4,0},{5,1},{6,2},{7,3},{8,12},{9,13},{10,... | collective-permute-start | bytes 393224 | tf_op jit(solution)/shard_map/ppermute | solution.py:148
  79.7 25.3 %copy-start.10 = (f32[128,2304]{1,0:T(8,128)}, f32[128,2304]{1,0:T(8,128)S(1)}, u32[]{:S(2)}) copy-start(f32[128,2304]{1,0:T(8,128)S(1)} %convert_add_fusion) | copy-start | bytes 3538948
  83.4 21.6 %collective-permute-start.25 = (bf16[32,2304]{1,0:T(8,128)(2,1)S(1)}, bf16[32,2304]{1,0:T(8,128)(2,1)S(1)}, u32[]{:S(2)}, u32[]{:S(2)}) collective-permute-start(bf16[32,2304]{1,0:T(8,128)(2,1)S(1)} %get-tuple-element.33), channel_id=1, source_target_pairs={{0,2},{1,3},{2,0},{3,1},{4,6},{5,7},{6,4},{7,5},{8,10},{9,11},{10,... | collective-permute-start | bytes 442376 | tf_op jit(solution)/shard_map/ppermute | solution.py:148
  87.7 17.4 %collective-permute-start.23 = (bf16[32,2304]{1,0:T(8,128)(2,1)S(1)}, bf16[32,2304]{1,0:T(8,128)(2,1)S(1)}, u32[]{:S(2)}, u32[]{:S(2)}) collective-permute-start(bf16[32,2304]{1,0:T(8,128)(2,1)S(1)} %get-tuple-element.34), channel_id=1, source_target_pairs={{0,2},{1,3},{2,0},{3,1},{4,6},{5,7},{6,4},{7,5},{8,10},{9,11},{10,... | collective-permute-start | bytes 442376 | tf_op jit(solution)/shard_map/ppermute | solution.py:148
  88.2 16.0 %collective-permute-start.8 = (bf16[4,2,256,128]{3,2,1,0:T(8,128)(2,1)S(1)}, bf16[4,2,256,128]{3,2,1,0:T(8,128)(2,1)S(1)}, u32[]{:S(2)}, u32[]{:S(2)}) collective-permute-start(bf16[4,2,256,128]{3,2,1,0:T(8,128)(2,1)S(1)} %pad_maximum_fusion.2), channel_id=1, source_target_pairs={{0,2},{1,3},{2,0},{3,1},{4,6},{5,7},{6,4},{7,5},{8,10},{9,11},{10,... | collective-permute-start | bytes 1572872 | tf_op jit(solution)/shard_map/ppermute | solution.py:148
  91.8 18.6 %copy-start.8 = (f32[2,16,16]{2,1,0:T(8,128)S(1)}, f32[2,16,16]{2,1,0:T(8,128)}, u32[]{:S(2)}) copy-start(f32[2,16,16]{2,1,0:T(8,128)} %rate_ref.1) | copy-start | bytes 6148
  91.9 18.6 %copy-start.9 = (s32[2]{0:T(128)S(1)}, s32[2]{0:T(128)}, u32[]{:S(2)}) copy-start(s32[2]{0:T(128)} %counts.1) | copy-start | bytes 28
  105.0 18.6 %collective-permute-start.9 = (bf16[8,2,256,128]{3,2,1,0:T(8,128)(2,1)}, bf16[8,2,256,128]{3,2,1,0:T(8,128)(2,1)}, u32[]{:S(2)}, u32[]{:S(2)}) collective-permute-start(bf16[8,2,256,128]{3,2,1,0:T(8,128)(2,1)} %constant_dynamic-update-slice_fusion.refs_0_), channel_id=1, source_target_pairs={{0,1},{1,0},{2,3},{3,2},{4,5},{5,4},{6,7},{7,6},{8,9},{9,8},{10,11... | collective-permute-start | bytes 3145736 | tf_op jit(solution)/shard_map/ppermute | solution.py:148
  105.8 13.3 %collective-permute-start.22 = (bf16[32,2304]{1,0:T(8,128)(2,1)}, bf16[32,2304]{1,0:T(8,128)(2,1)}, u32[]{:S(2)}, u32[]{:S(2)}) collective-permute-start(bf16[32,2304]{1,0:T(8,128)(2,1)} %get-tuple-element.28), channel_id=1, source_target_pairs={{0,12},{1,13},{2,14},{3,15},{4,8},{5,9},{6,10},{7,11},{8,4},{9,5},... | collective-permute-start | bytes 442376 | tf_op jit(solution)/shard_map/ppermute | solution.py:148
  108.1 11.4 %collective-permute-start.26 = (bf16[32,2304]{1,0:T(8,128)(2,1)S(1)}, bf16[32,2304]{1,0:T(8,128)(2,1)}, u32[]{:S(2)}, u32[]{:S(2)}) collective-permute-start(bf16[32,2304]{1,0:T(8,128)(2,1)S(1)} %get-tuple-element.29), channel_id=1, source_target_pairs={{0,4},{1,5},{2,6},{3,7},{4,0},{5,1},{6,2},{7,3},{8,12},{9,13},{10,... | collective-permute-start | bytes 442376 | tf_op jit(solution)/shard_map/ppermute | solution.py:148
  108.1 13.6 %collective-permute-start.24 = (bf16[32,2304]{1,0:T(8,128)(2,1)S(1)}, bf16[32,2304]{1,0:T(8,128)(2,1)}, u32[]{:S(2)}, u32[]{:S(2)}) collective-permute-start(bf16[32,2304]{1,0:T(8,128)(2,1)S(1)} %get-tuple-element.30), channel_id=1, source_target_pairs={{0,8},{1,9},{2,10},{3,11},{4,12},{5,13},{6,14},{7,15},{8,0},{9,1},... | collective-permute-start | bytes 442376 | tf_op jit(solution)/shard_map/ppermute | solution.py:148
  (11 other events, 95.8 us)

commit v2 on v1

v2 whole, which is shorter than its diff:
```python
import functools

import jax
import jax.numpy as jnp
from jax import lax
from jax.experimental import pallas as pl
from jax.experimental.pallas import tpu as pltpu
from jax.sharding import PartitionSpec as P

D = 2304
FF = 512
H = 16
DK = 128
DV = 128
TOP = 8
T_MAX = 16
AXES = ("dev", "side")
HIGHEST = lax.Precision.HIGHEST
VMEM_LIMIT = 48 * 1024 * 1024


def dot_nt(a, b):
    return lax.dot_general(
        a, b, (((1,), (1,)), ((), ())), precision=HIGHEST, preferred_element_type=jnp.float32
    )


def dot_nn(a, b):
    return lax.dot_general(
        a, b, (((1,), (0,)), ((), ())), precision=HIGHEST, preferred_element_type=jnp.float32
    )


def pack_kernel(scalars, send_in, keep_in, send_ref, keep_ref):
    send_ref[...] = send_in[0].astype(jnp.bfloat16)
    keep_ref[...] = keep_in[0].astype(jnp.bfloat16)


def unit(vectors):
    return vectors * lax.rsqrt(jnp.sum(vectors * vectors, axis=-1, keepdims=True) + 1e-06)


def prep_kernel(
    counts, q_ref, k_ref, v_ref, decay_ref, rate_ref, z_ref, uo_ref, key_ref, kept_ref
):
    r = pl.program_id(0)
    count = counts[r]
    times = lax.broadcasted_iota(jnp.int32, (T_MAX, 1), 0)
    live = (times < count).astype(jnp.float32)
    rows = lax.broadcasted_iota(jnp.int32, (T_MAX, T_MAX), 0)
    cols = lax.broadcasted_iota(jnp.int32, (T_MAX, T_MAX), 1)
    lower = (cols <= rows).astype(jnp.float32)
    decay = decay_ref[0] * live
    total = dot_nn(lower, decay)
    rates = rate_ref[0] * live
    for h in range(q_ref.shape[2] // DK):
        lanes = slice(h * DK, (h + 1) * DK)
        cum = total[:, lanes]
        grown = jnp.exp(-cum)
        key = unit(k_ref[0, :, lanes].astype(jnp.float32))
        query = unit(q_ref[0, :, lanes].astype(jnp.float32)) * live
        value = v_ref[0, :, lanes].astype(jnp.float32)
        rate = rates[:, h : h + 1]
        key_in = key * grown
        query_in = query * grown
        key_out = key * jnp.exp(cum)
        gram = dot_nt(jnp.concatenate([key_in, query_in], axis=0), key_out)
        mix = jnp.where(cols < rows, gram[:T_MAX], 0.0) * rate
        read = jnp.where(cols <= rows, gram[T_MAX:], 0.0)
        solved = jnp.concatenate([value, key_in], axis=1) * rate
        for s in range(T_MAX - 1):
            solved = solved - mix[:, s : s + 1] * solved[s : s + 1, :]
        seen = dot_nn(read, solved)
        high, low = split(jnp.concatenate([solved[:, DV:], query_in - seen[:, DV:]], axis=0))
        z_ref[0, h] = jnp.concatenate([high, high, low], axis=1)
        uo_ref[0, h, :T_MAX] = solved[:, :DV]
        uo_ref[0, h, T_MAX:] = seen[:, :DV]
        last = cum[T_MAX - 1 : T_MAX]
        high, low = split(key * jnp.exp(cum - last))
        key_ref[0, h] = jnp.concatenate([high, high, low], axis=0)
        kept_ref[0, h] = jnp.broadcast_to(jnp.exp(-last), (8, DK))


def split(x):
    high = x.astype(jnp.bfloat16)
    return high, (x - high.astype(jnp.float32)).astype(jnp.bfloat16)


def finish_kernel(
    heads,
    block_rows,
    scalars,
    states_ref,
    mine,
    near,
    other,
    z_ref,
    uo_ref,
    key_ref,
    kept_ref,
    new_ref,
    out_ref,
):
    r = pl.program_id(0)
    first = pl.program_id(1) * heads
    source = scalars[1 + r]
    partner = jnp.where(source == 1, 1 - r, r)
    for h in range(heads):
        row = (first + h) * DK
        block = jnp.bitwise_xor(row // block_rows, scalars[0])
        at = pl.ds(pl.multiple_of(row % block_rows, DK), DK)
        arrived = jnp.where(
            source == 2, mine[block, at], jnp.where(source == 3, near[block, at], other[block, at])
        )
        state = jnp.where(source >= 2, arrived.astype(jnp.float32), states_ref[partner, h])
        high, low = split(state)
        both = jnp.dot(
            z_ref[0, h],
            jnp.concatenate([high, low, high], axis=0),
            preferred_element_type=jnp.float32,
        )
        writes = uo_ref[0, h, :T_MAX] - both[:T_MAX]
        read = uo_ref[0, h, T_MAX:] + both[T_MAX:]
        out_ref[0, :, h * DV : (h + 1) * DV] = read.astype(out_ref.dtype)
        high, low = split(writes)
        written = lax.dot_general(
            key_ref[0, h],
            jnp.concatenate([high, low, high], axis=0),
            (((0,), (0,)), ((), ())),
            preferred_element_type=jnp.float32,
        )
        new_ref[0, h] = jnp.transpose(kept_ref[0, h])[:, :1] * state + written


def per_device(
    states,
    swap_pairs,
    token_counts,
    query_vectors,
    key_vectors,
    value_vectors,
    decay_log,
    write_rate,
    hidden_rows,
    expert_ids,
    route_weights,
    gate_up_weight,
    down_weight,
):
    local_reqs = states.shape[0]
    dev_count = lax.axis_size("dev")
    side_count = lax.axis_size("side")
    peer_count = dev_count * side_count
    position = lax.axis_index(AXES)
    side = lax.axis_index("side")
    dev = lax.axis_index("dev")
    inner = 2
    outer = dev_count // inner
    masks = []
    while len(masks) == 0 or masks[-1] + 1 < outer:
        masks.append(2 ** (len(masks) + 1) - 1)
    f32, bf16 = jnp.float32, jnp.bfloat16

    def flip(x, dz=0, dy=0, ds=0):
        pairs = []
        for d in range(dev_count):
            for s in range(side_count):
                to = (((d // inner) ^ dz) * inner + ((d % inner) ^ dy)) * side_count + (s ^ ds)
                pairs.append((d * side_count + s, to))
        return lax.ppermute(x, AXES, pairs)

    def after(x, *earlier):
        return lax.optimization_barrier((x, *earlier))[0]

    row_total = local_reqs * T_MAX
    rows_flat = hidden_rows.reshape(row_total, D)
    ids = expert_ids.reshape(row_total, TOP)
    gates = route_weights.reshape(row_total, TOP)
    experts = jnp.arange(peer_count, dtype=jnp.int32)
    table = jnp.sum(jnp.where(ids[:, :, None] == experts, gates[:, :, None], 0.0), axis=1)
    high = lax.reduce_precision(table, 8, 7)
    low = (table - high).astype(bf16)
    pad = -2 * peer_count % 128
    row = jnp.concatenate(
        [rows_flat, high.astype(bf16), low, jnp.zeros((row_total, pad), bf16)], axis=1
    )
    line = [row]
    across = [flip(row, dy=1)]
    for mask in reversed(masks):
        fresh = [flip(x, dz=mask) for x in line]
        across = across + [flip(x, dy=1) for x in fresh]
        line = line + fresh

    first_slot = position * local_reqs
    blocks = dev_count // 2
    block_rows = H * DK // blocks
    line_at = dev // inner
    gray = line_at ^ (line_at >> 1)
    chip = dev % inner
    for bit in range(len(masks) - 1):
        chip = chip * 2 + (gray >> bit) % 2
    owners = swap_pairs // local_reqs
    slot_in = swap_pairs % local_reqs
    local_pair = owners[:, 0] == owners[:, 1]
    owned = owners == position
    held_slot = jnp.where(owned[:, 0], slot_in[:, 0], slot_in[:, 1])
    pair = side
    pick = jnp.stack([chip, held_slot[1 - pair], held_slot[pair]]).astype(jnp.int32)

    def state_spec(which):
        return pl.BlockSpec(
            (1, 1, block_rows, DV), lambda g, s: (s[which], jnp.bitwise_xor(g, s[0]), 0, 0)
        )

    packed = jax.ShapeDtypeStruct((blocks, block_rows, DV), bf16)
    out_spec = pl.BlockSpec((1, block_rows, DV), lambda g, s: (g, 0, 0))
    state_blocks = states.reshape(local_reqs, blocks, block_rows, DV)
    send, keep = pl.pallas_call(
        pack_kernel,
        out_shape=(packed, packed),
        grid_spec=pltpu.PrefetchScalarGridSpec(
            num_scalar_prefetch=1,
            grid=(blocks,),
            in_specs=[state_spec(1), state_spec(2)],
            out_specs=[out_spec, out_spec],
        ),
        name="pack",
    )(pick, state_blocks, state_blocks)
    homes = lax.dynamic_index_in_dim(owners, pair, 0, keepdims=False)
    one, two = homes[0], homes[1]
    from_core = flip(send, ds=1)
    held = jnp.where((one == position) | (two == position), keep, from_core)
    cube = [(dev, one // side_count, two // side_count, dict(dy=1))]
    for mask in masks:
        me, x, y, _ = cube[-1]
        cube.append((me // 2, x // 2, y // 2, dict(dz=mask)))
    up = []
    for me, x, y, way in cube[:-1]:
        n = held.shape[0] // 2
        came = flip(held[n:], **way)
        apart = (x // 2 == y // 2) & (x // 2 == me // 2) & (x != y)
        up.append((held[:n], came, apart, way))
        held = jnp.where((x == me) | (y == me), held[:n], came)
    needed = flip(held, **cube[-1][3])
    for own_half, came, apart, way in reversed(up):
        back = flip(jnp.where(apart, own_half, needed), **way)
        needed = jnp.concatenate([jnp.where(apart, came, needed), back])
    cores_apart = (one // side_count == dev) & (two // side_count == dev) & (one != two)
    other = flip(jnp.where(cores_apart, keep, needed), ds=1)

    lanes = H * DK
    vec_spec = pl.BlockSpec((1, T_MAX, lanes), lambda r, c: (r, 0, 0))

    per_head = [
        (2 * T_MAX, 3 * DK, bf16),
        (2 * T_MAX, DV, f32),
        (3 * T_MAX, DK, bf16),
        (8, DK, f32),
    ]
    prepared = pl.pallas_call(
        prep_kernel,
        out_shape=[jax.ShapeDtypeStruct((local_reqs, H, n, m), t) for n, m, t in per_head],
        grid_spec=pltpu.PrefetchScalarGridSpec(
            num_scalar_prefetch=1,
            grid=(local_reqs,),
            in_specs=[vec_spec] * 4 + [pl.BlockSpec((1, T_MAX, H), lambda r, c: (r, 0, 0))],
            out_specs=[
                pl.BlockSpec((1, H, n, m), lambda r, c: (r, 0, 0, 0)) for n, m, t in per_head
            ],
        ),
        compiler_params=pltpu.CompilerParams(vmem_limit_bytes=VMEM_LIMIT),
        name="prep",
    )(token_counts, query_vectors, key_vectors, value_vectors, decay_log, write_rate)

    def feed(x):
        gate = x[:, D:].astype(f32)
        picked = (experts == position).astype(f32)
        weight = jnp.sum(
            (gate[:, :peer_count] + gate[:, peer_count : 2 * peer_count]) * picked, axis=1
        )
        gate_up = jnp.dot(x[:, :D], gate_up_weight[0], preferred_element_type=f32)
        activated = (jax.nn.silu(gate_up[:, :FF]) * gate_up[:, FF:]).astype(bf16)
        produced = jnp.dot(activated, down_weight[0], preferred_element_type=f32)
        return (produced * weight[:, None]).astype(bf16)

    def chip_sum(group):
        n = group.shape[0]
        fed = feed(jnp.concatenate([group, flip(group, ds=1)]))
        return fed[:n].astype(f32) + flip(fed[n:], ds=1).astype(f32)

    near = chip_sum(jnp.concatenate(line))
    far = chip_sum(jnp.concatenate(across)).astype(bf16)

    def chunk(x, k):
        return x[k * row_total : (k + 1) * row_total]

    def total_of(k, level):
        if level == 0:
            return chunk(near, k) + flip(chunk(far, k), dy=1).astype(f32)
        n = outer >> level
        mask = masks[level - 1]
        return total_of(k, level - 1) + flip(
            total_of(k + n, level - 1).astype(bf16), dz=mask
        ).astype(f32)

    expert_out = total_of(0, len(masks)).astype(bf16).reshape(local_reqs, T_MAX, D)

    my_slots = first_slot + jnp.arange(local_reqs, dtype=jnp.int32)
    match = my_slots[:, None, None] == swap_pairs[None]
    mine_pair = jnp.arange(side_count, dtype=jnp.int32) == pair
    kind = jnp.where(local_pair, 1, jnp.where(mine_pair, jnp.where(cores_apart, 3, 2), 4))
    source = jnp.sum(jnp.where(match, kind[None, :, None], 0), axis=(1, 2))
    scalars = jnp.concatenate([chip[None], source]).astype(jnp.int32)
    heads = H // 2

    def head_spec(n, m):
        return pl.BlockSpec((1, heads, n, m), lambda r, g, s: (r, g, 0, 0))

    piece_spec = pl.BlockSpec((blocks, block_rows, DV), lambda r, g, s: (0, 0, 0))
    new_states, attention_out = pl.pallas_call(
        functools.partial(finish_kernel, heads, block_rows),
        out_shape=(
            jax.ShapeDtypeStruct(states.shape, f32),
            jax.ShapeDtypeStruct(query_vectors.shape, bf16),
        ),
        grid_spec=pltpu.PrefetchScalarGridSpec(
            num_scalar_prefetch=1,
            grid=(local_reqs, H // heads),
            in_specs=[pl.BlockSpec((local_reqs, heads, DK, DV), lambda r, g, s: (0, g, 0, 0))]
            + [piece_spec] * 3
            + [head_spec(n, m) for n, m, _ in per_head],
            out_specs=[
                head_spec(DK, DV),
                pl.BlockSpec((1, T_MAX, heads * DV), lambda r, g, s: (r, 0, g)),
            ],
        ),
        compiler_params=pltpu.CompilerParams(vmem_limit_bytes=VMEM_LIMIT),
        name="finish",
    )(scalars, states, needed, from_core, other, *prepared)
    return (new_states, attention_out, expert_out)


def solution(mesh):
    slots = P(("groups", "dev", "side"))
    experts = P(("dev", "side"))
    in_specs = (slots, P("groups")) + (slots,) * 9 + (experts, experts)
    return jax.shard_map(
        per_device, mesh=mesh, in_specs=in_specs, out_specs=(slots, slots, slots), check_vma=False
    )
```

time: 141 us -> 102 us (0.72)
  waiting for transfers between devices: 62.4 us -> 30.7 us
  Pallas kernels: 28.6 us -> 17.2 us
  between operations: 0.98 us -> 9.01 us
  local copies, waits for them, and re-layouts: 9.53 us -> 7.12 us
    ppermute x28 -> x25, waiting for transfers between devices: 62.4 us -> 30.7 us  [flip(): return lax.ppermute(x, AXES, pairs)]
    pallas_call x2, Pallas kernels: 22.3 us -> 13 us  [the longest x1 7.25 us: per_device(): pl.pallas_call(functools.partial(finish_kernel, heads, block_rows), out_s...]
    unnamed x43 -> x34, local copies, waits for them, and re-layouts: 6.86 us -> 4.38 us
    pallas_call x1, Pallas kernels: 6.33 us -> 4.22 us  [per_device(): pl.pallas_call(pack_kernel, out_shape=(packed, packed), grid_spec=pltpu.P...]
    convert_element_type x2 -> x3, other arithmetic: 2.67 us -> 0.85 us  [the longest x1 0.74 us: per_device(): total_of(0, len(masks)).astype(bf16).reshape(local_reqs, T_MAX, D)]
    another operation x2 -> x1, other arithmetic: 0.08 us -> 1.88 us  [per_device(): jnp.stack([chip, held_slot[1 - pair], held_slot[pair]]).astype(jnp.int32)]
    ppermute x28 -> x25, starting transfers between devices: 27.5 us -> 27.5 us  [flip(): return lax.ppermute(x, AXES, pairs)]
  transfers between devices with their start and end apart: 28 -> 25, of which waited for: 14 -> 9; matrix products, arithmetic and copies ran while one was open for 10% -> 13% of each run, Pallas kernels for 9% -> 17%
where the time goes in v2:
time: 102 us
  waiting for transfers between devices  30.7 us (30%)
  starting transfers between devices  27.5 us (27%)
  Pallas kernels  17.2 us (17%)
  between operations  9.01 us (9%)
  local copies, waits for them, and re-layouts  7.12 us (7%)
  other arithmetic  5.62 us (6%)
  matrix products  4.47 us (4%)
    ppermute x25, waiting for transfers between devices, flip(): return lax.ppermute(x, AXES, pairs)  30.7 us
    ppermute x25, starting transfers between devices, flip(): return lax.ppermute(x, AXES, pairs)  27.5 us
    pallas_call x1, Pallas kernels, per_device(): pl.pallas_call(functools.partial(finish_kernel, heads, block_rows), out_s...  7.25 us
    pallas_call x1, Pallas kernels, per_device(): pl.pallas_call(prep_kernel, out_shape=[jax.ShapeDtypeStruct((local_reqs,...  5.74 us
    unnamed x34, local copies, waits for them, and re-layouts  4.38 us
    pallas_call x1, Pallas kernels, per_device(): pl.pallas_call(pack_kernel, out_shape=(packed, packed), grid_spec=pltpu.P...  4.22 us
    dot_general x2, matrix products, feed(): gate_up = jnp.dot(x[:, :D], gate_up_weight[0], preferred_element_type=f32)  2.76 us
  transfers between devices with their start and end apart: 25, of which 9 were waited for; matrix products, arithmetic and copies ran while one was open for 13% of the time, Pallas kernels for 17%

profile of v2, /device:TPU:0, one launch (start us, length us, event | category | flops | bytes accessed | tf_op | source)
XLA Modules:
  0.0 101.7 jit_solution(5991549207368679007)
XLA Ops:
  0.6 0.9 copy.21
  2.6 1.0 concatenate.29
  3.6 5.1 %collective-permute-start.7 = (bf16[32,2432]{1,0:T(8,128)(2,1)S(1)}, bf16[32,2432]{1,0:T(8,128)(2,1)S(1)}, u32[]{:S(2)}, u32[]{:S(2)}) collective-permute-start(bf16[32,2432]{1,0:T(8,128)(2,1)S(1)} %concatenate.29), channel_id=1, source_target_pairs={{0,12},{1,13},{2,14},{3,15},{4,8},{5,9},{6,10},{7,11},{8,4},{9,5},... | collective-permute-start | bytes 466952 | tf_op jit(solution)/shard_map/ppermute | solution.py:170
  8.7 1.5 %collective-permute-start.12 = (bf16[32,2432]{1,0:T(8,128)(2,1)S(1)}, bf16[32,2432]{1,0:T(8,128)(2,1)S(1)}, u32[]{:S(2)}, u32[]{:S(2)}) collective-permute-start(bf16[32,2432]{1,0:T(8,128)(2,1)S(1)} %concatenate.29), channel_id=1, source_target_pairs={{0,2},{1,3},{2,0},{3,1},{4,6},{5,7},{6,4},{7,5},{8,10},{9,11},{10,... | collective-permute-start | bytes 466952 | tf_op jit(solution)/shard_map/ppermute | solution.py:170
  12.2 1.9 %pad_add_fusion.1.scalars = s32[3]{0:T(128)} fusion(s32[1]{0:T(128)} %bitcast.4, s32[1]{0:T(128)} %bitcast.3, s32[1]{0:T(128)} %bitcast), kind=kLoop, calls=%fused_computation.82 | loop fusion | flops 6 | bytes 24 | tf_op jit(solution)/shard_map/stack | solution.py:208
  14.1 4.2 %pack.1 = (bf16[4,512,128]{2,1,0:T(8,128)(2,1)}, bf16[4,512,128]{2,1,0:T(8,128)(2,1)}) custom-call(s32[3]{0:T(128)} %pad_add_fusion.1.scalars, f32[2,4,512,128]{3,2,1,0:T(8,128)} %bitcast.22, f32[2,4,512,128]{3,2,1,0:T(8,128)} %bitcast.23), custom_call_target="tpu_custom_call" | custom-call | tf_op jit(solution)/shard_map/pack/pallas_call | solution.py:218
  28.4 2.1 %collective-permute-start.9 = (bf16[32,2432]{1,0:T(8,128)(2,1)S(1)}, bf16[32,2432]{1,0:T(8,128)(2,1)S(1)}, u32[]{:S(2)}, u32[]{:S(2)}) collective-permute-start(bf16[32,2432]{1,0:T(8,128)(2,1)S(1)} %collective-permute-done.7), channel_id=1, source_target_pairs={{0,4},{1,5},{2,6},{3,7},{4,0},{5,1},{6,2},{7,3},{8,12},{9,13},{10,... | collective-permute-start | bytes 466952 | tf_op jit(solution)/shard_map/ppermute | solution.py:170
  30.6 1.6 %collective-permute-start.14 = (bf16[32,2432]{1,0:T(8,128)(2,1)S(1)}, bf16[32,2432]{1,0:T(8,128)(2,1)S(1)}, u32[]{:S(2)}, u32[]{:S(2)}) collective-permute-start(bf16[32,2432]{1,0:T(8,128)(2,1)S(1)} %collective-permute-done.8), channel_id=1, source_target_pairs={{0,2},{1,3},{2,0},{3,1},{4,6},{5,7},{6,4},{7,5},{8,10},{9,11},{10,... | collective-permute-start | bytes 466952 | tf_op jit(solution)/shard_map/ppermute | solution.py:170
  33.5 1.4 %collective-permute-done.9 = bf16[32,2432]{1,0:T(8,128)(2,1)S(1)} collective-permute-done((bf16[32,2432]{1,0:T(8,128)(2,1)S(1)}, bf16[32,2432]{1,0:T(8,128)(2,1)S(1)}, u32[]{:S(2)}, u32[]{:S(2)}) %collective-permute-start.9) | collective-permute-done | bytes 155680 | tf_op jit(solution)/shard_map/ppermute | solution.py:170
  35.1 1.6 %collective-permute-start.15 = (bf16[32,2432]{1,0:T(8,128)(2,1)S(1)}, bf16[32,2432]{1,0:T(8,128)(2,1)S(1)}, u32[]{:S(2)}, u32[]{:S(2)}) collective-permute-start(bf16[32,2432]{1,0:T(8,128)(2,1)S(1)} %collective-permute-done.9), channel_id=1, source_target_pairs={{0,2},{1,3},{2,0},{3,1},{4,6},{5,7},{6,4},{7,5},{8,10},{9,11},{10,... | collective-permute-start | bytes 466952 | tf_op jit(solution)/shard_map/ppermute | solution.py:170
  38.4 3.6 %collective-permute-done.15 = bf16[32,2432]{1,0:T(8,128)(2,1)S(1)} collective-permute-done((bf16[32,2432]{1,0:T(8,128)(2,1)S(1)}, bf16[32,2432]{1,0:T(8,128)(2,1)S(1)}, u32[]{:S(2)}, u32[]{:S(2)}) %collective-permute-start.15) | collective-permute-done | bytes 155680 | tf_op jit(solution)/shard_map/ppermute | solution.py:170
  42.1 5.0 %collective-permute-done.1 = bf16[2,512,128]{2,1,0:T(8,128)(2,1)S(1)} collective-permute-done((bf16[2,512,128]{2,1,0:T(8,128)(2,1)S(1)}, bf16[2,512,128]{2,1,0:T(8,128)(2,1)S(1)}, u32[]{:S(2)}, u32[]{:S(2)}) %collective-permute-start.1) | collective-permute-done | bytes 262176 | tf_op jit(solution)/shard_map/ppermute | solution.py:170
  47.2 1.8 %collective-permute-start.2 = (bf16[1,512,128]{2,1,0:T(8,128)(2,1)S(1)}, bf16[1,512,128]{2,1,0:T(8,128)(2,1)S(1)}, u32[]{:S(2)}, u32[]{:S(2)}) collective-permute-start(bf16[1,512,128]{2,1,0:T(8,128)(2,1)S(1)} %slice.146), channel_id=1, source_target_pairs={{0,4},{1,5},{2,6},{3,7},{4,0},{5,1},{6,2},{7,3},{8,12},{9,13},{10,... | collective-permute-start | bytes 393224 | tf_op jit(solution)/shard_map/ppermute | solution.py:170
  49.0 3.3 %collective-permute-done.2 = bf16[1,512,128]{2,1,0:T(8,128)(2,1)S(1)} collective-permute-done((bf16[1,512,128]{2,1,0:T(8,128)(2,1)S(1)}, bf16[1,512,128]{2,1,0:T(8,128)(2,1)S(1)}, u32[]{:S(2)}, u32[]{:S(2)}) %collective-permute-start.2) | collective-permute-done | bytes 131104 | tf_op jit(solution)/shard_map/ppermute | solution.py:170
  53.0 1.4 %fusion.2 = f32[256,1024]{1,0:T(8,128)S(1)} fusion(bf16[1,2304,1024]{2,1,0:T(8,128)(2,1)S(1)} %copy-done.11, bf16[256,2432]{1,0:T(8,128)(2,1)S(1)} %constant_dynamic-update-slice_fusion), kind=kOutput, calls=%fused_computation.2 | convolution fusion | flops 1207959552 | bytes 6946816 | tf_op jit(solution)/shard_map/dot_general | solution.py:281
  54.4 4.9 %collective-permute-done.3 = bf16[1,512,128]{2,1,0:T(8,128)(2,1)S(1)} collective-permute-done((bf16[1,512,128]{2,1,0:T(8,128)(2,1)S(1)}, bf16[1,512,128]{2,1,0:T(8,128)(2,1)S(1)}, u32[]{:S(2)}, u32[]{:S(2)}) %collective-permute-start.3) | collective-permute-done | bytes 131104 | tf_op jit(solution)/shard_map/ppermute | solution.py:170
  59.3 1.9 %collective-permute-start.4 = (bf16[1,512,128]{2,1,0:T(8,128)(2,1)S(1)}, bf16[1,512,128]{2,1,0:T(8,128)(2,1)S(1)}, u32[]{:S(2)}, u32[]{:S(2)}) collective-permute-start(bf16[1,512,128]{2,1,0:T(8,128)(2,1)S(1)} %get-tuple-element.34), channel_id=1, source_target_pairs={{0,4},{1,5},{2,6},{3,7},{4,0},{5,1},{6,2},{7,3},{8,12},{9,13},{10,... | collective-permute-start | bytes 393224 | tf_op jit(solution)/shard_map/ppermute | solution.py:170
  61.3 1.4 %fusion = f32[256,1024]{1,0:T(8,128)S(1)} fusion(bf16[1,2304,1024]{2,1,0:T(8,128)(2,1)S(1)} %copy-done.11, bf16[256,2432]{1,0:T(8,128)(2,1)S(1)} %constant_dynamic-update-slice_fusion.5), kind=kOutput, calls=%fused_computation | convolution fusion | flops 1207959552 | bytes 6946816 | tf_op jit(solution)/shard_map/dot_general | solution.py:281
  62.9 0.9 fusion.5
  63.9 0.9 fusion.4
  65.5 1.6 %collective-permute-start.5 = (bf16[2,512,128]{2,1,0:T(8,128)(2,1)S(1)}, bf16[2,512,128]{2,1,0:T(8,128)(2,1)S(1)}, u32[]{:S(2)}, u32[]{:S(2)}) collective-permute-start(bf16[2,512,128]{2,1,0:T(8,128)(2,1)S(1)} %get-tuple-element.32), channel_id=1, source_target_pairs={{0,2},{1,3},{2,0},{3,1},{4,6},{5,7},{6,4},{7,5},{8,10},{9,11},{10,... | collective-permute-start | bytes 786440 | tf_op jit(solution)/shard_map/ppermute | solution.py:170
  67.8 1.5 %collective-permute-start.22 = (bf16[32,2304]{1,0:T(8,128)(2,1)S(1)}, bf16[32,2304]{1,0:T(8,128)(2,1)S(1)}, u32[]{:S(2)}, u32[]{:S(2)}) collective-permute-start(bf16[32,2304]{1,0:T(8,128)(2,1)S(1)} %get-tuple-element.26), channel_id=1, source_target_pairs={{0,2},{1,3},{2,0},{3,1},{4,6},{5,7},{6,4},{7,5},{8,10},{9,11},{10,... | collective-permute-start | bytes 442376 | tf_op jit(solution)/shard_map/ppermute | solution.py:170
  70.0 7.8 %collective-permute-done.19 = bf16[32,2304]{1,0:T(8,128)(2,1)S(1)} collective-permute-done((bf16[32,2304]{1,0:T(8,128)(2,1)S(1)}, bf16[32,2304]{1,0:T(8,128)(2,1)S(1)}, u32[]{:S(2)}, u32[]{:S(2)}) %collective-permute-start.19) | collective-permute-done | bytes 147488 | tf_op jit(solution)/shard_map/ppermute | solution.py:170
  77.9 3.2 %collective-permute-done.22 = bf16[32,2304]{1,0:T(8,128)(2,1)S(1)} collective-permute-done((bf16[32,2304]{1,0:T(8,128)(2,1)S(1)}, bf16[32,2304]{1,0:T(8,128)(2,1)S(1)}, u32[]{:S(2)}, u32[]{:S(2)}) %collective-permute-start.22) | collective-permute-done | bytes 147488 | tf_op jit(solution)/shard_map/ppermute | solution.py:170
  81.1 0.9 collective-permute-start.23
  82.2 1.6 %collective-permute-start.18 = (bf16[32,2304]{1,0:T(8,128)(2,1)S(1)}, bf16[32,2304]{1,0:T(8,128)(2,1)S(1)}, u32[]{:S(2)}, u32[]{:S(2)}) collective-permute-start(bf16[32,2304]{1,0:T(8,128)(2,1)S(1)} %get-tuple-element.25), channel_id=1, source_target_pairs={{0,2},{1,3},{2,0},{3,1},{4,6},{5,7},{6,4},{7,5},{8,10},{9,11},{10,... | collective-permute-start | bytes 442376 | tf_op jit(solution)/shard_map/ppermute | solution.py:170
  83.8 1.2 %collective-permute-start.20 = (bf16[32,2304]{1,0:T(8,128)(2,1)S(1)}, bf16[32,2304]{1,0:T(8,128)(2,1)S(1)}, u32[]{:S(2)}, u32[]{:S(2)}) collective-permute-start(bf16[32,2304]{1,0:T(8,128)(2,1)S(1)} %get-tuple-element.23), channel_id=1, source_target_pairs={{0,4},{1,5},{2,6},{3,7},{4,0},{5,1},{6,2},{7,3},{8,12},{9,13},{10,... | collective-permute-start | bytes 442376 | tf_op jit(solution)/shard_map/ppermute | solution.py:170
  85.0 1.3 %collective-permute-done.23 = bf16[32,2304]{1,0:T(8,128)(2,1)S(1)} collective-permute-done((bf16[32,2304]{1,0:T(8,128)(2,1)S(1)}, bf16[32,2304]{1,0:T(8,128)(2,1)S(1)}, u32[]{:S(2)}, u32[]{:S(2)}) %collective-permute-start.23) | collective-permute-done | bytes 147488 | tf_op jit(solution)/shard_map/ppermute | solution.py:170
  86.3 1.2 %collective-permute-start.24 = (bf16[32,2304]{1,0:T(8,128)(2,1)S(1)}, bf16[32,2304]{1,0:T(8,128)(2,1)S(1)}, u32[]{:S(2)}, u32[]{:S(2)}) collective-permute-start(bf16[32,2304]{1,0:T(8,128)(2,1)S(1)} %fusion.14), channel_id=1, source_target_pairs={{0,12},{1,13},{2,14},{3,15},{4,8},{5,9},{6,10},{7,11},{8,4},{9,5},... | collective-permute-start | bytes 442376 | tf_op jit(solution)/shard_map/ppermute | solution.py:170
  87.8 5.7 %prep.1 = (bf16[2,16,32,384]{3,2,1,0:T(8,128)(2,1)S(1)}, f32[2,16,32,128]{3,2,1,0:T(8,128)S(1)}, bf16[2,16,48,128]{3,2,1,0:T(8,128)(2,1)S(1)}, f32[2,16,8,128]{3,2,1,0:T(8,128)S(1)}) custom-call(s32[2]{0:T(128)S(1)} %copy-done.7, bf16[2,16,2048]{2,1,0:T(8,128)(2,1)S(1)} %copy-done.3, bf16[2,16,2048]{2,1,0:T(8,128)(2,1)S(1)} %copy-done.4, ...), custom_call_target="tpu_custom_call" | custom-call | tf_op jit(solution)/shard_map/prep/pallas_call | solution.py:260
  93.6 7.3 %finish.1 = (f32[2,16,128,128]{3,2,1,0:T(8,128)}, bf16[2,16,2048]{2,1,0:T(8,128)(2,1)}) custom-call(s32[3]{0:T(128)S(1)} %pad_add_fusion.scalars, f32[2,16,128,128]{3,2,1,0:T(8,128)S(1)} %copy-done.1, bf16[4,512,128]{2,1,0:T(8,128)(2,1)S(1)} %get-tuple-element.30.mine, bf16[4,512,128]{2,1,0:T(8,128)(2,1)S(1)} %collective-permute-done.near, ...), custom_call_target="tpu_custom_call" | custom-call | tf_op jit(solution)/shard_map/finish/pallas_call | solution.py:320
  100.9 0.7 fusion.18
  (103 shorter events, 12.3 us)
Async XLA Ops:
  0.6 62.3 %copy-start = (bf16[1,512,2304]{2,1,0:T(8,128)(2,1)S(1)}, bf16[1,512,2304]{2,1,0:T(8,128)(2,1)}, u32[]{:S(2)}) copy-start(bf16[1,512,2304]{2,1,0:T(8,128)(2,1)} %param.25) | copy-start | bytes 7077892
  3.6 24.2 %collective-permute-start.7 = (bf16[32,2432]{1,0:T(8,128)(2,1)S(1)}, bf16[32,2432]{1,0:T(8,128)(2,1)S(1)}, u32[]{:S(2)}, u32[]{:S(2)}) collective-permute-start(bf16[32,2432]{1,0:T(8,128)(2,1)S(1)} %concatenate.29), channel_id=1, source_target_pairs={{0,12},{1,13},{2,14},{3,15},{4,8},{5,9},{6,10},{7,11},{8,4},{9,5},... | collective-permute-start | bytes 466952 | tf_op jit(solution)/shard_map/ppermute | solution.py:170
  8.7 21.8 %collective-permute-start.12 = (bf16[32,2432]{1,0:T(8,128)(2,1)S(1)}, bf16[32,2432]{1,0:T(8,128)(2,1)S(1)}, u32[]{:S(2)}, u32[]{:S(2)}) collective-permute-start(bf16[32,2432]{1,0:T(8,128)(2,1)S(1)} %concatenate.29), channel_id=1, source_target_pairs={{0,2},{1,3},{2,0},{3,1},{4,6},{5,7},{6,4},{7,5},{8,10},{9,11},{10,... | collective-permute-start | bytes 466952 | tf_op jit(solution)/shard_map/ppermute | solution.py:170
  10.2 20.3 %collective-permute-start.8 = (bf16[32,2432]{1,0:T(8,128)(2,1)S(1)}, bf16[32,2432]{1,0:T(8,128)(2,1)S(1)}, u32[]{:S(2)}, u32[]{:S(2)}) collective-permute-start(bf16[32,2432]{1,0:T(8,128)(2,1)S(1)} %concatenate.29), channel_id=1, source_target_pairs={{0,4},{1,5},{2,6},{3,7},{4,0},{5,1},{6,2},{7,3},{8,12},{9,13},{10,... | collective-permute-start | bytes 466952 | tf_op jit(solution)/shard_map/ppermute | solution.py:170
  18.3 19.3 %collective-permute-start = (bf16[4,512,128]{2,1,0:T(8,128)(2,1)}, bf16[4,512,128]{2,1,0:T(8,128)(2,1)S(1)}, u32[]{:S(2)}, u32[]{:S(2)}) collective-permute-start(bf16[4,512,128]{2,1,0:T(8,128)(2,1)} %get-tuple-element.12), channel_id=1, source_target_pairs={{0,1},{1,0},{2,3},{3,2},{4,5},{5,4},{6,7},{7,6},{8,9},{9,8},{10,11... | collective-permute-start | bytes 1572872 | tf_op jit(solution)/shard_map/ppermute | solution.py:170
  27.8 9.6 %collective-permute-start.13 = (bf16[32,2432]{1,0:T(8,128)(2,1)S(1)}, bf16[32,2432]{1,0:T(8,128)(2,1)S(1)}, u32[]{:S(2)}, u32[]{:S(2)}) collective-permute-start(bf16[32,2432]{1,0:T(8,128)(2,1)S(1)} %collective-permute-done.7), channel_id=1, source_target_pairs={{0,2},{1,3},{2,0},{3,1},{4,6},{5,7},{6,4},{7,5},{8,10},{9,11},{10,... | collective-permute-start | bytes 466952 | tf_op jit(solution)/shard_map/ppermute | solution.py:170
  28.4 6.5 %collective-permute-start.9 = (bf16[32,2432]{1,0:T(8,128)(2,1)S(1)}, bf16[32,2432]{1,0:T(8,128)(2,1)S(1)}, u32[]{:S(2)}, u32[]{:S(2)}) collective-permute-start(bf16[32,2432]{1,0:T(8,128)(2,1)S(1)} %collective-permute-done.7), channel_id=1, source_target_pairs={{0,4},{1,5},{2,6},{3,7},{4,0},{5,1},{6,2},{7,3},{8,12},{9,13},{10,... | collective-permute-start | bytes 466952 | tf_op jit(solution)/shard_map/ppermute | solution.py:170
  30.6 7.0 %collective-permute-start.14 = (bf16[32,2432]{1,0:T(8,128)(2,1)S(1)}, bf16[32,2432]{1,0:T(8,128)(2,1)S(1)}, u32[]{:S(2)}, u32[]{:S(2)}) collective-permute-start(bf16[32,2432]{1,0:T(8,128)(2,1)S(1)} %collective-permute-done.8), channel_id=1, source_target_pairs={{0,2},{1,3},{2,0},{3,1},{4,6},{5,7},{6,4},{7,5},{8,10},{9,11},{10,... | collective-permute-start | bytes 466952 | tf_op jit(solution)/shard_map/ppermute | solution.py:170
  35.0 17.9 %collective-permute-start.10 = (bf16[128,2432]{1,0:T(8,128)(2,1)S(1)}, bf16[128,2432]{1,0:T(8,128)(2,1)S(1)}, u32[]{:S(2)}, u32[]{:S(2)}) collective-permute-start(bf16[128,2432]{1,0:T(8,128)(2,1)S(1)} %pad_maximum_fusion), channel_id=1, source_target_pairs={{0,1},{1,0},{2,3},{3,2},{4,5},{5,4},{6,7},{7,6},{8,9},{9,8},{10,11... | collective-permute-start | bytes 1867784 | tf_op jit(solution)/shard_map/ppermute | solution.py:170
  35.1 6.9 %collective-permute-start.15 = (bf16[32,2432]{1,0:T(8,128)(2,1)S(1)}, bf16[32,2432]{1,0:T(8,128)(2,1)S(1)}, u32[]{:S(2)}, u32[]{:S(2)}) collective-permute-start(bf16[32,2432]{1,0:T(8,128)(2,1)S(1)} %collective-permute-done.9), channel_id=1, source_target_pairs={{0,2},{1,3},{2,0},{3,1},{4,6},{5,7},{6,4},{7,5},{8,10},{9,11},{10,... | collective-permute-start | bytes 466952 | tf_op jit(solution)/shard_map/ppermute | solution.py:170
  36.7 16.3 %copy-start.11 = (bf16[1,2304,1024]{2,1,0:T(8,128)(2,1)S(1)}, bf16[1,2304,1024]{2,1,0:T(8,128)(2,1)}, u32[]{:S(2)}) copy-start(bf16[1,2304,1024]{2,1,0:T(8,128)(2,1)} %param.24) | copy-start | bytes 14155780
  37.7 15.2 %copy-start.9 = (bf16[256,2432]{1,0:T(8,128)(2,1)S(1)}, bf16[256,2432]{1,0:T(8,128)(2,1)}, u32[]{:S(2)}) copy-start(bf16[256,2432]{1,0:T(8,128)(2,1)} %constant_dynamic-update-slice_fusion.1) | copy-start | bytes 3735556
  37.7 9.4 %collective-permute-start.1 = (bf16[2,512,128]{2,1,0:T(8,128)(2,1)S(1)}, bf16[2,512,128]{2,1,0:T(8,128)(2,1)S(1)}, u32[]{:S(2)}, u32[]{:S(2)}) collective-permute-start(bf16[2,512,128]{2,1,0:T(8,128)(2,1)S(1)} %slice.144), channel_id=1, source_target_pairs={{0,2},{1,3},{2,0},{3,1},{4,6},{5,7},{6,4},{7,5},{8,10},{9,11},{10,... | collective-permute-start | bytes 786440 | tf_op jit(solution)/shard_map/ppermute | solution.py:170
  42.0 19.2 %collective-permute-start.16 = (bf16[128,2432]{1,0:T(8,128)(2,1)S(1)}, bf16[128,2432]{1,0:T(8,128)(2,1)S(1)}, u32[]{:S(2)}, u32[]{:S(2)}) collective-permute-start(bf16[128,2432]{1,0:T(8,128)(2,1)S(1)} %pad_maximum_fusion.1), channel_id=1, source_target_pairs={{0,1},{1,0},{2,3},{3,2},{4,5},{5,4},{6,7},{7,6},{8,9},{9,8},{10,11... | collective-permute-start | bytes 1867784 | tf_op jit(solution)/shard_map/ppermute | solution.py:170
  47.2 5.1 %collective-permute-start.2 = (bf16[1,512,128]{2,1,0:T(8,128)(2,1)S(1)}, bf16[1,512,128]{2,1,0:T(8,128)(2,1)S(1)}, u32[]{:S(2)}, u32[]{:S(2)}) collective-permute-start(bf16[1,512,128]{2,1,0:T(8,128)(2,1)S(1)} %slice.146), channel_id=1, source_target_pairs={{0,4},{1,5},{2,6},{3,7},{4,0},{5,1},{6,2},{7,3},{8,12},{9,13},{10,... | collective-permute-start | bytes 393224 | tf_op jit(solution)/shard_map/ppermute | solution.py:170
  52.3 6.9 %collective-permute-start.3 = (bf16[1,512,128]{2,1,0:T(8,128)(2,1)S(1)}, bf16[1,512,128]{2,1,0:T(8,128)(2,1)S(1)}, u32[]{:S(2)}, u32[]{:S(2)}) collective-permute-start(bf16[1,512,128]{2,1,0:T(8,128)(2,1)S(1)} %broadcast_select_fusion.5), channel_id=1, source_target_pairs={{0,12},{1,13},{2,14},{3,15},{4,8},{5,9},{6,10},{7,11},{8,4},{9,5},... | collective-permute-start | bytes 393224 | tf_op jit(solution)/shard_map/ppermute | solution.py:170
  59.3 6.1 %collective-permute-start.4 = (bf16[1,512,128]{2,1,0:T(8,128)(2,1)S(1)}, bf16[1,512,128]{2,1,0:T(8,128)(2,1)S(1)}, u32[]{:S(2)}, u32[]{:S(2)}) collective-permute-start(bf16[1,512,128]{2,1,0:T(8,128)(2,1)S(1)} %get-tuple-element.34), channel_id=1, source_target_pairs={{0,4},{1,5},{2,6},{3,7},{4,0},{5,1},{6,2},{7,3},{8,12},{9,13},{10,... | collective-permute-start | bytes 393224 | tf_op jit(solution)/shard_map/ppermute | solution.py:170
  63.9 3.2 %collective-permute-start.17 = (bf16[128,2304]{1,0:T(8,128)(2,1)S(1)}, bf16[128,2304]{1,0:T(8,128)(2,1)S(1)}, u32[]{:S(2)}, u32[]{:S(2)}) collective-permute-start(bf16[128,2304]{1,0:T(8,128)(2,1)S(1)} %slice.164), channel_id=1, source_target_pairs={{0,1},{1,0},{2,3},{3,2},{4,5},{5,4},{6,7},{7,6},{8,9},{9,8},{10,11... | collective-permute-start | bytes 1769480 | tf_op jit(solution)/shard_map/ppermute | solution.py:170
  64.8 5.0 %collective-permute-start.11 = (bf16[128,2304]{1,0:T(8,128)(2,1)S(1)}, bf16[128,2304]{1,0:T(8,128)(2,1)S(1)}, u32[]{:S(2)}, u32[]{:S(2)}) collective-permute-start(bf16[128,2304]{1,0:T(8,128)(2,1)S(1)} %slice.155), channel_id=1, source_target_pairs={{0,1},{1,0},{2,3},{3,2},{4,5},{5,4},{6,7},{7,6},{8,9},{9,8},{10,11... | collective-permute-start | bytes 1769480 | tf_op jit(solution)/shard_map/ppermute | solution.py:170
  65.5 16.5 %collective-permute-start.5 = (bf16[2,512,128]{2,1,0:T(8,128)(2,1)S(1)}, bf16[2,512,128]{2,1,0:T(8,128)(2,1)S(1)}, u32[]{:S(2)}, u32[]{:S(2)}) collective-permute-start(bf16[2,512,128]{2,1,0:T(8,128)(2,1)S(1)} %get-tuple-element.32), channel_id=1, source_target_pairs={{0,2},{1,3},{2,0},{3,1},{4,6},{5,7},{6,4},{7,5},{8,10},{9,11},{10,... | collective-permute-start | bytes 786440 | tf_op jit(solution)/shard_map/ppermute | solution.py:170
  67.3 10.6 %collective-permute-start.19 = (bf16[32,2304]{1,0:T(8,128)(2,1)S(1)}, bf16[32,2304]{1,0:T(8,128)(2,1)S(1)}, u32[]{:S(2)}, u32[]{:S(2)}) collective-permute-start(bf16[32,2304]{1,0:T(8,128)(2,1)S(1)} %get-tuple-element.28), channel_id=1, source_target_pairs={{0,2},{1,3},{2,0},{3,1},{4,6},{5,7},{6,4},{7,5},{8,10},{9,11},{10,... | collective-permute-start | bytes 442376 | tf_op jit(solution)/shard_map/ppermute | solution.py:170
  67.8 13.2 %collective-permute-start.22 = (bf16[32,2304]{1,0:T(8,128)(2,1)S(1)}, bf16[32,2304]{1,0:T(8,128)(2,1)S(1)}, u32[]{:S(2)}, u32[]{:S(2)}) collective-permute-start(bf16[32,2304]{1,0:T(8,128)(2,1)S(1)} %get-tuple-element.26), channel_id=1, source_target_pairs={{0,2},{1,3},{2,0},{3,1},{4,6},{5,7},{6,4},{7,5},{8,10},{9,11},{10,... | collective-permute-start | bytes 442376 | tf_op jit(solution)/shard_map/ppermute | solution.py:170
  69.4 15.7 %collective-permute-start.21 = (bf16[32,2304]{1,0:T(8,128)(2,1)S(1)}, bf16[32,2304]{1,0:T(8,128)(2,1)S(1)}, u32[]{:S(2)}, u32[]{:S(2)}) collective-permute-start(bf16[32,2304]{1,0:T(8,128)(2,1)S(1)} %get-tuple-element.27), channel_id=1, source_target_pairs={{0,2},{1,3},{2,0},{3,1},{4,6},{5,7},{6,4},{7,5},{8,10},{9,11},{10,... | collective-permute-start | bytes 442376 | tf_op jit(solution)/shard_map/ppermute | solution.py:170
  81.1 5.2 %collective-permute-start.23 = (bf16[32,2304]{1,0:T(8,128)(2,1)S(1)}, bf16[32,2304]{1,0:T(8,128)(2,1)S(1)}, u32[]{:S(2)}, u32[]{:S(2)}) collective-permute-start(bf16[32,2304]{1,0:T(8,128)(2,1)S(1)} %get-tuple-element.24), channel_id=1, source_target_pairs={{0,4},{1,5},{2,6},{3,7},{4,0},{5,1},{6,2},{7,3},{8,12},{9,13},{10,... | collective-permute-start | bytes 442376 | tf_op jit(solution)/shard_map/ppermute | solution.py:170
  82.0 5.8 %copy-start.3 = (bf16[2,16,2048]{2,1,0:T(8,128)(2,1)S(1)}, bf16[2,16,2048]{2,1,0:T(8,128)(2,1)}, u32[]{:S(2)}) copy-start(bf16[2,16,2048]{2,1,0:T(8,128)(2,1)} %q_ref.1) | copy-start | bytes 393220
  82.0 5.8 %copy-start.4 = (bf16[2,16,2048]{2,1,0:T(8,128)(2,1)S(1)}, bf16[2,16,2048]{2,1,0:T(8,128)(2,1)}, u32[]{:S(2)}) copy-start(bf16[2,16,2048]{2,1,0:T(8,128)(2,1)} %k_ref.1) | copy-start | bytes 393220
  82.0 5.8 %copy-start.5 = (bf16[2,16,2048]{2,1,0:T(8,128)(2,1)S(1)}, bf16[2,16,2048]{2,1,0:T(8,128)(2,1)}, u32[]{:S(2)}) copy-start(bf16[2,16,2048]{2,1,0:T(8,128)(2,1)} %v_ref.1) | copy-start | bytes 393220
  82.0 11.6 %copy-start.1 = (f32[2,16,128,128]{3,2,1,0:T(8,128)S(1)}, f32[2,16,128,128]{3,2,1,0:T(8,128)}, u32[]{:S(2)}) copy-start(f32[2,16,128,128]{3,2,1,0:T(8,128)} %states_ref.1) | copy-start | bytes 6291460
  82.1 11.5 %collective-permute-start.6 = (bf16[4,512,128]{2,1,0:T(8,128)(2,1)S(1)}, bf16[4,512,128]{2,1,0:T(8,128)(2,1)S(1)}, u32[]{:S(2)}, u32[]{:S(2)}) collective-permute-start(bf16[4,512,128]{2,1,0:T(8,128)(2,1)S(1)} %get-tuple-element.29), channel_id=1, source_target_pairs={{0,1},{1,0},{2,3},{3,2},{4,5},{5,4},{6,7},{7,6},{8,9},{9,8},{10,11... | collective-permute-start | bytes 1572872 | tf_op jit(solution)/shard_map/ppermute | solution.py:170
  82.2 18.7 %collective-permute-start.18 = (bf16[32,2304]{1,0:T(8,128)(2,1)S(1)}, bf16[32,2304]{1,0:T(8,128)(2,1)S(1)}, u32[]{:S(2)}, u32[]{:S(2)}) collective-permute-start(bf16[32,2304]{1,0:T(8,128)(2,1)S(1)} %get-tuple-element.25), channel_id=1, source_target_pairs={{0,2},{1,3},{2,0},{3,1},{4,6},{5,7},{6,4},{7,5},{8,10},{9,11},{10,... | collective-permute-start | bytes 442376 | tf_op jit(solution)/shard_map/ppermute | solution.py:170
  83.8 17.1 %collective-permute-start.20 = (bf16[32,2304]{1,0:T(8,128)(2,1)S(1)}, bf16[32,2304]{1,0:T(8,128)(2,1)S(1)}, u32[]{:S(2)}, u32[]{:S(2)}) collective-permute-start(bf16[32,2304]{1,0:T(8,128)(2,1)S(1)} %get-tuple-element.23), channel_id=1, source_target_pairs={{0,4},{1,5},{2,6},{3,7},{4,0},{5,1},{6,2},{7,3},{8,12},{9,13},{10,... | collective-permute-start | bytes 442376 | tf_op jit(solution)/shard_map/ppermute | solution.py:170
  86.3 14.6 %collective-permute-start.24 = (bf16[32,2304]{1,0:T(8,128)(2,1)S(1)}, bf16[32,2304]{1,0:T(8,128)(2,1)S(1)}, u32[]{:S(2)}, u32[]{:S(2)}) collective-permute-start(bf16[32,2304]{1,0:T(8,128)(2,1)S(1)} %fusion.14), channel_id=1, source_target_pairs={{0,12},{1,13},{2,14},{3,15},{4,8},{5,9},{6,10},{7,11},{8,4},{9,5},... | collective-permute-start | bytes 442376 | tf_op jit(solution)/shard_map/ppermute | solution.py:170
  (5 other events, 27.7 us)

commit v3 on v2

--- a/solution.py
+++ b/solution.py
@@ -31,9 +31,56 @@
     )
 
 
-def pack_kernel(scalars, send_in, keep_in, send_ref, keep_ref):
+def rows_kernel(experts, hidden_ref, ids_ref, gates_ref, out_ref):
+    width = out_ref.shape[1] - D
+    for r in range(hidden_ref.shape[0]):
+        here = slice(r * T_MAX, (r + 1) * T_MAX)
+        out_ref[here, :D] = hidden_ref[r]
+        number = lax.broadcasted_iota(jnp.int32, (experts, T_MAX), 0)
+        table = jnp.zeros((experts, T_MAX), jnp.float32)
+        for k in range(TOP):
+            table = jnp.where(ids_ref[r, k : k + 1] == number, gates_ref[r, k : k + 1], table)
+        high = table.astype(jnp.bfloat16).astype(jnp.float32)
+        parts = [high, table - high]
+        if width > 2 * experts:
+            parts.append(jnp.zeros((width - 2 * experts, T_MAX), jnp.float32))
+        out_ref[here, D:] = jnp.transpose(jnp.concatenate(parts, axis=0)).astype(jnp.bfloat16)
+
+
+def chip_of(position, sides, bits):
+    dev = lax.div(position, sides)
+    line_at = lax.shift_right_logical(dev, 1)
+    gray = jnp.bitwise_xor(line_at, lax.shift_right_logical(line_at, 1))
+    chip = jnp.bitwise_and(dev, 1)
+    for bit in range(bits):
+        chip = chip * 2 + jnp.bitwise_and(lax.shift_right_logical(gray, bit), 1)
+    return chip
+
+
+def pack_kernel(sides, slots, levels, swaps, where_at, send_in, keep_in, send_ref, keep_ref, plan):
     send_ref[...] = send_in[0].astype(jnp.bfloat16)
     keep_ref[...] = keep_in[0].astype(jnp.bfloat16)
+
+    @pl.when(pl.program_id(0) == 0)
+    def _():
+        position = where_at[0]
+        pair = lax.rem(position, sides)
+        one = lax.div(swaps[pair, 0], slots)
+        two = lax.div(swaps[pair, 1], slots)
+        me = lax.div(position, sides)
+        x = lax.div(one, sides)
+        y = lax.div(two, sides)
+        flags = [(one == position) | (two == position), (x == me) & (y == me) & (one != two)]
+        for level in range(levels):
+            near = (x == me) | (y == me)
+            differ = x != y
+            x, y, me = x >> 1, y >> 1, me >> 1
+            flags.extend([differ & (x == me) & (y == me), near])
+        row = lax.broadcasted_iota(jnp.int32, plan.shape, 0)
+        value = jnp.zeros(plan.shape, jnp.int32)
+        for i, flag in enumerate(flags):
+            value = jnp.where(row == i, flag.astype(jnp.int32), value)
+        plan[...] = value.astype(jnp.float32).astype(plan.dtype)
 
 
 def unit(vectors):
@@ -89,7 +136,10 @@
 def finish_kernel(
     heads,
     block_rows,
-    scalars,
+    sides,
+    bits,
+    swaps,
+    where_at,
     states_ref,
     mine,
     near,
@@ -103,12 +153,23 @@
 ):
     r = pl.program_id(0)
     first = pl.program_id(1) * heads
-    source = scalars[1 + r]
+    position = where_at[0]
+    slots = states_ref.shape[0]
+    chip = chip_of(position, sides, bits)
+    source = jnp.int32(0)
+    for p in range(swaps.shape[0]):
+        one = lax.div(swaps[p, 0], slots)
+        two = lax.div(swaps[p, 1], slots)
+        apart = lax.div(one, sides) == lax.div(two, sides)
+        kind = jnp.where(lax.rem(position, sides) == p, jnp.where(apart, 3, 2), 4)
+        kind = jnp.where(one == two, 1, kind)
+        slot = position * slots + r
+        source = jnp.where((swaps[p, 0] == slot) | (swaps[p, 1] == slot), kind, source)
     partner = jnp.where(source == 1, 1 - r, r)
     for h in range(heads):
         row = (first + h) * DK
-        block = jnp.bitwise_xor(row // block_rows, scalars[0])
-        at = pl.ds(pl.multiple_of(row % block_rows, DK), DK)
+        block = jnp.bitwise_xor(lax.div(row, block_rows), chip)
+        at = pl.ds(pl.multiple_of(lax.rem(row, block_rows), DK), DK)
         arrived = jnp.where(
             source == 2, mine[block, at], jnp.where(source == 3, near[block, at], other[block, at])
         )
@@ -152,8 +213,6 @@
     side_count = lax.axis_size("side")
     peer_count = dev_count * side_count
     position = lax.axis_index(AXES)
-    side = lax.axis_index("side")
-    dev = lax.axis_index("dev")
     inner = 2
     outer = dev_count // inner
     masks = []
@@ -169,84 +228,62 @@
                 pairs.append((d * side_count + s, to))
         return lax.ppermute(x, AXES, pairs)
 
-    def after(x, *earlier):
-        return lax.optimization_barrier((x, *earlier))[0]
-
     row_total = local_reqs * T_MAX
-    rows_flat = hidden_rows.reshape(row_total, D)
-    ids = expert_ids.reshape(row_total, TOP)
-    gates = route_weights.reshape(row_total, TOP)
     experts = jnp.arange(peer_count, dtype=jnp.int32)
-    table = jnp.sum(jnp.where(ids[:, :, None] == experts, gates[:, :, None], 0.0), axis=1)
-    high = lax.reduce_precision(table, 8, 7)
-    low = (table - high).astype(bf16)
-    pad = -2 * peer_count % 128
-    row = jnp.concatenate(
-        [rows_flat, high.astype(bf16), low, jnp.zeros((row_total, pad), bf16)], axis=1
-    )
+    width = D + -(-2 * peer_count // 128) * 128
+    row = pl.pallas_call(
+        functools.partial(rows_kernel, peer_count),
+        out_shape=jax.ShapeDtypeStruct((row_total, width), bf16),
+        name="rows",
+    )(hidden_rows, jnp.swapaxes(expert_ids, 1, 2), jnp.swapaxes(route_weights, 1, 2))
+    def together(*values):
+        return lax.optimization_barrier(values)
+
     line = [row]
     across = [flip(row, dy=1)]
-    for mask in reversed(masks):
-        fresh = [flip(x, dz=mask) for x in line]
+    direct = [flip(row, dz=mask) for mask in reversed(masks)]
+
+    blocks = dev_count // 2
+    block_rows = H * DK // blocks
+    levels = len(masks)
+    here = position.astype(jnp.int32).reshape(1)
+
+    def state_spec(own):
+        def index(g, swaps, at):
+            pair = lax.rem(at[0], side_count)
+            pair = pair if own else 1 - pair
+            one, two = swaps[pair, 0], swaps[pair, 1]
+            held = jnp.where(lax.div(one, local_reqs) == at[0], one, two)
+            chip = chip_of(at[0], side_count, levels - 1)
+            return (lax.rem(held, local_reqs), jnp.bitwise_xor(g, chip), 0, 0)
+
+        return pl.BlockSpec((1, 1, block_rows, DV), index)
+
+    packed = jax.ShapeDtypeStruct((blocks, block_rows, DV), bf16)
+    out_spec = pl.BlockSpec((1, block_rows, DV), lambda g, swaps, at: (g, 0, 0))
+    state_blocks = states.reshape(local_reqs, blocks, block_rows, DV)
+    send, keep, plan = pl.pallas_call(
+        functools.partial(pack_kernel, side_count, local_reqs, levels),
+        out_shape=(packed, packed, jax.ShapeDtypeStruct((16, DV), bf16)),
+        grid_spec=pltpu.PrefetchScalarGridSpec(
+            num_scalar_prefetch=2,
+            grid=(blocks,),
+            in_specs=[state_spec(False), state_spec(True)],
+            out_specs=[out_spec, out_spec, pl.BlockSpec((16, DV), lambda g, swaps, at: (0, 0))],
+        ),
+        name="pack",
+    )(swap_pairs, here, state_blocks, state_blocks)
+    from_core = flip(send, ds=1)
+
+    def choose(flag, yes, no):
+        return jnp.where(plan[flag] > 0, yes, no)
+
+    held = choose(0, keep, from_core)
+    direct[0], held = together(direct[0], held)
+    for i, mask in enumerate(reversed(masks)):
+        fresh = direct[i : i + 1] + [flip(x, dz=mask) for x in line[1:]]
         across = across + [flip(x, dy=1) for x in fresh]
         line = line + fresh
-
-    first_slot = position * local_reqs
-    blocks = dev_count // 2
-    block_rows = H * DK // blocks
-    line_at = dev // inner
-    gray = line_at ^ (line_at >> 1)
-    chip = dev % inner
-    for bit in range(len(masks) - 1):
-        chip = chip * 2 + (gray >> bit) % 2
-    owners = swap_pairs // local_reqs
-    slot_in = swap_pairs % local_reqs
-    local_pair = owners[:, 0] == owners[:, 1]
-    owned = owners == position
-    held_slot = jnp.where(owned[:, 0], slot_in[:, 0], slot_in[:, 1])
-    pair = side
-    pick = jnp.stack([chip, held_slot[1 - pair], held_slot[pair]]).astype(jnp.int32)
-
-    def state_spec(which):
-        return pl.BlockSpec(
-            (1, 1, block_rows, DV), lambda g, s: (s[which], jnp.bitwise_xor(g, s[0]), 0, 0)
-        )
-
-    packed = jax.ShapeDtypeStruct((blocks, block_rows, DV), bf16)
-    out_spec = pl.BlockSpec((1, block_rows, DV), lambda g, s: (g, 0, 0))
-    state_blocks = states.reshape(local_reqs, blocks, block_rows, DV)
-    send, keep = pl.pallas_call(
-        pack_kernel,
-        out_shape=(packed, packed),
-        grid_spec=pltpu.PrefetchScalarGridSpec(
-            num_scalar_prefetch=1,
-            grid=(blocks,),
-            in_specs=[state_spec(1), state_spec(2)],
-            out_specs=[out_spec, out_spec],
-        ),
-        name="pack",
-    )(pick, state_blocks, state_blocks)
-    homes = lax.dynamic_index_in_dim(owners, pair, 0, keepdims=False)
-    one, two = homes[0], homes[1]
-    from_core = flip(send, ds=1)
-    held = jnp.where((one == position) | (two == position), keep, from_core)
-    cube = [(dev, one // side_count, two // side_count, dict(dy=1))]
-    for mask in masks:
-        me, x, y, _ = cube[-1]
-        cube.append((me // 2, x // 2, y // 2, dict(dz=mask)))
-    up = []
-    for me, x, y, way in cube[:-1]:
-        n = held.shape[0] // 2
-        came = flip(held[n:], **way)
-        apart = (x // 2 == y // 2) & (x // 2 == me // 2) & (x != y)
-        up.append((held[:n], came, apart, way))
-        held = jnp.where((x == me) | (y == me), held[:n], came)
-    needed = flip(held, **cube[-1][3])
-    for own_half, came, apart, way in reversed(up):
-        back = flip(jnp.where(apart, own_half, needed), **way)
-        needed = jnp.concatenate([jnp.where(apart, came, needed), back])
-    cores_apart = (one // side_count == dev) & (two // side_count == dev) & (one != two)
-    other = flip(jnp.where(cores_apart, keep, needed), ds=1)
 
     lanes = H * DK
     vec_spec = pl.BlockSpec((1, T_MAX, lanes), lambda r, c: (r, 0, 0))
@@ -257,6 +294,7 @@
         (3 * T_MAX, DK, bf16),
         (8, DK, f32),
     ]
+    counts, line[-1] = together(token_counts, line[-1])
     prepared = pl.pallas_call(
         prep_kernel,
         out_shape=[jax.ShapeDtypeStruct((local_reqs, H, n, m), t) for n, m, t in per_head],
@@ -270,8 +308,18 @@
         ),
         compiler_params=pltpu.CompilerParams(vmem_limit_bytes=VMEM_LIMIT),
         name="prep",
-    )(token_counts, query_vectors, key_vectors, value_vectors, decay_log, write_rate)
-
+    )(counts, query_vectors, key_vectors, value_vectors, decay_log, write_rate)
+
+    ways = [dict(dy=1)] + [dict(dz=mask) for mask in masks]
+    up = []
+    for level in range(levels):
+        n = held.shape[0] // 2
+        came = flip(held[n:], **ways[level])
+        if level == 0:
+            came, *prepared = lax.optimization_barrier((came, *prepared))
+        up.append((held[:n], came))
+        held = choose(3 + 2 * level, held[:n], came)
+    needed = flip(held, **ways[levels])
     def feed(x):
         gate = x[:, D:].astype(f32)
         picked = (experts == position).astype(f32)
@@ -290,6 +338,13 @@
 
     near = chip_sum(jnp.concatenate(line))
     far = chip_sum(jnp.concatenate(across)).astype(bf16)
+    needed, far = together(needed, far)
+
+    for level in range(levels - 1, -1, -1):
+        own_half, came = up[level]
+        back = flip(choose(2 + 2 * level, own_half, needed), **ways[level])
+        needed = jnp.concatenate([choose(2 + 2 * level, came, needed), back])
+    other = flip(choose(1, keep, needed), ds=1)
 
     def chunk(x, k):
         return x[k * row_total : (k + 1) * row_total]
@@ -305,38 +360,32 @@
 
     expert_out = total_of(0, len(masks)).astype(bf16).reshape(local_reqs, T_MAX, D)
 
-    my_slots = first_slot + jnp.arange(local_reqs, dtype=jnp.int32)
-    match = my_slots[:, None, None] == swap_pairs[None]
-    mine_pair = jnp.arange(side_count, dtype=jnp.int32) == pair
-    kind = jnp.where(local_pair, 1, jnp.where(mine_pair, jnp.where(cores_apart, 3, 2), 4))
-    source = jnp.sum(jnp.where(match, kind[None, :, None], 0), axis=(1, 2))
-    scalars = jnp.concatenate([chip[None], source]).astype(jnp.int32)
     heads = H // 2
 
     def head_spec(n, m):
-        return pl.BlockSpec((1, heads, n, m), lambda r, g, s: (r, g, 0, 0))
-
-    piece_spec = pl.BlockSpec((blocks, block_rows, DV), lambda r, g, s: (0, 0, 0))
+        return pl.BlockSpec((1, heads, n, m), lambda r, g, swaps, at: (r, g, 0, 0))
+
+    piece_spec = pl.BlockSpec((blocks, block_rows, DV), lambda r, g, swaps, at: (0, 0, 0))
     new_states, attention_out = pl.pallas_call(
-        functools.partial(finish_kernel, heads, block_rows),
+        functools.partial(finish_kernel, heads, block_rows, side_count, levels - 1),
         out_shape=(
             jax.ShapeDtypeStruct(states.shape, f32),
             jax.ShapeDtypeStruct(query_vectors.shape, bf16),
         ),
         grid_spec=pltpu.PrefetchScalarGridSpec(
-            num_scalar_prefetch=1,
+            num_scalar_prefetch=2,
             grid=(local_reqs, H // heads),
-            in_specs=[pl.BlockSpec((local_reqs, heads, DK, DV), lambda r, g, s: (0, g, 0, 0))]
+            in_specs=[pl.BlockSpec((local_reqs, heads, DK, DV), lambda r, g, swaps, at: (0, g, 0, 0))]
             + [piece_spec] * 3
             + [head_spec(n, m) for n, m, _ in per_head],
             out_specs=[
                 head_spec(DK, DV),
-                pl.BlockSpec((1, T_MAX, heads * DV), lambda r, g, s: (r, 0, g)),
+                pl.BlockSpec((1, T_MAX, heads * DV), lambda r, g, swaps, at: (r, 0, g)),
             ],
         ),
         compiler_params=pltpu.CompilerParams(vmem_limit_bytes=VMEM_LIMIT),
         name="finish",
-    )(scalars, states, needed, from_core, other, *prepared)
+    )(swap_pairs, here, states, needed, from_core, other, *prepared)
     return (new_states, attention_out, expert_out)
 
 

time: 102 us -> 79.4 us (0.78)
  waiting for transfers between devices: 30.7 us -> 19 us
  between operations: 9.01 us -> 1.07 us
  local copies, waits for them, and re-layouts: 7.12 us -> 0.49 us
  matrix products: 4.47 us -> 7.08 us
  Pallas kernels: 17.2 us -> 19.4 us
  other arithmetic: 5.62 us -> 3.72 us
    ppermute x25, waiting for transfers between devices: 30.7 us -> 19 us  [flip(): return lax.ppermute(x, AXES, pairs)]
    unnamed x34, local copies, waits for them, and re-layouts: 4.38 us -> 0.21 us
    dot_general x2, matrix products: 2.76 us -> 5.39 us  [feed(): gate_up = jnp.dot(x[:, :D], gate_up_weight[0], preferred_element_type=f32)]
    pallas_call x2 -> x3, Pallas kernels: 11.5 us -> 13.7 us  [the longest x1 7.35 us: per_device(): pl.pallas_call(functools.partial(finish_kernel, heads, block_rows, side_c...]
    another operation x1 -> x0, other arithmetic: 1.88 us -> none  [per_device(): jnp.stack([chip, held_slot[1 - pair], held_slot[pair]]).astype(jnp.int32)]
  transfers between devices with their start and end apart: 25 -> 25, of which waited for: 9 -> 9; matrix products, arithmetic and copies ran while one was open for 13% -> 14% of each run, Pallas kernels for 17% -> 13%
where the time goes in v3:
time: 79.4 us; the launch traced here: 79.1 us
  starting transfers between devices  28.3 us (36%)
  Pallas kernels  19.4 us (24%)
  waiting for transfers between devices  19 us (24%)
  matrix products  7.08 us (9%)
  other arithmetic  3.72 us (5%)
  between operations  1.07 us (1%)
    ppermute x25, starting transfers between devices, flip(): return lax.ppermute(x, AXES, pairs)  28.3 us
    ppermute x25, waiting for transfers between devices, flip(): return lax.ppermute(x, AXES, pairs)  19 us
    pallas_call x1, Pallas kernels, per_device(): pl.pallas_call(functools.partial(finish_kernel, heads, block_rows, side_c...  7.35 us
    pallas_call x1, Pallas kernels, per_device(): pl.pallas_call(prep_kernel, out_shape=[jax.ShapeDtypeStruct((local_reqs,...  5.75 us
    dot_general x2, matrix products, feed(): gate_up = jnp.dot(x[:, :D], gate_up_weight[0], preferred_element_type=f32)  5.39 us
    pallas_call x1, Pallas kernels, per_device(): pl.pallas_call(functools.partial(pack_kernel, side_count, local_reqs, lev...  4.52 us
    pallas_call x1, Pallas kernels, per_device(): pl.pallas_call(functools.partial(rows_kernel, peer_count), out_shape=jax....  1.83 us
    dot_general x2, matrix products, feed(): produced = jnp.dot(activated, down_weight[0], preferred_element_type=f32)  1.7 us
  transfers between devices with their start and end apart: 25, of which 9 were waited for; matrix products, arithmetic and copies ran while one was open for 14% of the time, Pallas kernels for 13%

profile of v3, /device:TPU:0, one launch (start us, length us, event | category | flops | bytes accessed | tf_op | source)
XLA Modules:
  0.0 79.1 jit_solution(3721707498781013177)
XLA Ops:
  0.6 1.8 %rows.1 = bf16[32,2432]{1,0:T(8,128)(2,1)} custom-call(bf16[2,16,2304]{2,1,0:T(8,128)(2,1)} %hidden_ref.1, s32[2,8,16]{2,1,0:T(8,128)} %bitcast.30, f32[2,8,16]{2,1,0:T(8,128)} %bitcast.31), custom_call_target="tpu_custom_call" | custom-call | tf_op jit(solution)/shard_map/rows/pallas_call | solution.py:234
  2.5 5.0 %collective-permute-start = (bf16[32,2432]{1,0:T(8,128)(2,1)}, bf16[32,2432]{1,0:T(8,128)(2,1)S(1)}, u32[]{:S(2)}, u32[]{:S(2)}) collective-permute-start(bf16[32,2432]{1,0:T(8,128)(2,1)} %rows.1), channel_id=1, source_target_pairs={{0,12},{1,13},{2,14},{3,15},{4,8},{5,9},{6,10},{7,11},{8,4},{9,5},... | collective-permute-start | bytes 466952 | tf_op jit(solution)/shard_map/ppermute | solution.py:229
  7.5 1.5 %collective-permute-start.6 = (bf16[32,2432]{1,0:T(8,128)(2,1)}, bf16[32,2432]{1,0:T(8,128)(2,1)S(1)}, u32[]{:S(2)}, u32[]{:S(2)}) collective-permute-start(bf16[32,2432]{1,0:T(8,128)(2,1)} %rows.1), channel_id=1, source_target_pairs={{0,2},{1,3},{2,0},{3,1},{4,6},{5,7},{6,4},{7,5},{8,10},{9,11},{10,... | collective-permute-start | bytes 466952 | tf_op jit(solution)/shard_map/ppermute | solution.py:229
  9.1 4.5 %pack.1 = (bf16[4,512,128]{2,1,0:T(8,128)(2,1)}, bf16[4,512,128]{2,1,0:T(8,128)(2,1)}, bf16[16,128]{1,0:T(8,128)(2,1)}) custom-call(s32[2,2]{1,0:T(2,128)} %swaps.3, s32[1]{0:T(128)} %bitcast.where_at, f32[2,4,512,128]{3,2,1,0:T(8,128)} %bitcast.27, f32[2,4,512,128]{3,2,1,0:T(8,128)} %bitcast.28), custom_call_target="tpu_custom_call" | custom-call | tf_op jit(solution)/shard_map/pack/pallas_call | solution.py:265
  13.7 0.9 %compare_bitcast_fusion = (pred[128]{0:T(512)(128)(4,1)S(1)}, pred[128]{0:T(512)(128)(4,1)S(1)}, pred[128]{0:T(512)(128)(4,1)S(1)}, pred[128]{0:T(512)(128)(4,1)...) fusion(bf16[16,128]{1,0:T(8,128)(2,1)} %get-tuple-element.23), kind=kLoop, calls=%fused_computation.61 | loop fusion | flops 768 | bytes 2304 | tf_op jit(solution)/shard_map/gt | solution.py:279
  15.2 1.5 %collective-permute-start.9 = (bf16[32,2432]{1,0:T(8,128)(2,1)S(1)}, bf16[32,2432]{1,0:T(8,128)(2,1)S(1)}, u32[]{:S(2)}, u32[]{:S(2)}) collective-permute-start(bf16[32,2432]{1,0:T(8,128)(2,1)S(1)} %collective-permute-done.8), channel_id=1, source_target_pairs={{0,2},{1,3},{2,0},{3,1},{4,6},{5,7},{6,4},{7,5},{8,10},{9,11},{10,... | collective-permute-start | bytes 466952 | tf_op jit(solution)/shard_map/ppermute | solution.py:229
  16.7 1.1 %broadcast_select_fusion.1 = bf16[4,512,128]{2,1,0:T(8,128)(2,1)S(1)} fusion(bf16[4,512,128]{2,1,0:T(8,128)(2,1)} %get-tuple-element.24, bf16[4,512,128]{2,1,0:T(8,128)(2,1)S(1)} %collective-permute-done.1.near, pred[128]{0:T(512)(128)(4,1)S(1)} %get-tuple-element.61), kind=kLoop, calls=%fused_computation.22 | loop fusion | flops 262144 | bytes 1572992 | tf_op jit(solution)/shard_map/jit(_where)/select_n | solution.py:279
  18.5 1.7 %collective-permute-start.3 = (bf16[32,2432]{1,0:T(8,128)(2,1)S(1)}, bf16[32,2432]{1,0:T(8,128)(2,1)S(1)}, u32[]{:S(2)}, u32[]{:S(2)}) collective-permute-start(bf16[32,2432]{1,0:T(8,128)(2,1)S(1)} %collective-permute-done), channel_id=1, source_target_pairs={{0,4},{1,5},{2,6},{3,7},{4,0},{5,1},{6,2},{7,3},{8,12},{9,13},{10,... | collective-permute-start | bytes 466952 | tf_op jit(solution)/shard_map/ppermute | solution.py:229
  20.2 1.6 %collective-permute-start.2 = (bf16[2,512,128]{2,1,0:T(8,128)(2,1)S(1)}, bf16[2,512,128]{2,1,0:T(8,128)(2,1)S(1)}, u32[]{:S(2)}, u32[]{:S(2)}) collective-permute-start(bf16[2,512,128]{2,1,0:T(8,128)(2,1)S(1)} %slice.108), channel_id=1, source_target_pairs={{0,2},{1,3},{2,0},{3,1},{4,6},{5,7},{6,4},{7,5},{8,10},{9,11},{10,... | collective-permute-start | bytes 786440 | tf_op jit(solution)/shard_map/ppermute | solution.py:229
  21.8 2.2 %collective-permute-done.3 = bf16[32,2432]{1,0:T(8,128)(2,1)S(1)} collective-permute-done((bf16[32,2432]{1,0:T(8,128)(2,1)S(1)}, bf16[32,2432]{1,0:T(8,128)(2,1)S(1)}, u32[]{:S(2)}, u32[]{:S(2)}) %collective-permute-start.3) | collective-permute-done | bytes 155680 | tf_op jit(solution)/shard_map/ppermute | solution.py:229
  24.2 5.7 %prep.1 = (bf16[2,16,32,384]{3,2,1,0:T(8,128)(2,1)S(1)}, f32[2,16,32,128]{3,2,1,0:T(8,128)S(1)}, bf16[2,16,48,128]{3,2,1,0:T(8,128)(2,1)S(1)}, f32[2,16,8,128]{3,2,1,0:T(8,128)S(1)}) custom-call(s32[2]{0:T(128)S(1)} %copy-done.8, bf16[2,16,2048]{2,1,0:T(8,128)(2,1)S(1)} %copy-done.3, bf16[2,16,2048]{2,1,0:T(8,128)(2,1)S(1)} %copy-done.4, ...), custom_call_target="tpu_custom_call" | custom-call | tf_op jit(solution)/shard_map/prep/pallas_call | solution.py:298
  30.0 1.2 %collective-permute-start.10 = (bf16[32,2432]{1,0:T(8,128)(2,1)S(1)}, bf16[32,2432]{1,0:T(8,128)(2,1)S(1)}, u32[]{:S(2)}, u32[]{:S(2)}) collective-permute-start(bf16[32,2432]{1,0:T(8,128)(2,1)S(1)} %collective-permute-done.3), channel_id=1, source_target_pairs={{0,2},{1,3},{2,0},{3,1},{4,6},{5,7},{6,4},{7,5},{8,10},{9,11},{10,... | collective-permute-start | bytes 466952 | tf_op jit(solution)/shard_map/ppermute | solution.py:229
  31.3 1.7 %collective-permute-start.4 = (bf16[1,512,128]{2,1,0:T(8,128)(2,1)S(1)}, bf16[1,512,128]{2,1,0:T(8,128)(2,1)S(1)}, u32[]{:S(2)}, u32[]{:S(2)}) collective-permute-start(bf16[1,512,128]{2,1,0:T(8,128)(2,1)S(1)} %slice.140), channel_id=1, source_target_pairs={{0,4},{1,5},{2,6},{3,7},{4,0},{5,1},{6,2},{7,3},{8,12},{9,13},{10,... | collective-permute-start | bytes 393224 | tf_op jit(solution)/shard_map/ppermute | solution.py:229
  33.1 3.4 %collective-permute-done.10 = bf16[32,2432]{1,0:T(8,128)(2,1)S(1)} collective-permute-done((bf16[32,2432]{1,0:T(8,128)(2,1)S(1)}, bf16[32,2432]{1,0:T(8,128)(2,1)S(1)}, u32[]{:S(2)}, u32[]{:S(2)}) %collective-permute-start.10) | collective-permute-done | bytes 155680 | tf_op jit(solution)/shard_map/ppermute | solution.py:229
  37.0 2.2 %collective-permute-start.5 = (bf16[1,512,128]{2,1,0:T(8,128)(2,1)S(1)}, bf16[1,512,128]{2,1,0:T(8,128)(2,1)S(1)}, u32[]{:S(2)}, u32[]{:S(2)}) collective-permute-start(bf16[1,512,128]{2,1,0:T(8,128)(2,1)S(1)} %broadcast_select_fusion.5), channel_id=1, source_target_pairs={{0,12},{1,13},{2,14},{3,15},{4,8},{5,9},{6,10},{7,11},{8,4},{9,5},... | collective-permute-start | bytes 393224 | tf_op jit(solution)/shard_map/ppermute | solution.py:229
  39.4 3.9 %fusion.2 = f32[256,1024]{1,0:T(8,128)S(1)} fusion(bf16[1,2304,1024]{2,1,0:T(8,128)(2,1)} %param.24, bf16[256,2432]{1,0:T(8,128)(2,1)S(1)} %constant_dynamic-update-slice_fusion), kind=kOutput, calls=%fused_computation.2 | convolution fusion | flops 1207959552 | bytes 6946816 | tf_op jit(solution)/shard_map/dot_general | solution.py:329
  43.6 0.8 %fusion.4 = bf16[256,2304]{1,0:T(8,128)(2,1)S(1)} fusion(bf16[1,512,2304]{2,1,0:T(8,128)(2,1)S(1)} %copy-done, f32[256]{0:T(256)S(1)} %get-tuple-element.44, f32[256,1024]{1,0:T(8,128)S(1)} %fusion.2), kind=kOutput, calls=%fused_computation.6 | convolution fusion | flops 605945856 | bytes 4588544 | tf_op jit(solution)/shard_map/dot_general | solution.py:331
  44.8 1.5 %fusion = f32[256,1024]{1,0:T(8,128)S(1)} fusion(bf16[1,2304,1024]{2,1,0:T(8,128)(2,1)S(1)} %bitcast.33, bf16[256,2432]{1,0:T(8,128)(2,1)S(1)} %constant_dynamic-update-slice_fusion.5), kind=kOutput, calls=%fused_computation | convolution fusion | flops 1207959552 | bytes 6946816 | tf_op jit(solution)/shard_map/dot_general | solution.py:329
  46.3 0.9 %fusion.5 = bf16[256,2304]{1,0:T(8,128)(2,1)S(1)} fusion(bf16[1,512,2304]{2,1,0:T(8,128)(2,1)S(1)} %copy-done, f32[256]{0:T(256)S(1)} %get-tuple-element.43, f32[256,1024]{1,0:T(8,128)S(1)} %fusion), kind=kOutput, calls=%fused_computation.7 | convolution fusion | flops 605945856 | bytes 4588544 | tf_op jit(solution)/shard_map/dot_general | solution.py:331
  47.8 1.3 %collective-permute-start.19 = (bf16[32,2304]{1,0:T(8,128)(2,1)S(1)}, bf16[32,2304]{1,0:T(8,128)(2,1)S(1)}, u32[]{:S(2)}, u32[]{:S(2)}) collective-permute-start(bf16[32,2304]{1,0:T(8,128)(2,1)S(1)} %get-tuple-element.50), channel_id=1, source_target_pairs={{0,2},{1,3},{2,0},{3,1},{4,6},{5,7},{6,4},{7,5},{8,10},{9,11},{10,... | collective-permute-start | bytes 442376 | tf_op jit(solution)/shard_map/ppermute | solution.py:229
  49.9 1.2 %collective-permute-start.21 = (bf16[32,2304]{1,0:T(8,128)(2,1)S(1)}, bf16[32,2304]{1,0:T(8,128)(2,1)S(1)}, u32[]{:S(2)}, u32[]{:S(2)}) collective-permute-start(bf16[32,2304]{1,0:T(8,128)(2,1)S(1)} %get-tuple-element.49), channel_id=1, source_target_pairs={{0,2},{1,3},{2,0},{3,1},{4,6},{5,7},{6,4},{7,5},{8,10},{9,11},{10,... | collective-permute-start | bytes 442376 | tf_op jit(solution)/shard_map/ppermute | solution.py:229
  51.9 1.1 %collective-permute-start.13 = (bf16[1,512,128]{2,1,0:T(8,128)(2,1)S(1)}, bf16[1,512,128]{2,1,0:T(8,128)(2,1)S(1)}, u32[]{:S(2)}, u32[]{:S(2)}) collective-permute-start(bf16[1,512,128]{2,1,0:T(8,128)(2,1)S(1)} %get-tuple-element.56), channel_id=1, source_target_pairs={{0,4},{1,5},{2,6},{3,7},{4,0},{5,1},{6,2},{7,3},{8,12},{9,13},{10,... | collective-permute-start | bytes 393224 | tf_op jit(solution)/shard_map/ppermute | solution.py:229
  53.1 1.4 %collective-permute-done.19 = bf16[32,2304]{1,0:T(8,128)(2,1)S(1)} collective-permute-done((bf16[32,2304]{1,0:T(8,128)(2,1)S(1)}, bf16[32,2304]{1,0:T(8,128)(2,1)S(1)}, u32[]{:S(2)}, u32[]{:S(2)}) %collective-permute-start.19) | collective-permute-done | bytes 147488 | tf_op jit(solution)/shard_map/ppermute | solution.py:229
  54.5 3.2 %collective-permute-done.22 = bf16[32,2304]{1,0:T(8,128)(2,1)S(1)} collective-permute-done((bf16[32,2304]{1,0:T(8,128)(2,1)S(1)}, bf16[32,2304]{1,0:T(8,128)(2,1)S(1)}, u32[]{:S(2)}, u32[]{:S(2)}) %collective-permute-start.22) | collective-permute-done | bytes 147488 | tf_op jit(solution)/shard_map/ppermute | solution.py:229
  57.7 1.1 %collective-permute-start.23 = (bf16[32,2304]{1,0:T(8,128)(2,1)S(1)}, bf16[32,2304]{1,0:T(8,128)(2,1)S(1)}, u32[]{:S(2)}, u32[]{:S(2)}) collective-permute-start(bf16[32,2304]{1,0:T(8,128)(2,1)S(1)} %get-tuple-element.46), channel_id=1, source_target_pairs={{0,4},{1,5},{2,6},{3,7},{4,0},{5,1},{6,2},{7,3},{8,12},{9,13},{10,... | collective-permute-start | bytes 442376 | tf_op jit(solution)/shard_map/ppermute | solution.py:229
  58.9 1.2 %collective-permute-start.14 = (bf16[2,512,128]{2,1,0:T(8,128)(2,1)S(1)}, bf16[2,512,128]{2,1,0:T(8,128)(2,1)S(1)}, u32[]{:S(2)}, u32[]{:S(2)}) collective-permute-start(bf16[2,512,128]{2,1,0:T(8,128)(2,1)S(1)} %get-tuple-element.54), channel_id=1, source_target_pairs={{0,2},{1,3},{2,0},{3,1},{4,6},{5,7},{6,4},{7,5},{8,10},{9,11},{10,... | collective-permute-start | bytes 786440 | tf_op jit(solution)/shard_map/ppermute | solution.py:229
  60.1 1.1 %collective-permute-start.20 = (bf16[32,2304]{1,0:T(8,128)(2,1)S(1)}, bf16[32,2304]{1,0:T(8,128)(2,1)S(1)}, u32[]{:S(2)}, u32[]{:S(2)}) collective-permute-start(bf16[32,2304]{1,0:T(8,128)(2,1)S(1)} %get-tuple-element.45), channel_id=1, source_target_pairs={{0,4},{1,5},{2,6},{3,7},{4,0},{5,1},{6,2},{7,3},{8,12},{9,13},{10,... | collective-permute-start | bytes 442376 | tf_op jit(solution)/shard_map/ppermute | solution.py:229
  61.2 2.6 %collective-permute-done.23 = bf16[32,2304]{1,0:T(8,128)(2,1)S(1)} collective-permute-done((bf16[32,2304]{1,0:T(8,128)(2,1)S(1)}, bf16[32,2304]{1,0:T(8,128)(2,1)S(1)}, u32[]{:S(2)}, u32[]{:S(2)}) %collective-permute-start.23) | collective-permute-done | bytes 147488 | tf_op jit(solution)/shard_map/ppermute | solution.py:229
  63.9 1.7 %collective-permute-start.24 = (bf16[32,2304]{1,0:T(8,128)(2,1)S(1)}, bf16[32,2304]{1,0:T(8,128)(2,1)S(1)}, u32[]{:S(2)}, u32[]{:S(2)}) collective-permute-start(bf16[32,2304]{1,0:T(8,128)(2,1)S(1)} %fusion.14), channel_id=1, source_target_pairs={{0,12},{1,13},{2,14},{3,15},{4,8},{5,9},{6,10},{7,11},{8,4},{9,5},... | collective-permute-start | bytes 442376 | tf_op jit(solution)/shard_map/ppermute | solution.py:229
  65.5 3.3 %collective-permute-done.14 = bf16[2,512,128]{2,1,0:T(8,128)(2,1)S(1)} collective-permute-done((bf16[2,512,128]{2,1,0:T(8,128)(2,1)S(1)}, bf16[2,512,128]{2,1,0:T(8,128)(2,1)S(1)}, u32[]{:S(2)}, u32[]{:S(2)}) %collective-permute-start.14) | collective-permute-done | bytes 262176 | tf_op jit(solution)/shard_map/ppermute | solution.py:229
  69.1 1.9 %collective-permute-done.24 = bf16[32,2304]{1,0:T(8,128)(2,1)S(1)} collective-permute-done((bf16[32,2304]{1,0:T(8,128)(2,1)S(1)}, bf16[32,2304]{1,0:T(8,128)(2,1)S(1)}, u32[]{:S(2)}, u32[]{:S(2)}) %collective-permute-start.24) | collective-permute-done | bytes 147488 | tf_op jit(solution)/shard_map/ppermute | solution.py:229
  71.7 7.3 %finish.1 = (f32[2,16,128,128]{3,2,1,0:T(8,128)}, bf16[2,16,2048]{2,1,0:T(8,128)(2,1)}) custom-call(s32[2,2]{1,0:T(2,128)S(1)} %copy-done.7, s32[1]{0:T(128)} %bitcast.where_at, f32[2,16,128,128]{3,2,1,0:T(8,128)S(1)} %copy-done.1, bf16[4,512,128]{2,1,0:T(8,128)(2,1)S(1)} %get-tuple-element.52.mine, bf16[4,512,128]{2,1,0:T(8,128)(2,1)S(1)} %collective-permute-done.1.near, ...), custom_call_target="tpu_custom_call" | custom-call | tf_op jit(solution)/shard_map/finish/pallas_call | solution.py:369
  (86 shorter events, 6.3 us)
Async XLA Ops:
  0.6 43.0 %copy-start = (bf16[1,512,2304]{2,1,0:T(8,128)(2,1)S(1)}, bf16[1,512,2304]{2,1,0:T(8,128)(2,1)}, u32[]{:S(2)}) copy-start(bf16[1,512,2304]{2,1,0:T(8,128)(2,1)} %param.25) | copy-start | bytes 7077892
  2.5 15.4 %collective-permute-start = (bf16[32,2432]{1,0:T(8,128)(2,1)}, bf16[32,2432]{1,0:T(8,128)(2,1)S(1)}, u32[]{:S(2)}, u32[]{:S(2)}) collective-permute-start(bf16[32,2432]{1,0:T(8,128)(2,1)} %rows.1), channel_id=1, source_target_pairs={{0,12},{1,13},{2,14},{3,15},{4,8},{5,9},{6,10},{7,11},{8,4},{9,5},... | collective-permute-start | bytes 466952 | tf_op jit(solution)/shard_map/ppermute | solution.py:229
  7.5 9.2 %collective-permute-start.6 = (bf16[32,2432]{1,0:T(8,128)(2,1)}, bf16[32,2432]{1,0:T(8,128)(2,1)S(1)}, u32[]{:S(2)}, u32[]{:S(2)}) collective-permute-start(bf16[32,2432]{1,0:T(8,128)(2,1)} %rows.1), channel_id=1, source_target_pairs={{0,2},{1,3},{2,0},{3,1},{4,6},{5,7},{6,4},{7,5},{8,10},{9,11},{10,... | collective-permute-start | bytes 466952 | tf_op jit(solution)/shard_map/ppermute | solution.py:229
  9.0 6.2 %collective-permute-start.8 = (bf16[32,2432]{1,0:T(8,128)(2,1)}, bf16[32,2432]{1,0:T(8,128)(2,1)S(1)}, u32[]{:S(2)}, u32[]{:S(2)}) collective-permute-start(bf16[32,2432]{1,0:T(8,128)(2,1)} %rows.1), channel_id=1, source_target_pairs={{0,4},{1,5},{2,6},{3,7},{4,0},{5,1},{6,2},{7,3},{8,12},{9,13},{10,... | collective-permute-start | bytes 466952 | tf_op jit(solution)/shard_map/ppermute | solution.py:229
  9.0 4.6 %copy-start.10 = (bf16[32,2432]{1,0:T(8,128)(2,1)S(1)}, bf16[32,2432]{1,0:T(8,128)(2,1)}, u32[]{:S(2)}) copy-start(bf16[32,2432]{1,0:T(8,128)(2,1)} %rows.1) | copy-start | bytes 466948
  13.6 3.2 %collective-permute-start.1 = (bf16[4,512,128]{2,1,0:T(8,128)(2,1)}, bf16[4,512,128]{2,1,0:T(8,128)(2,1)S(1)}, u32[]{:S(2)}, u32[]{:S(2)}) collective-permute-start(bf16[4,512,128]{2,1,0:T(8,128)(2,1)} %get-tuple-element.25), channel_id=1, source_target_pairs={{0,1},{1,0},{2,3},{3,2},{4,5},{5,4},{6,7},{7,6},{8,9},{9,8},{10,11... | collective-permute-start | bytes 1572872 | tf_op jit(solution)/shard_map/ppermute | solution.py:229
  15.2 16.0 %collective-permute-start.9 = (bf16[32,2432]{1,0:T(8,128)(2,1)S(1)}, bf16[32,2432]{1,0:T(8,128)(2,1)S(1)}, u32[]{:S(2)}, u32[]{:S(2)}) collective-permute-start(bf16[32,2432]{1,0:T(8,128)(2,1)S(1)} %collective-permute-done.8), channel_id=1, source_target_pairs={{0,2},{1,3},{2,0},{3,1},{4,6},{5,7},{6,4},{7,5},{8,10},{9,11},{10,... | collective-permute-start | bytes 466952 | tf_op jit(solution)/shard_map/ppermute | solution.py:229
  17.9 13.3 %collective-permute-start.7 = (bf16[32,2432]{1,0:T(8,128)(2,1)S(1)}, bf16[32,2432]{1,0:T(8,128)(2,1)S(1)}, u32[]{:S(2)}, u32[]{:S(2)}) collective-permute-start(bf16[32,2432]{1,0:T(8,128)(2,1)S(1)} %collective-permute-done), channel_id=1, source_target_pairs={{0,2},{1,3},{2,0},{3,1},{4,6},{5,7},{6,4},{7,5},{8,10},{9,11},{10,... | collective-permute-start | bytes 466952 | tf_op jit(solution)/shard_map/ppermute | solution.py:229
  18.5 5.6 %collective-permute-start.3 = (bf16[32,2432]{1,0:T(8,128)(2,1)S(1)}, bf16[32,2432]{1,0:T(8,128)(2,1)S(1)}, u32[]{:S(2)}, u32[]{:S(2)}) collective-permute-start(bf16[32,2432]{1,0:T(8,128)(2,1)S(1)} %collective-permute-done), channel_id=1, source_target_pairs={{0,4},{1,5},{2,6},{3,7},{4,0},{5,1},{6,2},{7,3},{8,12},{9,13},{10,... | collective-permute-start | bytes 466952 | tf_op jit(solution)/shard_map/ppermute | solution.py:229
  20.1 4.0 %copy-start.2 = (f32[2,16,2048]{2,1,0:T(8,128)S(1)}, f32[2,16,2048]{2,1,0:T(8,128)}, u32[]{:S(2)}) copy-start(f32[2,16,2048]{2,1,0:T(8,128)} %decay_ref.1) | copy-start | bytes 786436
  20.2 4.0 %copy-start.3 = (bf16[2,16,2048]{2,1,0:T(8,128)(2,1)S(1)}, bf16[2,16,2048]{2,1,0:T(8,128)(2,1)}, u32[]{:S(2)}) copy-start(bf16[2,16,2048]{2,1,0:T(8,128)(2,1)} %q_ref.1) | copy-start | bytes 393220
  20.2 11.0 %collective-permute-start.2 = (bf16[2,512,128]{2,1,0:T(8,128)(2,1)S(1)}, bf16[2,512,128]{2,1,0:T(8,128)(2,1)S(1)}, u32[]{:S(2)}, u32[]{:S(2)}) collective-permute-start(bf16[2,512,128]{2,1,0:T(8,128)(2,1)S(1)} %slice.108), channel_id=1, source_target_pairs={{0,2},{1,3},{2,0},{3,1},{4,6},{5,7},{6,4},{7,5},{8,10},{9,11},{10,... | collective-permute-start | bytes 786440 | tf_op jit(solution)/shard_map/ppermute | solution.py:229
  24.1 15.1 %collective-permute-start.16 = (bf16[128,2432]{1,0:T(8,128)(2,1)S(1)}, bf16[128,2432]{1,0:T(8,128)(2,1)S(1)}, u32[]{:S(2)}, u32[]{:S(2)}) collective-permute-start(bf16[128,2432]{1,0:T(8,128)(2,1)S(1)} %pad_maximum_fusion.1), channel_id=1, source_target_pairs={{0,1},{1,0},{2,3},{3,2},{4,5},{5,4},{6,7},{7,6},{8,9},{9,8},{10,11... | collective-permute-start | bytes 1867784 | tf_op jit(solution)/shard_map/ppermute | solution.py:229
  30.0 6.4 %collective-permute-start.10 = (bf16[32,2432]{1,0:T(8,128)(2,1)S(1)}, bf16[32,2432]{1,0:T(8,128)(2,1)S(1)}, u32[]{:S(2)}, u32[]{:S(2)}) collective-permute-start(bf16[32,2432]{1,0:T(8,128)(2,1)S(1)} %collective-permute-done.3), channel_id=1, source_target_pairs={{0,2},{1,3},{2,0},{3,1},{4,6},{5,7},{6,4},{7,5},{8,10},{9,11},{10,... | collective-permute-start | bytes 466952 | tf_op jit(solution)/shard_map/ppermute | solution.py:229
  31.3 5.6 %collective-permute-start.4 = (bf16[1,512,128]{2,1,0:T(8,128)(2,1)S(1)}, bf16[1,512,128]{2,1,0:T(8,128)(2,1)S(1)}, u32[]{:S(2)}, u32[]{:S(2)}) collective-permute-start(bf16[1,512,128]{2,1,0:T(8,128)(2,1)S(1)} %slice.140), channel_id=1, source_target_pairs={{0,4},{1,5},{2,6},{3,7},{4,0},{5,1},{6,2},{7,3},{8,12},{9,13},{10,... | collective-permute-start | bytes 393224 | tf_op jit(solution)/shard_map/ppermute | solution.py:229
  36.5 2.8 %collective-permute-start.11 = (bf16[128,2432]{1,0:T(8,128)(2,1)S(1)}, bf16[128,2432]{1,0:T(8,128)(2,1)S(1)}, u32[]{:S(2)}, u32[]{:S(2)}) collective-permute-start(bf16[128,2432]{1,0:T(8,128)(2,1)S(1)} %pad_maximum_fusion), channel_id=1, source_target_pairs={{0,1},{1,0},{2,3},{3,2},{4,5},{5,4},{6,7},{7,6},{8,9},{9,8},{10,11... | collective-permute-start | bytes 1867784 | tf_op jit(solution)/shard_map/ppermute | solution.py:229
  37.0 10.7 %collective-permute-start.5 = (bf16[1,512,128]{2,1,0:T(8,128)(2,1)S(1)}, bf16[1,512,128]{2,1,0:T(8,128)(2,1)S(1)}, u32[]{:S(2)}, u32[]{:S(2)}) collective-permute-start(bf16[1,512,128]{2,1,0:T(8,128)(2,1)S(1)} %broadcast_select_fusion.5), channel_id=1, source_target_pairs={{0,12},{1,13},{2,14},{3,15},{4,8},{5,9},{6,10},{7,11},{8,4},{9,5},... | collective-permute-start | bytes 393224 | tf_op jit(solution)/shard_map/ppermute | solution.py:229
  39.3 5.5 %slice-start = ((s8[4718592]{0:T(1024)(128)(4,1)}), s8[4194304]{0:T(1024)(128)(4,1)S(1)}, s32[]{:S(2)}) async-start(s8[4718592]{0:T(1024)(128)(4,1)} %bitcast.32), calls=%async_computation | async-start | bytes 8388608
  39.4 5.4 %slice-start.1 = ((s8[4718592]{0:T(1024)(128)(4,1)}), s8[524288]{0:T(1024)(128)(4,1)S(1)}, s32[]{:S(2)}) async-start(s8[4718592]{0:T(1024)(128)(4,1)} %bitcast.32), calls=%async_computation.1 | async-start | bytes 1048576
  44.5 3.0 %collective-permute-start.12 = (bf16[128,2304]{1,0:T(8,128)(2,1)S(1)}, bf16[128,2304]{1,0:T(8,128)(2,1)S(1)}, u32[]{:S(2)}, u32[]{:S(2)}) collective-permute-start(bf16[128,2304]{1,0:T(8,128)(2,1)S(1)} %slice.149), channel_id=1, source_target_pairs={{0,1},{1,0},{2,3},{3,2},{4,5},{5,4},{6,7},{7,6},{8,9},{9,8},{10,11... | collective-permute-start | bytes 1769480 | tf_op jit(solution)/shard_map/ppermute | solution.py:229
  47.2 4.7 %collective-permute-start.17 = (bf16[128,2304]{1,0:T(8,128)(2,1)S(1)}, bf16[128,2304]{1,0:T(8,128)(2,1)S(1)}, u32[]{:S(2)}, u32[]{:S(2)}) collective-permute-start(bf16[128,2304]{1,0:T(8,128)(2,1)S(1)} %slice.157), channel_id=1, source_target_pairs={{0,1},{1,0},{2,3},{3,2},{4,5},{5,4},{6,7},{7,6},{8,9},{9,8},{10,11... | collective-permute-start | bytes 1769480 | tf_op jit(solution)/shard_map/ppermute | solution.py:229
  47.8 6.7 %collective-permute-start.19 = (bf16[32,2304]{1,0:T(8,128)(2,1)S(1)}, bf16[32,2304]{1,0:T(8,128)(2,1)S(1)}, u32[]{:S(2)}, u32[]{:S(2)}) collective-permute-start(bf16[32,2304]{1,0:T(8,128)(2,1)S(1)} %get-tuple-element.50), channel_id=1, source_target_pairs={{0,2},{1,3},{2,0},{3,1},{4,6},{5,7},{6,4},{7,5},{8,10},{9,11},{10,... | collective-permute-start | bytes 442376 | tf_op jit(solution)/shard_map/ppermute | solution.py:229
  49.1 8.6 %collective-permute-start.22 = (bf16[32,2304]{1,0:T(8,128)(2,1)S(1)}, bf16[32,2304]{1,0:T(8,128)(2,1)S(1)}, u32[]{:S(2)}, u32[]{:S(2)}) collective-permute-start(bf16[32,2304]{1,0:T(8,128)(2,1)S(1)} %get-tuple-element.48), channel_id=1, source_target_pairs={{0,2},{1,3},{2,0},{3,1},{4,6},{5,7},{6,4},{7,5},{8,10},{9,11},{10,... | collective-permute-start | bytes 442376 | tf_op jit(solution)/shard_map/ppermute | solution.py:229
  49.9 11.4 %collective-permute-start.21 = (bf16[32,2304]{1,0:T(8,128)(2,1)S(1)}, bf16[32,2304]{1,0:T(8,128)(2,1)S(1)}, u32[]{:S(2)}, u32[]{:S(2)}) collective-permute-start(bf16[32,2304]{1,0:T(8,128)(2,1)S(1)} %get-tuple-element.49), channel_id=1, source_target_pairs={{0,2},{1,3},{2,0},{3,1},{4,6},{5,7},{6,4},{7,5},{8,10},{9,11},{10,... | collective-permute-start | bytes 442376 | tf_op jit(solution)/shard_map/ppermute | solution.py:229
  51.1 18.0 %collective-permute-start.18 = (bf16[32,2304]{1,0:T(8,128)(2,1)S(1)}, bf16[32,2304]{1,0:T(8,128)(2,1)S(1)}, u32[]{:S(2)}, u32[]{:S(2)}) collective-permute-start(bf16[32,2304]{1,0:T(8,128)(2,1)S(1)} %get-tuple-element.47), channel_id=1, source_target_pairs={{0,2},{1,3},{2,0},{3,1},{4,6},{5,7},{6,4},{7,5},{8,10},{9,11},{10,... | collective-permute-start | bytes 442376 | tf_op jit(solution)/shard_map/ppermute | solution.py:229
  51.9 6.9 %collective-permute-start.13 = (bf16[1,512,128]{2,1,0:T(8,128)(2,1)S(1)}, bf16[1,512,128]{2,1,0:T(8,128)(2,1)S(1)}, u32[]{:S(2)}, u32[]{:S(2)}) collective-permute-start(bf16[1,512,128]{2,1,0:T(8,128)(2,1)S(1)} %get-tuple-element.56), channel_id=1, source_target_pairs={{0,4},{1,5},{2,6},{3,7},{4,0},{5,1},{6,2},{7,3},{8,12},{9,13},{10,... | collective-permute-start | bytes 393224 | tf_op jit(solution)/shard_map/ppermute | solution.py:229
  57.7 11.2 %copy-start.9 = (bf16[4,512,128]{2,1,0:T(8,128)(2,1)S(1)}, bf16[4,512,128]{2,1,0:T(8,128)(2,1)}, u32[]{:S(2)}) copy-start(bf16[4,512,128]{2,1,0:T(8,128)(2,1)} %get-tuple-element.24) | copy-start | bytes 1572868
  57.7 6.1 %collective-permute-start.23 = (bf16[32,2304]{1,0:T(8,128)(2,1)S(1)}, bf16[32,2304]{1,0:T(8,128)(2,1)S(1)}, u32[]{:S(2)}, u32[]{:S(2)}) collective-permute-start(bf16[32,2304]{1,0:T(8,128)(2,1)S(1)} %get-tuple-element.46), channel_id=1, source_target_pairs={{0,4},{1,5},{2,6},{3,7},{4,0},{5,1},{6,2},{7,3},{8,12},{9,13},{10,... | collective-permute-start | bytes 442376 | tf_op jit(solution)/shard_map/ppermute | solution.py:229
  58.9 10.0 %collective-permute-start.14 = (bf16[2,512,128]{2,1,0:T(8,128)(2,1)S(1)}, bf16[2,512,128]{2,1,0:T(8,128)(2,1)S(1)}, u32[]{:S(2)}, u32[]{:S(2)}) collective-permute-start(bf16[2,512,128]{2,1,0:T(8,128)(2,1)S(1)} %get-tuple-element.54), channel_id=1, source_target_pairs={{0,2},{1,3},{2,0},{3,1},{4,6},{5,7},{6,4},{7,5},{8,10},{9,11},{10,... | collective-permute-start | bytes 786440 | tf_op jit(solution)/shard_map/ppermute | solution.py:229
  60.1 9.0 %collective-permute-start.20 = (bf16[32,2304]{1,0:T(8,128)(2,1)S(1)}, bf16[32,2304]{1,0:T(8,128)(2,1)S(1)}, u32[]{:S(2)}, u32[]{:S(2)}) collective-permute-start(bf16[32,2304]{1,0:T(8,128)(2,1)S(1)} %get-tuple-element.45), channel_id=1, source_target_pairs={{0,4},{1,5},{2,6},{3,7},{4,0},{5,1},{6,2},{7,3},{8,12},{9,13},{10,... | collective-permute-start | bytes 442376 | tf_op jit(solution)/shard_map/ppermute | solution.py:229
  63.9 7.1 %collective-permute-start.24 = (bf16[32,2304]{1,0:T(8,128)(2,1)S(1)}, bf16[32,2304]{1,0:T(8,128)(2,1)S(1)}, u32[]{:S(2)}, u32[]{:S(2)}) collective-permute-start(bf16[32,2304]{1,0:T(8,128)(2,1)S(1)} %fusion.14), channel_id=1, source_target_pairs={{0,12},{1,13},{2,14},{3,15},{4,8},{5,9},{6,10},{7,11},{8,4},{9,5},... | collective-permute-start | bytes 442376 | tf_op jit(solution)/shard_map/ppermute | solution.py:229
  69.0 2.7 %collective-permute-start.15 = (bf16[4,512,128]{2,1,0:T(8,128)(2,1)S(1)}, bf16[4,512,128]{2,1,0:T(8,128)(2,1)S(1)}, u32[]{:S(2)}, u32[]{:S(2)}) collective-permute-start(bf16[4,512,128]{2,1,0:T(8,128)(2,1)S(1)} %get-tuple-element.51), channel_id=1, source_target_pairs={{0,1},{1,0},{2,3},{3,2},{4,5},{5,4},{6,7},{7,6},{8,9},{9,8},{10,11... | collective-permute-start | bytes 1572872 | tf_op jit(solution)/shard_map/ppermute | solution.py:229
  (6 other events, 21.7 us)

commit v4 on v3

--- a/solution.py
+++ b/solution.py
@@ -16,7 +16,7 @@
 T_MAX = 16
 AXES = ("dev", "side")
 HIGHEST = lax.Precision.HIGHEST
-VMEM_LIMIT = 48 * 1024 * 1024
+VMEM_LIMIT = 16 * 1024 * 1024
 
 
 def dot_nt(a, b):
@@ -58,8 +58,11 @@
 
 
 def pack_kernel(sides, slots, levels, swaps, where_at, send_in, keep_in, send_ref, keep_ref, plan):
-    send_ref[...] = send_in[0].astype(jnp.bfloat16)
-    keep_ref[...] = keep_in[0].astype(jnp.bfloat16)
+    count = send_ref.shape[0]
+    swapped = lax.rem(chip_of(where_at[0], sides, levels - 1), count)
+    for k in range(count):
+        send_ref[k] = send_in[0, jnp.bitwise_xor(swapped, k)].astype(jnp.bfloat16)
+        keep_ref[k] = keep_in[0, jnp.bitwise_xor(swapped, k)].astype(jnp.bfloat16)
 
     @pl.when(pl.program_id(0) == 0)
     def _():
@@ -119,7 +122,7 @@
             solved = solved - mix[:, s : s + 1] * solved[s : s + 1, :]
         seen = dot_nn(read, solved)
         high, low = split(jnp.concatenate([solved[:, DV:], query_in - seen[:, DV:]], axis=0))
-        z_ref[0, h] = jnp.concatenate([high, high, low], axis=1)
+        z_ref[0, h] = jnp.concatenate([high, low], axis=0)
         uo_ref[0, h, :T_MAX] = solved[:, :DV]
         uo_ref[0, h, T_MAX:] = seen[:, :DV]
         last = cum[T_MAX - 1 : T_MAX]
@@ -174,12 +177,8 @@
             source == 2, mine[block, at], jnp.where(source == 3, near[block, at], other[block, at])
         )
         state = jnp.where(source >= 2, arrived.astype(jnp.float32), states_ref[partner, h])
-        high, low = split(state)
-        both = jnp.dot(
-            z_ref[0, h],
-            jnp.concatenate([high, low, high], axis=0),
-            preferred_element_type=jnp.float32,
-        )
+        both = jnp.dot(z_ref[0, h], state.astype(jnp.bfloat16), preferred_element_type=jnp.float32)
+        both = both[: 2 * T_MAX] + both[2 * T_MAX :]
         writes = uo_ref[0, h, :T_MAX] - both[:T_MAX]
         read = uo_ref[0, h, T_MAX:] + both[T_MAX:]
         out_ref[0, :, h * DV : (h + 1) * DV] = read.astype(out_ref.dtype)
@@ -254,20 +253,20 @@
             pair = pair if own else 1 - pair
             one, two = swaps[pair, 0], swaps[pair, 1]
             held = jnp.where(lax.div(one, local_reqs) == at[0], one, two)
-            chip = chip_of(at[0], side_count, levels - 1)
-            return (lax.rem(held, local_reqs), jnp.bitwise_xor(g, chip), 0, 0)
-
-        return pl.BlockSpec((1, 1, block_rows, DV), index)
+            across_at = jnp.bitwise_and(lax.div(at[0], side_count), 1)
+            return (lax.rem(held, local_reqs), jnp.bitwise_xor(g, across_at), 0, 0)
+
+        return pl.BlockSpec((1, blocks // 2, block_rows, DV), index)
 
     packed = jax.ShapeDtypeStruct((blocks, block_rows, DV), bf16)
-    out_spec = pl.BlockSpec((1, block_rows, DV), lambda g, swaps, at: (g, 0, 0))
+    out_spec = pl.BlockSpec((blocks // 2, block_rows, DV), lambda g, swaps, at: (g, 0, 0))
     state_blocks = states.reshape(local_reqs, blocks, block_rows, DV)
     send, keep, plan = pl.pallas_call(
         functools.partial(pack_kernel, side_count, local_reqs, levels),
         out_shape=(packed, packed, jax.ShapeDtypeStruct((16, DV), bf16)),
         grid_spec=pltpu.PrefetchScalarGridSpec(
             num_scalar_prefetch=2,
-            grid=(blocks,),
+            grid=(2,),
             in_specs=[state_spec(False), state_spec(True)],
             out_specs=[out_spec, out_spec, pl.BlockSpec((16, DV), lambda g, swaps, at: (0, 0))],
         ),
@@ -282,19 +281,25 @@
     direct[0], held = together(direct[0], held)
     for i, mask in enumerate(reversed(masks)):
         fresh = direct[i : i + 1] + [flip(x, dz=mask) for x in line[1:]]
-        across = across + [flip(x, dy=1) for x in fresh]
+        if i == 0:
+            across = across + [flip(x, dy=1) for x in fresh]
+        else:
+            across = across + [
+                flip(across[k], dz=mask) if k % 2 == 0 else flip(fresh[k], dy=1)
+                for k in range(len(fresh))
+            ]
         line = line + fresh
 
     lanes = H * DK
     vec_spec = pl.BlockSpec((1, T_MAX, lanes), lambda r, c: (r, 0, 0))
 
     per_head = [
-        (2 * T_MAX, 3 * DK, bf16),
+        (4 * T_MAX, DK, bf16),
         (2 * T_MAX, DV, f32),
         (3 * T_MAX, DK, bf16),
         (8, DK, f32),
     ]
-    counts, line[-1] = together(token_counts, line[-1])
+    counts = together(token_counts, across[1])[0]
     prepared = pl.pallas_call(
         prep_kernel,
         out_shape=[jax.ShapeDtypeStruct((local_reqs, H, n, m), t) for n, m, t in per_head],
@@ -316,7 +321,7 @@
         n = held.shape[0] // 2
         came = flip(held[n:], **ways[level])
         if level == 0:
-            came, *prepared = lax.optimization_barrier((came, *prepared))
+            came, *prepared = together(came, *prepared)
         up.append((held[:n], came))
         held = choose(3 + 2 * level, held[:n], came)
     needed = flip(held, **ways[levels])
@@ -331,14 +336,18 @@
         produced = jnp.dot(activated, down_weight[0], preferred_element_type=f32)
         return (produced * weight[:, None]).astype(bf16)
 
-    def chip_sum(group):
-        n = group.shape[0]
-        fed = feed(jnp.concatenate([group, flip(group, ds=1)]))
+    def chip_feed(group):
+        return feed(jnp.concatenate([group, flip(group, ds=1)]))
+
+    def chip_sum(fed):
+        n = fed.shape[0] // 2
         return fed[:n].astype(f32) + flip(fed[n:], ds=1).astype(f32)
 
-    near = chip_sum(jnp.concatenate(line))
-    far = chip_sum(jnp.concatenate(across)).astype(bf16)
-    needed, far = together(needed, far)
+    near = chip_feed(jnp.concatenate(line))
+    across[-1], near = together(across[-1], near)
+    far = chip_sum(chip_feed(jnp.concatenate(across))).astype(bf16)
+    near = chip_sum(near)
+    needed = together(needed, far)[0]
 
     for level in range(levels - 1, -1, -1):
         own_half, came = up[level]
@@ -349,16 +358,22 @@
     def chunk(x, k):
         return x[k * row_total : (k + 1) * row_total]
 
-    def total_of(k, level):
-        if level == 0:
-            return chunk(near, k) + flip(chunk(far, k), dy=1).astype(f32)
-        n = outer >> level
-        mask = masks[level - 1]
-        return total_of(k, level - 1) + flip(
-            total_of(k + n, level - 1).astype(bf16), dz=mask
-        ).astype(f32)
-
-    expert_out = total_of(0, len(masks)).astype(bf16).reshape(local_reqs, T_MAX, D)
+    def along(parts):
+        for mask in masks[:-1]:
+            n = len(parts) // 2
+            parts = [
+                parts[k].astype(f32) + flip(parts[k + n].astype(bf16), dz=mask).astype(f32)
+                for k in range(n)
+            ]
+        return parts[0].astype(f32)
+
+    crossed = [
+        chunk(near, k) + flip(chunk(far, k), dy=1).astype(f32) for k in range(1, outer, 2)
+    ]
+    near_sum = along([chunk(near, k) for k in range(0, outer, 2)])
+    far_sum = along([chunk(far, k) for k in range(0, outer, 2)])
+    own_sum = near_sum + flip(far_sum.astype(bf16), dy=1).astype(f32)
+    mirrored = flip(along(crossed).astype(bf16), dz=masks[-1])
 
     heads = H // 2
 
@@ -386,6 +401,8 @@
         compiler_params=pltpu.CompilerParams(vmem_limit_bytes=VMEM_LIMIT),
         name="finish",
     )(swap_pairs, here, states, needed, from_core, other, *prepared)
+    mirrored = together(mirrored, attention_out)[0]
+    expert_out = (own_sum + mirrored.astype(f32)).astype(bf16).reshape(local_reqs, T_MAX, D)
     return (new_states, attention_out, expert_out)
 
 

time: 79.4 us -> 67.3 us (0.85)
  waiting for transfers between devices: 19 us -> 14 us
  Pallas kernels: 19.4 us -> 15.2 us
  matrix products: 7.08 us -> 4.62 us
    ppermute x25, waiting for transfers between devices: 19 us -> 14 us  [flip(): return lax.ppermute(x, AXES, pairs)]
    pallas_call x1, Pallas kernels: 7.35 us -> 4.42 us  [per_device(): pl.pallas_call(functools.partial(finish_kernel, heads, block_rows, side_c...]
    dot_general x2, matrix products: 5.39 us -> 2.9 us  [feed(): gate_up = jnp.dot(x[:, :D], gate_up_weight[0], preferred_element_type=f32)]
    pallas_call x1, Pallas kernels: 4.52 us -> 3.23 us  [per_device(): pl.pallas_call(functools.partial(pack_kernel, side_count, local_reqs, lev...]
  transfers between devices with their start and end apart: 25 -> 25, of which waited for: 9 -> 9; matrix products, arithmetic and copies ran while one was open for 14% -> 12% of each run, Pallas kernels for 13% -> 20%
where the time goes in v4:
time: 67.3 us; the launch traced here: 67 us
  starting transfers between devices  27.7 us (41%)
  Pallas kernels  15.2 us (23%)
  waiting for transfers between devices  14 us (21%)
  matrix products  4.62 us (7%)
  other arithmetic  3.89 us (6%)
  between operations  1.06 us (2%)
    ppermute x25, starting transfers between devices, flip(): return lax.ppermute(x, AXES, pairs)  27.7 us
    ppermute x25, waiting for transfers between devices, flip(): return lax.ppermute(x, AXES, pairs)  14 us
    pallas_call x1, Pallas kernels, per_device(): pl.pallas_call(prep_kernel, out_shape=[jax.ShapeDtypeStruct((local_reqs,...  5.75 us
    pallas_call x1, Pallas kernels, per_device(): pl.pallas_call(functools.partial(finish_kernel, heads, block_rows, side_c...  4.42 us
    pallas_call x1, Pallas kernels, per_device(): pl.pallas_call(functools.partial(pack_kernel, side_count, local_reqs, lev...  3.23 us
    dot_general x2, matrix products, feed(): gate_up = jnp.dot(x[:, :D], gate_up_weight[0], preferred_element_type=f32)  2.9 us
    pallas_call x1, Pallas kernels, per_device(): pl.pallas_call(functools.partial(rows_kernel, peer_count), out_shape=jax....  1.83 us
    dot_general x2, matrix products, feed(): produced = jnp.dot(activated, down_weight[0], preferred_element_type=f32)  1.73 us
  transfers between devices with their start and end apart: 25, of which 9 were waited for; matrix products, arithmetic and copies ran while one was open for 12% of the time, Pallas kernels for 20%

profile of v4, /device:TPU:0, one launch (start us, length us, event | category | flops | bytes accessed | tf_op | source)
XLA Modules:
  0.0 67.0 jit_solution(11268610716833923049)
XLA Ops:
  0.6 1.8 %rows.1 = bf16[32,2432]{1,0:T(8,128)(2,1)} custom-call(bf16[2,16,2304]{2,1,0:T(8,128)(2,1)} %hidden_ref.1, s32[2,8,16]{2,1,0:T(8,128)} %bitcast.30, f32[2,8,16]{2,1,0:T(8,128)} %bitcast.31), custom_call_target="tpu_custom_call" | custom-call | tf_op jit(solution)/shard_map/rows/pallas_call | solution.py:233
  2.5 5.0 %collective-permute-start = (bf16[32,2432]{1,0:T(8,128)(2,1)}, bf16[32,2432]{1,0:T(8,128)(2,1)S(1)}, u32[]{:S(2)}, u32[]{:S(2)}) collective-permute-start(bf16[32,2432]{1,0:T(8,128)(2,1)} %rows.1), channel_id=1, source_target_pairs={{0,12},{1,13},{2,14},{3,15},{4,8},{5,9},{6,10},{7,11},{8,4},{9,5},... | collective-permute-start | bytes 466952 | tf_op jit(solution)/shard_map/ppermute | solution.py:228
  7.5 1.5 %collective-permute-start.6 = (bf16[32,2432]{1,0:T(8,128)(2,1)}, bf16[32,2432]{1,0:T(8,128)(2,1)S(1)}, u32[]{:S(2)}, u32[]{:S(2)}) collective-permute-start(bf16[32,2432]{1,0:T(8,128)(2,1)} %rows.1), channel_id=1, source_target_pairs={{0,2},{1,3},{2,0},{3,1},{4,6},{5,7},{6,4},{7,5},{8,10},{9,11},{10,... | collective-permute-start | bytes 466952 | tf_op jit(solution)/shard_map/ppermute | solution.py:228
  9.1 3.2 %pack.1 = (bf16[4,512,128]{2,1,0:T(8,128)(2,1)}, bf16[4,512,128]{2,1,0:T(8,128)(2,1)}, bf16[16,128]{1,0:T(8,128)(2,1)}) custom-call(s32[2,2]{1,0:T(2,128)} %swaps.3, s32[1]{0:T(128)} %bitcast.where_at, f32[2,4,512,128]{3,2,1,0:T(8,128)} %bitcast.27, f32[2,4,512,128]{3,2,1,0:T(8,128)} %bitcast.28), custom_call_target="tpu_custom_call" | custom-call | tf_op jit(solution)/shard_map/pack/pallas_call | solution.py:264
  12.4 0.9 %compare_bitcast_fusion = (pred[128]{0:T(512)(128)(4,1)S(1)}, pred[128]{0:T(512)(128)(4,1)S(1)}, pred[128]{0:T(512)(128)(4,1)S(1)}, pred[128]{0:T(512)(128)(4,1)...) fusion(bf16[16,128]{1,0:T(8,128)(2,1)} %get-tuple-element.24), kind=kLoop, calls=%fused_computation.61 | loop fusion | flops 768 | bytes 2304 | tf_op jit(solution)/shard_map/gt | solution.py:278
  13.3 2.1 %collective-permute-start.7 = (bf16[32,2432]{1,0:T(8,128)(2,1)S(1)}, bf16[32,2432]{1,0:T(8,128)(2,1)S(1)}, u32[]{:S(2)}, u32[]{:S(2)}) collective-permute-start(bf16[32,2432]{1,0:T(8,128)(2,1)S(1)} %collective-permute-done.6), channel_id=1, source_target_pairs={{0,4},{1,5},{2,6},{3,7},{4,0},{5,1},{6,2},{7,3},{8,12},{9,13},{10,... | collective-permute-start | bytes 466952 | tf_op jit(solution)/shard_map/ppermute | solution.py:228
  15.4 1.1 %broadcast_select_fusion.1 = bf16[4,512,128]{2,1,0:T(8,128)(2,1)S(1)} fusion(bf16[4,512,128]{2,1,0:T(8,128)(2,1)} %get-tuple-element.25, bf16[4,512,128]{2,1,0:T(8,128)(2,1)S(1)} %collective-permute-done.1.near, pred[128]{0:T(512)(128)(4,1)S(1)} %get-tuple-element.58), kind=kLoop, calls=%fused_computation.22 | loop fusion | flops 262144 | bytes 1572992 | tf_op jit(solution)/shard_map/jit(_where)/select_n | solution.py:278
  16.6 1.1 %collective-permute-start.8 = (bf16[32,2432]{1,0:T(8,128)(2,1)S(1)}, bf16[32,2432]{1,0:T(8,128)(2,1)S(1)}, u32[]{:S(2)}, u32[]{:S(2)}) collective-permute-start(bf16[32,2432]{1,0:T(8,128)(2,1)S(1)} %collective-permute-done), channel_id=1, source_target_pairs={{0,4},{1,5},{2,6},{3,7},{4,0},{5,1},{6,2},{7,3},{8,12},{9,13},{10,... | collective-permute-start | bytes 466952 | tf_op jit(solution)/shard_map/ppermute | solution.py:228
  18.4 1.5 %collective-permute-start.2 = (bf16[2,512,128]{2,1,0:T(8,128)(2,1)S(1)}, bf16[2,512,128]{2,1,0:T(8,128)(2,1)S(1)}, u32[]{:S(2)}, u32[]{:S(2)}) collective-permute-start(bf16[2,512,128]{2,1,0:T(8,128)(2,1)S(1)} %slice.109), channel_id=1, source_target_pairs={{0,2},{1,3},{2,0},{3,1},{4,6},{5,7},{6,4},{7,5},{8,10},{9,11},{10,... | collective-permute-start | bytes 786440 | tf_op jit(solution)/shard_map/ppermute | solution.py:228
  19.9 3.5 %collective-permute-done.8 = bf16[32,2432]{1,0:T(8,128)(2,1)S(1)} collective-permute-done((bf16[32,2432]{1,0:T(8,128)(2,1)S(1)}, bf16[32,2432]{1,0:T(8,128)(2,1)S(1)}, u32[]{:S(2)}, u32[]{:S(2)}) %collective-permute-start.8) | collective-permute-done | bytes 155680 | tf_op jit(solution)/shard_map/ppermute | solution.py:228
  24.7 5.8 %prep.1 = (bf16[2,16,64,128]{3,2,1,0:T(8,128)(2,1)S(1)}, f32[2,16,32,128]{3,2,1,0:T(8,128)S(1)}, bf16[2,16,48,128]{3,2,1,0:T(8,128)(2,1)S(1)}, f32[2,16,8,128]{3,2,1,0:T(8,128)S(1)}) custom-call(s32[2]{0:T(128)S(1)} %copy-done.8, bf16[2,16,2048]{2,1,0:T(8,128)(2,1)S(1)} %copy-done.3, bf16[2,16,2048]{2,1,0:T(8,128)(2,1)S(1)} %copy-done.4, ...), custom_call_target="tpu_custom_call" | custom-call | tf_op jit(solution)/shard_map/prep/pallas_call | solution.py:303
  30.5 1.5 %collective-permute-start.4 = (bf16[1,512,128]{2,1,0:T(8,128)(2,1)S(1)}, bf16[1,512,128]{2,1,0:T(8,128)(2,1)S(1)}, u32[]{:S(2)}, u32[]{:S(2)}) collective-permute-start(bf16[1,512,128]{2,1,0:T(8,128)(2,1)S(1)} %slice.141), channel_id=1, source_target_pairs={{0,4},{1,5},{2,6},{3,7},{4,0},{5,1},{6,2},{7,3},{8,12},{9,13},{10,... | collective-permute-start | bytes 393224 | tf_op jit(solution)/shard_map/ppermute | solution.py:228
  32.1 1.4 %fusion.2 = f32[256,1024]{1,0:T(8,128)S(1)} fusion(bf16[1,2304,1024]{2,1,0:T(8,128)(2,1)S(1)} %copy-done.11, bf16[256,2432]{1,0:T(8,128)(2,1)S(1)} %constant_dynamic-update-slice_fusion), kind=kOutput, calls=%fused_computation.2 | convolution fusion | flops 1207959552 | bytes 6946816 | tf_op jit(solution)/shard_map/dot_general | solution.py:334
  33.7 0.9 %fusion.4 = bf16[256,2304]{1,0:T(8,128)(2,1)S(1)} fusion(bf16[1,512,2304]{2,1,0:T(8,128)(2,1)S(1)} %copy-done, f32[256]{0:T(256)S(1)} %fusion.25, f32[256,1024]{1,0:T(8,128)S(1)} %fusion.2), kind=kOutput, calls=%fused_computation.6 | convolution fusion | flops 605945856 | bytes 4588544 | tf_op jit(solution)/shard_map/dot_general | solution.py:336
  34.8 1.0 %collective-permute-done.4 = bf16[1,512,128]{2,1,0:T(8,128)(2,1)S(1)} collective-permute-done((bf16[1,512,128]{2,1,0:T(8,128)(2,1)S(1)}, bf16[1,512,128]{2,1,0:T(8,128)(2,1)S(1)}, u32[]{:S(2)}, u32[]{:S(2)}) %collective-permute-start.4) | collective-permute-done | bytes 131104 | tf_op jit(solution)/shard_map/ppermute | solution.py:228
  35.8 1.0 %collective-permute-start.5 = (bf16[1,512,128]{2,1,0:T(8,128)(2,1)S(1)}, bf16[1,512,128]{2,1,0:T(8,128)(2,1)S(1)}, u32[]{:S(2)}, u32[]{:S(2)}) collective-permute-start(bf16[1,512,128]{2,1,0:T(8,128)(2,1)S(1)} %broadcast_select_fusion.5), channel_id=1, source_target_pairs={{0,12},{1,13},{2,14},{3,15},{4,8},{5,9},{6,10},{7,11},{8,4},{9,5},... | collective-permute-start | bytes 393224 | tf_op jit(solution)/shard_map/ppermute | solution.py:228
  37.1 1.4 %fusion = f32[256,1024]{1,0:T(8,128)S(1)} fusion(bf16[1,2304,1024]{2,1,0:T(8,128)(2,1)S(1)} %copy-done.11, bf16[256,2432]{1,0:T(8,128)(2,1)S(1)} %constant_dynamic-update-slice_fusion.5), kind=kOutput, calls=%fused_computation | convolution fusion | flops 1207959552 | bytes 6946816 | tf_op jit(solution)/shard_map/dot_general | solution.py:334
  38.8 0.9 %fusion.5 = bf16[256,2304]{1,0:T(8,128)(2,1)S(1)} fusion(bf16[1,512,2304]{2,1,0:T(8,128)(2,1)S(1)} %copy-done, f32[256]{0:T(256)S(1)} %fusion.23, f32[256,1024]{1,0:T(8,128)S(1)} %fusion), kind=kOutput, calls=%fused_computation.7 | convolution fusion | flops 605945856 | bytes 4588544 | tf_op jit(solution)/shard_map/dot_general | solution.py:336
  40.4 0.8 %collective-permute-start.18 = (bf16[32,2304]{1,0:T(8,128)(2,1)S(1)}, bf16[32,2304]{1,0:T(8,128)(2,1)S(1)}, u32[]{:S(2)}, u32[]{:S(2)}) collective-permute-start(bf16[32,2304]{1,0:T(8,128)(2,1)S(1)} %slice.224), channel_id=1, source_target_pairs={{0,4},{1,5},{2,6},{3,7},{4,0},{5,1},{6,2},{7,3},{8,12},{9,13},{10,... | collective-permute-start | bytes 442376 | tf_op jit(solution)/shard_map/ppermute | solution.py:228
  42.1 0.9 %collective-permute-start.19 = (bf16[32,2304]{1,0:T(8,128)(2,1)S(1)}, bf16[32,2304]{1,0:T(8,128)(2,1)S(1)}, u32[]{:S(2)}, u32[]{:S(2)}) collective-permute-start(bf16[32,2304]{1,0:T(8,128)(2,1)S(1)} %get-tuple-element.45), channel_id=1, source_target_pairs={{0,4},{1,5},{2,6},{3,7},{4,0},{5,1},{6,2},{7,3},{8,12},{9,13},{10,... | collective-permute-start | bytes 442376 | tf_op jit(solution)/shard_map/ppermute | solution.py:228
  43.0 1.4 %collective-permute-start.22 = (bf16[32,2304]{1,0:T(8,128)(2,1)S(1)}, bf16[32,2304]{1,0:T(8,128)(2,1)S(1)}, u32[]{:S(2)}, u32[]{:S(2)}) collective-permute-start(bf16[32,2304]{1,0:T(8,128)(2,1)S(1)} %get-tuple-element.46), channel_id=1, source_target_pairs={{0,2},{1,3},{2,0},{3,1},{4,6},{5,7},{6,4},{7,5},{8,10},{9,11},{10,... | collective-permute-start | bytes 442376 | tf_op jit(solution)/shard_map/ppermute | solution.py:228
  45.0 1.3 %collective-permute-start.14 = (bf16[1,512,128]{2,1,0:T(8,128)(2,1)S(1)}, bf16[1,512,128]{2,1,0:T(8,128)(2,1)S(1)}, u32[]{:S(2)}, u32[]{:S(2)}) collective-permute-start(bf16[1,512,128]{2,1,0:T(8,128)(2,1)S(1)} %get-tuple-element.53), channel_id=1, source_target_pairs={{0,4},{1,5},{2,6},{3,7},{4,0},{5,1},{6,2},{7,3},{8,12},{9,13},{10,... | collective-permute-start | bytes 393224 | tf_op jit(solution)/shard_map/ppermute | solution.py:228
  46.4 3.3 %collective-permute-done.22 = bf16[32,2304]{1,0:T(8,128)(2,1)S(1)} collective-permute-done((bf16[32,2304]{1,0:T(8,128)(2,1)S(1)}, bf16[32,2304]{1,0:T(8,128)(2,1)S(1)}, u32[]{:S(2)}, u32[]{:S(2)}) %collective-permute-start.22) | collective-permute-done | bytes 147488 | tf_op jit(solution)/shard_map/ppermute | solution.py:228
  49.7 1.3 %collective-permute-start.23 = (bf16[32,2304]{1,0:T(8,128)(2,1)S(1)}, bf16[32,2304]{1,0:T(8,128)(2,1)S(1)}, u32[]{:S(2)}, u32[]{:S(2)}) collective-permute-start(bf16[32,2304]{1,0:T(8,128)(2,1)S(1)} %fusion.12), channel_id=1, source_target_pairs={{0,4},{1,5},{2,6},{3,7},{4,0},{5,1},{6,2},{7,3},{8,12},{9,13},{10,... | collective-permute-start | bytes 442376 | tf_op jit(solution)/shard_map/ppermute | solution.py:228
  51.0 2.1 %collective-permute-done.14 = bf16[1,512,128]{2,1,0:T(8,128)(2,1)S(1)} collective-permute-done((bf16[1,512,128]{2,1,0:T(8,128)(2,1)S(1)}, bf16[1,512,128]{2,1,0:T(8,128)(2,1)S(1)}, u32[]{:S(2)}, u32[]{:S(2)}) %collective-permute-start.14) | collective-permute-done | bytes 131104 | tf_op jit(solution)/shard_map/ppermute | solution.py:228
  53.2 1.1 %collective-permute-start.15 = (bf16[2,512,128]{2,1,0:T(8,128)(2,1)S(1)}, bf16[2,512,128]{2,1,0:T(8,128)(2,1)S(1)}, u32[]{:S(2)}, u32[]{:S(2)}) collective-permute-start(bf16[2,512,128]{2,1,0:T(8,128)(2,1)S(1)} %get-tuple-element.51), channel_id=1, source_target_pairs={{0,2},{1,3},{2,0},{3,1},{4,6},{5,7},{6,4},{7,5},{8,10},{9,11},{10,... | collective-permute-start | bytes 786440 | tf_op jit(solution)/shard_map/ppermute | solution.py:228
  54.3 1.1 %collective-permute-done.23 = bf16[32,2304]{1,0:T(8,128)(2,1)S(1)} collective-permute-done((bf16[32,2304]{1,0:T(8,128)(2,1)S(1)}, bf16[32,2304]{1,0:T(8,128)(2,1)S(1)}, u32[]{:S(2)}, u32[]{:S(2)}) %collective-permute-start.23) | collective-permute-done | bytes 147488 | tf_op jit(solution)/shard_map/ppermute | solution.py:228
  55.4 2.9 %collective-permute-start.24 = (bf16[32,2304]{1,0:T(8,128)(2,1)S(1)}, bf16[32,2304]{1,0:T(8,128)(2,1)S(1)}, u32[]{:S(2)}, u32[]{:S(2)}) collective-permute-start(bf16[32,2304]{1,0:T(8,128)(2,1)S(1)} %fusion.14), channel_id=1, source_target_pairs={{0,12},{1,13},{2,14},{3,15},{4,8},{5,9},{6,10},{7,11},{8,4},{9,5},... | collective-permute-start | bytes 442376 | tf_op jit(solution)/shard_map/ppermute | solution.py:228
  58.3 1.4 %collective-permute-done.15 = bf16[2,512,128]{2,1,0:T(8,128)(2,1)S(1)} collective-permute-done((bf16[2,512,128]{2,1,0:T(8,128)(2,1)S(1)}, bf16[2,512,128]{2,1,0:T(8,128)(2,1)S(1)}, u32[]{:S(2)}, u32[]{:S(2)}) %collective-permute-start.15) | collective-permute-done | bytes 262176 | tf_op jit(solution)/shard_map/ppermute | solution.py:228
  60.0 1.3 %collective-permute-start.20 = (bf16[32,2304]{1,0:T(8,128)(2,1)S(1)}, bf16[32,2304]{1,0:T(8,128)(2,1)S(1)}, u32[]{:S(2)}, u32[]{:S(2)}) collective-permute-start(bf16[32,2304]{1,0:T(8,128)(2,1)S(1)} %add_convert_fusion.1), channel_id=1, source_target_pairs={{0,2},{1,3},{2,0},{3,1},{4,6},{5,7},{6,4},{7,5},{8,10},{9,11},{10,... | collective-permute-start | bytes 442376 | tf_op jit(solution)/shard_map/ppermute | solution.py:228
  61.8 4.4 %finish.1 = (f32[2,16,128,128]{3,2,1,0:T(8,128)}, bf16[2,16,2048]{2,1,0:T(8,128)(2,1)}) custom-call(s32[2,2]{1,0:T(2,128)S(1)} %copy-done.7, s32[1]{0:T(128)} %bitcast.where_at, f32[2,16,128,128]{3,2,1,0:T(8,128)S(1)} %copy-done.1, bf16[4,512,128]{2,1,0:T(8,128)(2,1)S(1)} %get-tuple-element.49.mine, bf16[4,512,128]{2,1,0:T(8,128)(2,1)S(1)} %collective-permute-done.1.near, ...), custom_call_target="tpu_custom_call" | custom-call | tf_op jit(solution)/shard_map/finish/pallas_call | solution.py:384
  66.3 0.7 %fusion.17 = bf16[32,2304]{1,0:T(8,128)(2,1)} fusion(f32[128,2304]{1,0:T(8,128)S(1)} %convert_add_fusion, bf16[32,2304]{1,0:T(8,128)(2,1)S(1)} %collective-permute-done.24, bf16[32,2304]{1,0:T(8,128)(2,1)S(1)} %collective-permute-done.20, bf16[32,2304]{1,0:T(8,128)(2,1)S(1)} %collective-permute-done.18), kind=kLoop, calls=%fused_computation.32 | loop fusion | flops 516096 | bytes 884736 | tf_op jit(solution)/shard_map/convert_element_type | solution.py:405
  (86 shorter events, 6.1 us)
Async XLA Ops:
  0.6 33.1 %copy-start = (bf16[1,512,2304]{2,1,0:T(8,128)(2,1)S(1)}, bf16[1,512,2304]{2,1,0:T(8,128)(2,1)}, u32[]{:S(2)}) copy-start(bf16[1,512,2304]{2,1,0:T(8,128)(2,1)} %param.25) | copy-start | bytes 7077892
  2.5 14.1 %collective-permute-start = (bf16[32,2432]{1,0:T(8,128)(2,1)}, bf16[32,2432]{1,0:T(8,128)(2,1)S(1)}, u32[]{:S(2)}, u32[]{:S(2)}) collective-permute-start(bf16[32,2432]{1,0:T(8,128)(2,1)} %rows.1), channel_id=1, source_target_pairs={{0,12},{1,13},{2,14},{3,15},{4,8},{5,9},{6,10},{7,11},{8,4},{9,5},... | collective-permute-start | bytes 466952 | tf_op jit(solution)/shard_map/ppermute | solution.py:228
  7.5 12.4 %collective-permute-start.10 = (bf16[32,2432]{1,0:T(8,128)(2,1)}, bf16[32,2432]{1,0:T(8,128)(2,1)S(1)}, u32[]{:S(2)}, u32[]{:S(2)}) collective-permute-start(bf16[32,2432]{1,0:T(8,128)(2,1)} %rows.1), channel_id=1, source_target_pairs={{0,4},{1,5},{2,6},{3,7},{4,0},{5,1},{6,2},{7,3},{8,12},{9,13},{10,... | collective-permute-start | bytes 466952 | tf_op jit(solution)/shard_map/ppermute | solution.py:228
  7.5 5.8 %collective-permute-start.6 = (bf16[32,2432]{1,0:T(8,128)(2,1)}, bf16[32,2432]{1,0:T(8,128)(2,1)S(1)}, u32[]{:S(2)}, u32[]{:S(2)}) collective-permute-start(bf16[32,2432]{1,0:T(8,128)(2,1)} %rows.1), channel_id=1, source_target_pairs={{0,2},{1,3},{2,0},{3,1},{4,6},{5,7},{6,4},{7,5},{8,10},{9,11},{10,... | collective-permute-start | bytes 466952 | tf_op jit(solution)/shard_map/ppermute | solution.py:228
  12.3 3.1 %collective-permute-start.1 = (bf16[4,512,128]{2,1,0:T(8,128)(2,1)}, bf16[4,512,128]{2,1,0:T(8,128)(2,1)S(1)}, u32[]{:S(2)}, u32[]{:S(2)}) collective-permute-start(bf16[4,512,128]{2,1,0:T(8,128)(2,1)} %get-tuple-element.26), channel_id=1, source_target_pairs={{0,1},{1,0},{2,3},{3,2},{4,5},{5,4},{6,7},{7,6},{8,9},{9,8},{10,11... | collective-permute-start | bytes 1572872 | tf_op jit(solution)/shard_map/ppermute | solution.py:228
  13.3 21.3 %collective-permute-start.7 = (bf16[32,2432]{1,0:T(8,128)(2,1)S(1)}, bf16[32,2432]{1,0:T(8,128)(2,1)S(1)}, u32[]{:S(2)}, u32[]{:S(2)}) collective-permute-start(bf16[32,2432]{1,0:T(8,128)(2,1)S(1)} %collective-permute-done.6), channel_id=1, source_target_pairs={{0,4},{1,5},{2,6},{3,7},{4,0},{5,1},{6,2},{7,3},{8,12},{9,13},{10,... | collective-permute-start | bytes 466952 | tf_op jit(solution)/shard_map/ppermute | solution.py:228
  16.6 6.9 %collective-permute-start.8 = (bf16[32,2432]{1,0:T(8,128)(2,1)S(1)}, bf16[32,2432]{1,0:T(8,128)(2,1)S(1)}, u32[]{:S(2)}, u32[]{:S(2)}) collective-permute-start(bf16[32,2432]{1,0:T(8,128)(2,1)S(1)} %collective-permute-done), channel_id=1, source_target_pairs={{0,4},{1,5},{2,6},{3,7},{4,0},{5,1},{6,2},{7,3},{8,12},{9,13},{10,... | collective-permute-start | bytes 466952 | tf_op jit(solution)/shard_map/ppermute | solution.py:228
  17.7 6.9 %collective-permute-start.3 = (bf16[32,2432]{1,0:T(8,128)(2,1)S(1)}, bf16[32,2432]{1,0:T(8,128)(2,1)S(1)}, u32[]{:S(2)}, u32[]{:S(2)}) collective-permute-start(bf16[32,2432]{1,0:T(8,128)(2,1)S(1)} %collective-permute-done), channel_id=1, source_target_pairs={{0,2},{1,3},{2,0},{3,1},{4,6},{5,7},{6,4},{7,5},{8,10},{9,11},{10,... | collective-permute-start | bytes 466952 | tf_op jit(solution)/shard_map/ppermute | solution.py:228
  18.3 6.3 %copy-start.2 = (f32[2,16,2048]{2,1,0:T(8,128)S(1)}, f32[2,16,2048]{2,1,0:T(8,128)}, u32[]{:S(2)}) copy-start(f32[2,16,2048]{2,1,0:T(8,128)} %decay_ref.1) | copy-start | bytes 786436
  18.3 6.3 %copy-start.3 = (bf16[2,16,2048]{2,1,0:T(8,128)(2,1)S(1)}, bf16[2,16,2048]{2,1,0:T(8,128)(2,1)}, u32[]{:S(2)}) copy-start(bf16[2,16,2048]{2,1,0:T(8,128)(2,1)} %q_ref.1) | copy-start | bytes 393220
  18.3 6.3 %copy-start.4 = (bf16[2,16,2048]{2,1,0:T(8,128)(2,1)S(1)}, bf16[2,16,2048]{2,1,0:T(8,128)(2,1)}, u32[]{:S(2)}) copy-start(bf16[2,16,2048]{2,1,0:T(8,128)(2,1)} %k_ref.1) | copy-start | bytes 393220
  18.4 6.3 %copy-start.5 = (bf16[2,16,2048]{2,1,0:T(8,128)(2,1)S(1)}, bf16[2,16,2048]{2,1,0:T(8,128)(2,1)}, u32[]{:S(2)}) copy-start(bf16[2,16,2048]{2,1,0:T(8,128)(2,1)} %v_ref.1) | copy-start | bytes 393220
  18.4 12.0 %collective-permute-start.2 = (bf16[2,512,128]{2,1,0:T(8,128)(2,1)S(1)}, bf16[2,512,128]{2,1,0:T(8,128)(2,1)S(1)}, u32[]{:S(2)}, u32[]{:S(2)}) collective-permute-start(bf16[2,512,128]{2,1,0:T(8,128)(2,1)S(1)} %slice.109), channel_id=1, source_target_pairs={{0,2},{1,3},{2,0},{3,1},{4,6},{5,7},{6,4},{7,5},{8,10},{9,11},{10,... | collective-permute-start | bytes 786440 | tf_op jit(solution)/shard_map/ppermute | solution.py:228
  23.4 8.7 %copy-start.11 = (bf16[1,2304,1024]{2,1,0:T(8,128)(2,1)S(1)}, bf16[1,2304,1024]{2,1,0:T(8,128)(2,1)}, u32[]{:S(2)}) copy-start(bf16[1,2304,1024]{2,1,0:T(8,128)(2,1)} %param.24) | copy-start | bytes 14155780
  23.5 8.5 %collective-permute-start.11 = (bf16[128,2432]{1,0:T(8,128)(2,1)S(1)}, bf16[128,2432]{1,0:T(8,128)(2,1)S(1)}, u32[]{:S(2)}, u32[]{:S(2)}) collective-permute-start(bf16[128,2432]{1,0:T(8,128)(2,1)S(1)} %pad_maximum_fusion), channel_id=1, source_target_pairs={{0,1},{1,0},{2,3},{3,2},{4,5},{5,4},{6,7},{7,6},{8,9},{9,8},{10,11... | collective-permute-start | bytes 1867784 | tf_op jit(solution)/shard_map/ppermute | solution.py:228
  23.6 11.0 %collective-permute-start.9 = (bf16[32,2432]{1,0:T(8,128)(2,1)S(1)}, bf16[32,2432]{1,0:T(8,128)(2,1)S(1)}, u32[]{:S(2)}, u32[]{:S(2)}) collective-permute-start(bf16[32,2432]{1,0:T(8,128)(2,1)S(1)} %collective-permute-done.8), channel_id=1, source_target_pairs={{0,2},{1,3},{2,0},{3,1},{4,6},{5,7},{6,4},{7,5},{8,10},{9,11},{10,... | collective-permute-start | bytes 466952 | tf_op jit(solution)/shard_map/ppermute | solution.py:228
  30.5 5.3 %collective-permute-start.4 = (bf16[1,512,128]{2,1,0:T(8,128)(2,1)S(1)}, bf16[1,512,128]{2,1,0:T(8,128)(2,1)S(1)}, u32[]{:S(2)}, u32[]{:S(2)}) collective-permute-start(bf16[1,512,128]{2,1,0:T(8,128)(2,1)S(1)} %slice.141), channel_id=1, source_target_pairs={{0,4},{1,5},{2,6},{3,7},{4,0},{5,1},{6,2},{7,3},{8,12},{9,13},{10,... | collective-permute-start | bytes 393224 | tf_op jit(solution)/shard_map/ppermute | solution.py:228
  34.7 2.4 %collective-permute-start.12 = (bf16[128,2432]{1,0:T(8,128)(2,1)S(1)}, bf16[128,2432]{1,0:T(8,128)(2,1)S(1)}, u32[]{:S(2)}, u32[]{:S(2)}) collective-permute-start(bf16[128,2432]{1,0:T(8,128)(2,1)S(1)} %pad_maximum_fusion.1), channel_id=1, source_target_pairs={{0,1},{1,0},{2,3},{3,2},{4,5},{5,4},{6,7},{7,6},{8,9},{9,8},{10,11... | collective-permute-start | bytes 1867784 | tf_op jit(solution)/shard_map/ppermute | solution.py:228
  35.8 9.2 %collective-permute-start.5 = (bf16[1,512,128]{2,1,0:T(8,128)(2,1)S(1)}, bf16[1,512,128]{2,1,0:T(8,128)(2,1)S(1)}, u32[]{:S(2)}, u32[]{:S(2)}) collective-permute-start(bf16[1,512,128]{2,1,0:T(8,128)(2,1)S(1)} %broadcast_select_fusion.5), channel_id=1, source_target_pairs={{0,12},{1,13},{2,14},{3,15},{4,8},{5,9},{6,10},{7,11},{8,4},{9,5},... | collective-permute-start | bytes 393224 | tf_op jit(solution)/shard_map/ppermute | solution.py:228
  36.9 3.3 %collective-permute-start.17 = (bf16[128,2304]{1,0:T(8,128)(2,1)S(1)}, bf16[128,2304]{1,0:T(8,128)(2,1)S(1)}, u32[]{:S(2)}, u32[]{:S(2)}) collective-permute-start(bf16[128,2304]{1,0:T(8,128)(2,1)S(1)} %slice.132), channel_id=1, source_target_pairs={{0,1},{1,0},{2,3},{3,2},{4,5},{5,4},{6,7},{7,6},{8,9},{9,8},{10,11... | collective-permute-start | bytes 1769480 | tf_op jit(solution)/shard_map/ppermute | solution.py:228
  39.7 2.2 %collective-permute-start.13 = (bf16[128,2304]{1,0:T(8,128)(2,1)S(1)}, bf16[128,2304]{1,0:T(8,128)(2,1)S(1)}, u32[]{:S(2)}, u32[]{:S(2)}) collective-permute-start(bf16[128,2304]{1,0:T(8,128)(2,1)S(1)} %slice.156), channel_id=1, source_target_pairs={{0,1},{1,0},{2,3},{3,2},{4,5},{5,4},{6,7},{7,6},{8,9},{9,8},{10,11... | collective-permute-start | bytes 1769480 | tf_op jit(solution)/shard_map/ppermute | solution.py:228
  40.4 25.8 %collective-permute-start.18 = (bf16[32,2304]{1,0:T(8,128)(2,1)S(1)}, bf16[32,2304]{1,0:T(8,128)(2,1)S(1)}, u32[]{:S(2)}, u32[]{:S(2)}) collective-permute-start(bf16[32,2304]{1,0:T(8,128)(2,1)S(1)} %slice.224), channel_id=1, source_target_pairs={{0,4},{1,5},{2,6},{3,7},{4,0},{5,1},{6,2},{7,3},{8,12},{9,13},{10,... | collective-permute-start | bytes 442376 | tf_op jit(solution)/shard_map/ppermute | solution.py:228
  42.1 17.8 %collective-permute-start.19 = (bf16[32,2304]{1,0:T(8,128)(2,1)S(1)}, bf16[32,2304]{1,0:T(8,128)(2,1)S(1)}, u32[]{:S(2)}, u32[]{:S(2)}) collective-permute-start(bf16[32,2304]{1,0:T(8,128)(2,1)S(1)} %get-tuple-element.45), channel_id=1, source_target_pairs={{0,4},{1,5},{2,6},{3,7},{4,0},{5,1},{6,2},{7,3},{8,12},{9,13},{10,... | collective-permute-start | bytes 442376 | tf_op jit(solution)/shard_map/ppermute | solution.py:228
  43.0 6.7 %collective-permute-start.22 = (bf16[32,2304]{1,0:T(8,128)(2,1)S(1)}, bf16[32,2304]{1,0:T(8,128)(2,1)S(1)}, u32[]{:S(2)}, u32[]{:S(2)}) collective-permute-start(bf16[32,2304]{1,0:T(8,128)(2,1)S(1)} %get-tuple-element.46), channel_id=1, source_target_pairs={{0,2},{1,3},{2,0},{3,1},{4,6},{5,7},{6,4},{7,5},{8,10},{9,11},{10,... | collective-permute-start | bytes 442376 | tf_op jit(solution)/shard_map/ppermute | solution.py:228
  44.4 9.9 %collective-permute-start.21 = (bf16[32,2304]{1,0:T(8,128)(2,1)S(1)}, bf16[32,2304]{1,0:T(8,128)(2,1)S(1)}, u32[]{:S(2)}, u32[]{:S(2)}) collective-permute-start(bf16[32,2304]{1,0:T(8,128)(2,1)S(1)} %get-tuple-element.47), channel_id=1, source_target_pairs={{0,2},{1,3},{2,0},{3,1},{4,6},{5,7},{6,4},{7,5},{8,10},{9,11},{10,... | collective-permute-start | bytes 442376 | tf_op jit(solution)/shard_map/ppermute | solution.py:228
  45.0 14.7 %copy-start.9 = (bf16[4,512,128]{2,1,0:T(8,128)(2,1)S(1)}, bf16[4,512,128]{2,1,0:T(8,128)(2,1)}, u32[]{:S(2)}) copy-start(bf16[4,512,128]{2,1,0:T(8,128)(2,1)} %get-tuple-element.25) | copy-start | bytes 1572868
  45.0 8.1 %collective-permute-start.14 = (bf16[1,512,128]{2,1,0:T(8,128)(2,1)S(1)}, bf16[1,512,128]{2,1,0:T(8,128)(2,1)S(1)}, u32[]{:S(2)}, u32[]{:S(2)}) collective-permute-start(bf16[1,512,128]{2,1,0:T(8,128)(2,1)S(1)} %get-tuple-element.53), channel_id=1, source_target_pairs={{0,4},{1,5},{2,6},{3,7},{4,0},{5,1},{6,2},{7,3},{8,12},{9,13},{10,... | collective-permute-start | bytes 393224 | tf_op jit(solution)/shard_map/ppermute | solution.py:228
  49.7 5.7 %collective-permute-start.23 = (bf16[32,2304]{1,0:T(8,128)(2,1)S(1)}, bf16[32,2304]{1,0:T(8,128)(2,1)S(1)}, u32[]{:S(2)}, u32[]{:S(2)}) collective-permute-start(bf16[32,2304]{1,0:T(8,128)(2,1)S(1)} %fusion.12), channel_id=1, source_target_pairs={{0,4},{1,5},{2,6},{3,7},{4,0},{5,1},{6,2},{7,3},{8,12},{9,13},{10,... | collective-permute-start | bytes 442376 | tf_op jit(solution)/shard_map/ppermute | solution.py:228
  53.2 6.5 %collective-permute-start.15 = (bf16[2,512,128]{2,1,0:T(8,128)(2,1)S(1)}, bf16[2,512,128]{2,1,0:T(8,128)(2,1)S(1)}, u32[]{:S(2)}, u32[]{:S(2)}) collective-permute-start(bf16[2,512,128]{2,1,0:T(8,128)(2,1)S(1)} %get-tuple-element.51), channel_id=1, source_target_pairs={{0,2},{1,3},{2,0},{3,1},{4,6},{5,7},{6,4},{7,5},{8,10},{9,11},{10,... | collective-permute-start | bytes 786440 | tf_op jit(solution)/shard_map/ppermute | solution.py:228
  55.4 10.8 %collective-permute-start.24 = (bf16[32,2304]{1,0:T(8,128)(2,1)S(1)}, bf16[32,2304]{1,0:T(8,128)(2,1)S(1)}, u32[]{:S(2)}, u32[]{:S(2)}) collective-permute-start(bf16[32,2304]{1,0:T(8,128)(2,1)S(1)} %fusion.14), channel_id=1, source_target_pairs={{0,12},{1,13},{2,14},{3,15},{4,8},{5,9},{6,10},{7,11},{8,4},{9,5},... | collective-permute-start | bytes 442376 | tf_op jit(solution)/shard_map/ppermute | solution.py:228
  59.8 2.0 %collective-permute-start.16 = (bf16[4,512,128]{2,1,0:T(8,128)(2,1)S(1)}, bf16[4,512,128]{2,1,0:T(8,128)(2,1)S(1)}, u32[]{:S(2)}, u32[]{:S(2)}) collective-permute-start(bf16[4,512,128]{2,1,0:T(8,128)(2,1)S(1)} %get-tuple-element.48), channel_id=1, source_target_pairs={{0,1},{1,0},{2,3},{3,2},{4,5},{5,4},{6,7},{7,6},{8,9},{9,8},{10,11... | collective-permute-start | bytes 1572872 | tf_op jit(solution)/shard_map/ppermute | solution.py:228
  60.0 6.3 %collective-permute-start.20 = (bf16[32,2304]{1,0:T(8,128)(2,1)S(1)}, bf16[32,2304]{1,0:T(8,128)(2,1)S(1)}, u32[]{:S(2)}, u32[]{:S(2)}) collective-permute-start(bf16[32,2304]{1,0:T(8,128)(2,1)S(1)} %add_convert_fusion.1), channel_id=1, source_target_pairs={{0,2},{1,3},{2,0},{3,1},{4,6},{5,7},{6,4},{7,5},{8,10},{9,11},{10,... | collective-permute-start | bytes 442376 | tf_op jit(solution)/shard_map/ppermute | solution.py:228
  (5 other events, 20.0 us)

commit v5 on v4

--- a/solution.py
+++ b/solution.py
@@ -90,10 +90,15 @@
     return vectors * lax.rsqrt(jnp.sum(vectors * vectors, axis=-1, keepdims=True) + 1e-06)
 
 
-def prep_kernel(
-    counts, q_ref, k_ref, v_ref, decay_ref, rate_ref, z_ref, uo_ref, key_ref, kept_ref
-):
-    r = pl.program_id(0)
+def fetch_and_prep_kernel(r, counts, weight_ref, *refs):
+    fetch = pltpu.make_async_copy(weight_ref, refs[-2], refs[-1])
+    fetch.start()
+    prep_kernel(r, counts, *refs[:-2])
+    fetch.wait()
+
+
+def prep_kernel(r, counts, q_ref, k_ref, v_ref, decay_ref, rate_ref, *refs):
+    z_ref, uo_ref, key_ref, kept_ref = refs[-4:]
     count = counts[r]
     times = lax.broadcasted_iota(jnp.int32, (T_MAX, 1), 0)
     live = (times < count).astype(jnp.float32)
@@ -157,7 +162,7 @@
     r = pl.program_id(0)
     first = pl.program_id(1) * heads
     position = where_at[0]
-    slots = states_ref.shape[0]
+    slots = z_ref.shape[0]
     chip = chip_of(position, sides, bits)
     source = jnp.int32(0)
     for p in range(swaps.shape[0]):
@@ -168,7 +173,6 @@
         kind = jnp.where(one == two, 1, kind)
         slot = position * slots + r
         source = jnp.where((swaps[p, 0] == slot) | (swaps[p, 1] == slot), kind, source)
-    partner = jnp.where(source == 1, 1 - r, r)
     for h in range(heads):
         row = (first + h) * DK
         block = jnp.bitwise_xor(lax.div(row, block_rows), chip)
@@ -176,20 +180,20 @@
         arrived = jnp.where(
             source == 2, mine[block, at], jnp.where(source == 3, near[block, at], other[block, at])
         )
-        state = jnp.where(source >= 2, arrived.astype(jnp.float32), states_ref[partner, h])
-        both = jnp.dot(z_ref[0, h], state.astype(jnp.bfloat16), preferred_element_type=jnp.float32)
+        state = jnp.where(source >= 2, arrived.astype(jnp.float32), states_ref[0, h])
+        both = jnp.dot(z_ref[r, first + h], state.astype(jnp.bfloat16), preferred_element_type=jnp.float32)
         both = both[: 2 * T_MAX] + both[2 * T_MAX :]
-        writes = uo_ref[0, h, :T_MAX] - both[:T_MAX]
-        read = uo_ref[0, h, T_MAX:] + both[T_MAX:]
+        writes = uo_ref[r, first + h, :T_MAX] - both[:T_MAX]
+        read = uo_ref[r, first + h, T_MAX:] + both[T_MAX:]
         out_ref[0, :, h * DV : (h + 1) * DV] = read.astype(out_ref.dtype)
         high, low = split(writes)
         written = lax.dot_general(
-            key_ref[0, h],
+            key_ref[r, first + h],
             jnp.concatenate([high, low, high], axis=0),
             (((0,), (0,)), ((), ())),
             preferred_element_type=jnp.float32,
         )
-        new_ref[0, h] = jnp.transpose(kept_ref[0, h])[:, :1] * state + written
+        new_ref[0, h] = jnp.transpose(kept_ref[r, first + h])[:, :1] * state + written
 
 
 def per_device(
@@ -270,17 +274,64 @@
             in_specs=[state_spec(False), state_spec(True)],
             out_specs=[out_spec, out_spec, pl.BlockSpec((16, DV), lambda g, swaps, at: (0, 0))],
         ),
+        compiler_params=pltpu.CompilerParams(vmem_limit_bytes=VMEM_LIMIT),
         name="pack",
     )(swap_pairs, here, state_blocks, state_blocks)
     from_core = flip(send, ds=1)
 
+    lanes = H * DK
+    per_head = [
+        (4 * T_MAX, DK, bf16),
+        (2 * T_MAX, DV, f32),
+        (3 * T_MAX, DK, bf16),
+        (8, DK, f32),
+    ]
+
+    def prepare(r, counts, weight=None, earlier=()):
+        anywhere = [pl.BlockSpec(memory_space=pl.ANY)]
+        fetched = [] if weight is None else [weight]
+        return pl.pallas_call(
+            functools.partial(fetch_and_prep_kernel if fetched else prep_kernel, r),
+            out_shape=[jax.ShapeDtypeStruct((local_reqs, H, n, m), t) for n, m, t in per_head]
+            + fetched,
+            grid_spec=pltpu.PrefetchScalarGridSpec(
+                num_scalar_prefetch=1,
+                grid=(1,),
+                in_specs=anywhere * len(fetched)
+                + [pl.BlockSpec((1, T_MAX, lanes), lambda g, c: (r, 0, 0))] * 4
+                + [pl.BlockSpec((1, T_MAX, H), lambda g, c: (r, 0, 0))]
+                + anywhere * len(earlier),
+                out_specs=[
+                    pl.BlockSpec((1, H, n, m), lambda g, c: (r, 0, 0, 0)) for n, m, t in per_head
+                ]
+                + anywhere * len(fetched),
+                scratch_shapes=[pltpu.SemaphoreType.DMA] * len(fetched),
+            ),
+            input_output_aliases={6 + len(fetched) + i: i for i in range(len(earlier))},
+            compiler_params=pltpu.CompilerParams(vmem_limit_bytes=VMEM_LIMIT),
+            name=f"prep{r}",
+        )(
+            counts,
+            *fetched,
+            query_vectors,
+            key_vectors,
+            value_vectors,
+            decay_log,
+            write_rate,
+            *earlier,
+        )
+
     def choose(flag, yes, no):
         return jnp.where(plan[flag] > 0, yes, no)
 
     held = choose(0, keep, from_core)
     direct[0], held = together(direct[0], held)
+    counts, = together(token_counts, held)[:1]
+    prepared = prepare(0, counts)
     for i, mask in enumerate(reversed(masks)):
         fresh = direct[i : i + 1] + [flip(x, dz=mask) for x in line[1:]]
+        if i == levels - 1:
+            fresh[-1], *prepared = together(fresh[-1], *prepared)
         if i == 0:
             across = across + [flip(x, dy=1) for x in fresh]
         else:
@@ -290,31 +341,8 @@
             ]
         line = line + fresh
 
-    lanes = H * DK
-    vec_spec = pl.BlockSpec((1, T_MAX, lanes), lambda r, c: (r, 0, 0))
-
-    per_head = [
-        (4 * T_MAX, DK, bf16),
-        (2 * T_MAX, DV, f32),
-        (3 * T_MAX, DK, bf16),
-        (8, DK, f32),
-    ]
     counts = together(token_counts, across[1])[0]
-    prepared = pl.pallas_call(
-        prep_kernel,
-        out_shape=[jax.ShapeDtypeStruct((local_reqs, H, n, m), t) for n, m, t in per_head],
-        grid_spec=pltpu.PrefetchScalarGridSpec(
-            num_scalar_prefetch=1,
-            grid=(local_reqs,),
-            in_specs=[vec_spec] * 4 + [pl.BlockSpec((1, T_MAX, H), lambda r, c: (r, 0, 0))],
-            out_specs=[
-                pl.BlockSpec((1, H, n, m), lambda r, c: (r, 0, 0, 0)) for n, m, t in per_head
-            ],
-        ),
-        compiler_params=pltpu.CompilerParams(vmem_limit_bytes=VMEM_LIMIT),
-        name="prep",
-    )(counts, query_vectors, key_vectors, value_vectors, decay_log, write_rate)
-
+    *prepared, first_weight = prepare(1, counts, gate_up_weight[0], prepared)
     ways = [dict(dy=1)] + [dict(dz=mask) for mask in masks]
     up = []
     for level in range(levels):
@@ -331,7 +359,7 @@
         weight = jnp.sum(
             (gate[:, :peer_count] + gate[:, peer_count : 2 * peer_count]) * picked, axis=1
         )
-        gate_up = jnp.dot(x[:, :D], gate_up_weight[0], preferred_element_type=f32)
+        gate_up = jnp.dot(x[:, :D], first_weight, preferred_element_type=f32)
         activated = (jax.nn.silu(gate_up[:, :FF]) * gate_up[:, FF:]).astype(bf16)
         produced = jnp.dot(activated, down_weight[0], preferred_element_type=f32)
         return (produced * weight[:, None]).astype(bf16)
@@ -367,11 +395,11 @@
             ]
         return parts[0].astype(f32)
 
-    crossed = [
-        chunk(near, k) + flip(chunk(far, k), dy=1).astype(f32) for k in range(1, outer, 2)
-    ]
+    arrived = [flip(chunk(far, k), dy=1) for k in range(1, outer, 2)]
+    crossed = [chunk(near, k) + arrived[k // 2].astype(f32) for k in range(1, outer, 2)]
     near_sum = along([chunk(near, k) for k in range(0, outer, 2)])
-    far_sum = along([chunk(far, k) for k in range(0, outer, 2)])
+    far_later = together(far, arrived[-1])[0]
+    far_sum = along([chunk(far_later, k) for k in range(0, outer, 2)])
     own_sum = near_sum + flip(far_sum.astype(bf16), dy=1).astype(f32)
     mirrored = flip(along(crossed).astype(bf16), dz=masks[-1])
 
@@ -380,7 +408,15 @@
     def head_spec(n, m):
         return pl.BlockSpec((1, heads, n, m), lambda r, g, swaps, at: (r, g, 0, 0))
 
-    piece_spec = pl.BlockSpec((blocks, block_rows, DV), lambda r, g, swaps, at: (0, 0, 0))
+    resident = pl.BlockSpec(memory_space=pltpu.VMEM)
+
+    def state_index(r, g, swaps, at):
+        inside = jnp.bool_(False)
+        for p in range(side_count):
+            one, two = lax.div(swaps[p, 0], local_reqs), lax.div(swaps[p, 1], local_reqs)
+            inside = inside | ((one == at[0]) & (two == at[0]))
+        return (jnp.where(inside, local_reqs - 1 - r, r), g, 0, 0)
+
     new_states, attention_out = pl.pallas_call(
         functools.partial(finish_kernel, heads, block_rows, side_count, levels - 1),
         out_shape=(
@@ -390,9 +426,7 @@
         grid_spec=pltpu.PrefetchScalarGridSpec(
             num_scalar_prefetch=2,
             grid=(local_reqs, H // heads),
-            in_specs=[pl.BlockSpec((local_reqs, heads, DK, DV), lambda r, g, swaps, at: (0, g, 0, 0))]
-            + [piece_spec] * 3
-            + [head_spec(n, m) for n, m, _ in per_head],
+            in_specs=[pl.BlockSpec((1, heads, DK, DV), state_index)] + [resident] * 7,
             out_specs=[
                 head_spec(DK, DV),
                 pl.BlockSpec((1, T_MAX, heads * DV), lambda r, g, swaps, at: (r, 0, g)),

time: 67.3 us -> 63.7 us (0.947)
  local copies, waits for them, and re-layouts: 0.49 us -> 2.81 us
  starting transfers between devices: 27.7 us -> 25.4 us
  other arithmetic: 3.89 us -> 2.01 us
  Pallas kernels: 15.2 us -> 13.4 us
    pallas_call x1, Pallas kernels: 3.23 us -> 0.76 us  [per_device(): pl.pallas_call(functools.partial(pack_kernel, side_count, local_reqs, lev...]
    unnamed x32 -> x34, local copies, waits for them, and re-layouts: 0.2 us -> 2.52 us
    ppermute x25, starting transfers between devices: 27.7 us -> 25.4 us  [flip(): return lax.ppermute(x, AXES, pairs)]
    select_n x6, other arithmetic: 1.36 us -> 0.3 us  [choose(): return jnp.where(plan[flag] > 0, yes, no)]
    gt x1, other arithmetic: 0.91 us -> 0.01 us  [choose(): return jnp.where(plan[flag] > 0, yes, no)]
    pallas_call x1 -> x2, Pallas kernels: 5.75 us -> 6.63 us  [prepare(): pl.pallas_call(functools.partial(fetch_and_prep_kernel if fetched else pr...]
  transfers between devices with their start and end apart: 25 -> 25, of which waited for: 9 -> 9; matrix products, arithmetic and copies ran while one was open for 12% -> 10% of each run, Pallas kernels for 20% -> 18%
where the time goes in v5:
time: 63.7 us; the launch traced here: 63.5 us
  starting transfers between devices  25.4 us (40%)
  waiting for transfers between devices  14.3 us (22%)
  Pallas kernels  13.4 us (21%)
  matrix products  4.62 us (7%)
  local copies, waits for them, and re-layouts  2.81 us (4%)
  other arithmetic  2.01 us (3%)
  between operations  1.06 us (2%)
    ppermute x25, starting transfers between devices, flip(): return lax.ppermute(x, AXES, pairs)  25.4 us
    ppermute x25, waiting for transfers between devices, flip(): return lax.ppermute(x, AXES, pairs)  14.3 us
    pallas_call x2, Pallas kernels, prepare(): pl.pallas_call(functools.partial(fetch_and_prep_kernel if fetched else pr...  6.63 us
    pallas_call x1, Pallas kernels, per_device(): pl.pallas_call(functools.partial(finish_kernel, heads, block_rows, side_c...  4.22 us
    dot_general x2, matrix products, feed(): gate_up = jnp.dot(x[:, :D], first_weight, preferred_element_type=f32)  2.89 us
    unnamed x34, local copies, waits for them, and re-layouts  2.52 us
    pallas_call x1, Pallas kernels, per_device(): pl.pallas_call(functools.partial(rows_kernel, peer_count), out_shape=jax....  1.83 us
    dot_general x2, matrix products, feed(): produced = jnp.dot(activated, down_weight[0], preferred_element_type=f32)  1.73 us
  transfers between devices with their start and end apart: 25, of which 9 were waited for; matrix products, arithmetic and copies ran while one was open for 10% of the time, Pallas kernels for 18%

profile of v5, /device:TPU:0, one launch (start us, length us, event | category | flops | bytes accessed | tf_op | source)
XLA Modules:
  0.0 63.5 jit_solution(697011764169282160)
XLA Ops:
  0.6 1.8 %rows.1 = bf16[32,2432]{1,0:T(8,128)(2,1)} custom-call(bf16[2,16,2304]{2,1,0:T(8,128)(2,1)} %hidden_ref.1, s32[2,8,16]{2,1,0:T(8,128)} %bitcast.29, f32[2,8,16]{2,1,0:T(8,128)} %bitcast.30), custom_call_target="tpu_custom_call" | custom-call | tf_op jit(solution)/shard_map/rows/pallas_call | solution.py:237
  2.5 5.0 %collective-permute-start = (bf16[32,2432]{1,0:T(8,128)(2,1)}, bf16[32,2432]{1,0:T(8,128)(2,1)S(1)}, u32[]{:S(2)}, u32[]{:S(2)}) collective-permute-start(bf16[32,2432]{1,0:T(8,128)(2,1)} %rows.1), channel_id=1, source_target_pairs={{0,12},{1,13},{2,14},{3,15},{4,8},{5,9},{6,10},{7,11},{8,4},{9,5},... | collective-permute-start | bytes 466952 | tf_op jit(solution)/shard_map/ppermute | solution.py:232
  7.5 1.5 %collective-permute-start.7 = (bf16[32,2432]{1,0:T(8,128)(2,1)}, bf16[32,2432]{1,0:T(8,128)(2,1)S(1)}, u32[]{:S(2)}, u32[]{:S(2)}) collective-permute-start(bf16[32,2432]{1,0:T(8,128)(2,1)} %rows.1), channel_id=1, source_target_pairs={{0,2},{1,3},{2,0},{3,1},{4,6},{5,7},{6,4},{7,5},{8,10},{9,11},{10,... | collective-permute-start | bytes 466952 | tf_op jit(solution)/shard_map/ppermute | solution.py:232
  9.1 1.6 %copy-done.1 = f32[2,16,128,128]{3,2,1,0:T(8,128)S(1)} copy-done((f32[2,16,128,128]{3,2,1,0:T(8,128)S(1)}, f32[2,16,128,128]{3,2,1,0:T(8,128)}, u32[]{:S(2)}) %copy-start.1) | copy-done | bytes 2097176
  11.3 0.8 %pack.1 = (bf16[4,512,128]{2,1,0:T(8,128)(2,1)S(1)}, bf16[4,512,128]{2,1,0:T(8,128)(2,1)S(1)}, bf16[16,128]{1,0:T(8,128)(2,1)S(1)}) custom-call(s32[2,2]{1,0:T(2,128)S(1)} %copy-done.9, s32[1]{0:T(128)} %bitcast.where_at, f32[2,4,512,128]{3,2,1,0:T(8,128)S(1)} %bitcast.25, f32[2,4,512,128]{3,2,1,0:T(8,128)S(1)} %bitcast.26), custom_call_target="tpu_custom_call" | custom-call | tf_op jit(solution)/shard_map/pack/pallas_call | solution.py:268
  12.3 0.9 %collective-permute-done.7 = bf16[32,2432]{1,0:T(8,128)(2,1)S(1)} collective-permute-done((bf16[32,2432]{1,0:T(8,128)(2,1)}, bf16[32,2432]{1,0:T(8,128)(2,1)S(1)}, u32[]{:S(2)}, u32[]{:S(2)}) %collective-permute-start.7) | collective-permute-done | bytes 155680 | tf_op jit(solution)/shard_map/ppermute | solution.py:232
  13.2 1.8 %collective-permute-start.8 = (bf16[32,2432]{1,0:T(8,128)(2,1)S(1)}, bf16[32,2432]{1,0:T(8,128)(2,1)S(1)}, u32[]{:S(2)}, u32[]{:S(2)}) collective-permute-start(bf16[32,2432]{1,0:T(8,128)(2,1)S(1)} %collective-permute-done.7), channel_id=1, source_target_pairs={{0,4},{1,5},{2,6},{3,7},{4,0},{5,1},{6,2},{7,3},{8,12},{9,13},{10,... | collective-permute-start | bytes 466952 | tf_op jit(solution)/shard_map/ppermute | solution.py:232
  15.1 1.1 %collective-permute-start.4 = (bf16[32,2432]{1,0:T(8,128)(2,1)S(1)}, bf16[32,2432]{1,0:T(8,128)(2,1)S(1)}, u32[]{:S(2)}, u32[]{:S(2)}) collective-permute-start(bf16[32,2432]{1,0:T(8,128)(2,1)S(1)} %collective-permute-done), channel_id=1, source_target_pairs={{0,4},{1,5},{2,6},{3,7},{4,0},{5,1},{6,2},{7,3},{8,12},{9,13},{10,... | collective-permute-start | bytes 466952 | tf_op jit(solution)/shard_map/ppermute | solution.py:232
  16.2 0.8 %collective-permute-start.3 = (bf16[32,2432]{1,0:T(8,128)(2,1)S(1)}, bf16[32,2432]{1,0:T(8,128)(2,1)S(1)}, u32[]{:S(2)}, u32[]{:S(2)}) collective-permute-start(bf16[32,2432]{1,0:T(8,128)(2,1)S(1)} %collective-permute-done), channel_id=1, source_target_pairs={{0,2},{1,3},{2,0},{3,1},{4,6},{5,7},{6,4},{7,5},{8,10},{9,11},{10,... | collective-permute-start | bytes 466952 | tf_op jit(solution)/shard_map/ppermute | solution.py:232
  17.0 1.3 %collective-permute-start.2 = (bf16[2,512,128]{2,1,0:T(8,128)(2,1)S(1)}, bf16[2,512,128]{2,1,0:T(8,128)(2,1)S(1)}, u32[]{:S(2)}, u32[]{:S(2)}) collective-permute-start(bf16[2,512,128]{2,1,0:T(8,128)(2,1)S(1)} %slice.109), channel_id=1, source_target_pairs={{0,2},{1,3},{2,0},{3,1},{4,6},{5,7},{6,4},{7,5},{8,10},{9,11},{10,... | collective-permute-start | bytes 786440 | tf_op jit(solution)/shard_map/ppermute | solution.py:232
  18.4 3.1 %prep0.1 = (bf16[2,16,64,128]{3,2,1,0:T(8,128)(2,1)S(1)}, f32[2,16,32,128]{3,2,1,0:T(8,128)S(1)}, bf16[2,16,48,128]{3,2,1,0:T(8,128)(2,1)S(1)}, f32[2,16,8,128]{3,2,1,0:T(8,128)S(1)}) custom-call(s32[2]{0:T(128)S(1)} %copy-done.11, bf16[2,16,2048]{2,1,0:T(8,128)(2,1)S(1)} %copy-done.5, bf16[2,16,2048]{2,1,0:T(8,128)(2,1)S(1)} %copy-done.6, ...), custom_call_target="tpu_custom_call" | custom-call | tf_op jit(solution)/shard_map/prep0/pallas_call | solution.py:293
  21.6 0.8 %collective-permute-done.4 = bf16[32,2432]{1,0:T(8,128)(2,1)S(1)} collective-permute-done((bf16[32,2432]{1,0:T(8,128)(2,1)S(1)}, bf16[32,2432]{1,0:T(8,128)(2,1)S(1)}, u32[]{:S(2)}, u32[]{:S(2)}) %collective-permute-start.4) | collective-permute-done | bytes 155680 | tf_op jit(solution)/shard_map/ppermute | solution.py:232
  22.3 1.0 %collective-permute-start.9 = (bf16[32,2432]{1,0:T(8,128)(2,1)S(1)}, bf16[32,2432]{1,0:T(8,128)(2,1)S(1)}, u32[]{:S(2)}, u32[]{:S(2)}) collective-permute-start(bf16[32,2432]{1,0:T(8,128)(2,1)S(1)} %collective-permute-done.4), channel_id=1, source_target_pairs={{0,2},{1,3},{2,0},{3,1},{4,6},{5,7},{6,4},{7,5},{8,10},{9,11},{10,... | collective-permute-start | bytes 466952 | tf_op jit(solution)/shard_map/ppermute | solution.py:232
  23.6 3.5 %prep1.1 = (bf16[2,16,64,128]{3,2,1,0:T(8,128)(2,1)S(1)}, f32[2,16,32,128]{3,2,1,0:T(8,128)S(1)}, bf16[2,16,48,128]{3,2,1,0:T(8,128)(2,1)S(1)}, f32[2,16,8,128]{3,2,1,0:T(8,128)S(1)}, bf16[2304,1024]{1,0:T(8,128)(2,1)S(1)}) custom-call(s32[2]{0:T(128)S(1)} %copy-done.11, ...), custom_call_target="tpu_custom_call", output_to_operand_aliasing={{0}: (7, {}), {1}: (8, {}), {2}: (9, {}), {3}: (10, {})} | custom-call | tf_op jit(solution)/shard_map/prep1/pallas_call | solution.py:293
  27.1 1.7 %collective-permute-done.2 = bf16[2,512,128]{2,1,0:T(8,128)(2,1)S(1)} collective-permute-done((bf16[2,512,128]{2,1,0:T(8,128)(2,1)S(1)}, bf16[2,512,128]{2,1,0:T(8,128)(2,1)S(1)}, u32[]{:S(2)}, u32[]{:S(2)}) %collective-permute-start.2) | collective-permute-done | bytes 262176 | tf_op jit(solution)/shard_map/ppermute | solution.py:232
  28.8 1.0 %collective-permute-start.5 = (bf16[1,512,128]{2,1,0:T(8,128)(2,1)S(1)}, bf16[1,512,128]{2,1,0:T(8,128)(2,1)S(1)}, u32[]{:S(2)}, u32[]{:S(2)}) collective-permute-start(bf16[1,512,128]{2,1,0:T(8,128)(2,1)S(1)} %slice.141), channel_id=1, source_target_pairs={{0,4},{1,5},{2,6},{3,7},{4,0},{5,1},{6,2},{7,3},{8,12},{9,13},{10,... | collective-permute-start | bytes 393224 | tf_op jit(solution)/shard_map/ppermute | solution.py:232
  29.9 1.4 %fusion.6 = f32[256,1024]{1,0:T(8,128)S(1)} fusion(bf16[2304,1024]{1,0:T(8,128)(2,1)S(1)} %get-tuple-element.57, bf16[256,2432]{1,0:T(8,128)(2,1)S(1)} %constant_dynamic-update-slice_fusion), kind=kOutput, calls=%fused_computation.8 | convolution fusion | flops 1207959552 | bytes 6946816 | tf_op jit(solution)/shard_map/dot_general | solution.py:362
  31.6 0.9 %fusion = bf16[256,2304]{1,0:T(8,128)(2,1)S(1)} fusion(bf16[1,512,2304]{2,1,0:T(8,128)(2,1)S(1)} %copy-done, f32[256]{0:T(256)S(1)} %fusion.23, f32[256,1024]{1,0:T(8,128)S(1)} %fusion.6), kind=kOutput, calls=%fused_computation.2 | convolution fusion | flops 605945856 | bytes 4588544 | tf_op jit(solution)/shard_map/dot_general | solution.py:364
  32.6 1.2 %collective-permute-done.5 = bf16[1,512,128]{2,1,0:T(8,128)(2,1)S(1)} collective-permute-done((bf16[1,512,128]{2,1,0:T(8,128)(2,1)S(1)}, bf16[1,512,128]{2,1,0:T(8,128)(2,1)S(1)}, u32[]{:S(2)}, u32[]{:S(2)}) %collective-permute-start.5) | collective-permute-done | bytes 131104 | tf_op jit(solution)/shard_map/ppermute | solution.py:232
  33.9 1.0 %collective-permute-start.6 = (bf16[1,512,128]{2,1,0:T(8,128)(2,1)S(1)}, bf16[1,512,128]{2,1,0:T(8,128)(2,1)S(1)}, u32[]{:S(2)}, u32[]{:S(2)}) collective-permute-start(bf16[1,512,128]{2,1,0:T(8,128)(2,1)S(1)} %broadcast_select_fusion.5), channel_id=1, source_target_pairs={{0,12},{1,13},{2,14},{3,15},{4,8},{5,9},{6,10},{7,11},{8,4},{9,5},... | collective-permute-start | bytes 393224 | tf_op jit(solution)/shard_map/ppermute | solution.py:232
  35.1 1.4 %fusion.4 = f32[256,1024]{1,0:T(8,128)S(1)} fusion(bf16[2304,1024]{1,0:T(8,128)(2,1)S(1)} %get-tuple-element.57, bf16[256,2432]{1,0:T(8,128)(2,1)S(1)} %constant_dynamic-update-slice_fusion.5), kind=kOutput, calls=%fused_computation.6 | convolution fusion | flops 1207959552 | bytes 6946816 | tf_op jit(solution)/shard_map/dot_general | solution.py:362
  36.7 0.9 %fusion.1 = bf16[256,2304]{1,0:T(8,128)(2,1)S(1)} fusion(bf16[1,512,2304]{2,1,0:T(8,128)(2,1)S(1)} %copy-done, f32[256]{0:T(256)S(1)} %fusion.21, f32[256,1024]{1,0:T(8,128)S(1)} %fusion.4), kind=kOutput, calls=%fused_computation.3 | convolution fusion | flops 605945856 | bytes 4588544 | tf_op jit(solution)/shard_map/dot_general | solution.py:364
  38.8 1.0 %collective-permute-done.13 = bf16[128,2304]{1,0:T(8,128)(2,1)S(1)} collective-permute-done((bf16[128,2304]{1,0:T(8,128)(2,1)S(1)}, bf16[128,2304]{1,0:T(8,128)(2,1)S(1)}, u32[]{:S(2)}, u32[]{:S(2)}) %collective-permute-start.13) | collective-permute-done | bytes 589856 | tf_op jit(solution)/shard_map/ppermute | solution.py:232
  40.6 1.5 %collective-permute-start.22 = (bf16[32,2304]{1,0:T(8,128)(2,1)S(1)}, bf16[32,2304]{1,0:T(8,128)(2,1)S(1)}, u32[]{:S(2)}, u32[]{:S(2)}) collective-permute-start(bf16[32,2304]{1,0:T(8,128)(2,1)S(1)} %get-tuple-element.69), channel_id=1, source_target_pairs={{0,2},{1,3},{2,0},{3,1},{4,6},{5,7},{6,4},{7,5},{8,10},{9,11},{10,... | collective-permute-start | bytes 442376 | tf_op jit(solution)/shard_map/ppermute | solution.py:232
  42.9 3.9 %collective-permute-done.19 = bf16[32,2304]{1,0:T(8,128)(2,1)S(1)} collective-permute-done((bf16[32,2304]{1,0:T(8,128)(2,1)S(1)}, bf16[32,2304]{1,0:T(8,128)(2,1)S(1)}, u32[]{:S(2)}, u32[]{:S(2)}) %collective-permute-start.19) | collective-permute-done | bytes 147488 | tf_op jit(solution)/shard_map/ppermute | solution.py:232
  46.8 0.8 %collective-permute-start.23 = (bf16[32,2304]{1,0:T(8,128)(2,1)S(1)}, bf16[32,2304]{1,0:T(8,128)(2,1)S(1)}, u32[]{:S(2)}, u32[]{:S(2)}) collective-permute-start(bf16[32,2304]{1,0:T(8,128)(2,1)S(1)} %fusion.10), channel_id=1, source_target_pairs={{0,4},{1,5},{2,6},{3,7},{4,0},{5,1},{6,2},{7,3},{8,12},{9,13},{10,... | collective-permute-start | bytes 442376 | tf_op jit(solution)/shard_map/ppermute | solution.py:232
  48.4 1.2 %collective-permute-start.20 = (bf16[32,2304]{1,0:T(8,128)(2,1)S(1)}, bf16[32,2304]{1,0:T(8,128)(2,1)S(1)}, u32[]{:S(2)}, u32[]{:S(2)}) collective-permute-start(bf16[32,2304]{1,0:T(8,128)(2,1)S(1)} %slice.137), channel_id=1, source_target_pairs={{0,4},{1,5},{2,6},{3,7},{4,0},{5,1},{6,2},{7,3},{8,12},{9,13},{10,... | collective-permute-start | bytes 442376 | tf_op jit(solution)/shard_map/ppermute | solution.py:232
  49.6 3.6 %collective-permute-done.23 = bf16[32,2304]{1,0:T(8,128)(2,1)S(1)} collective-permute-done((bf16[32,2304]{1,0:T(8,128)(2,1)S(1)}, bf16[32,2304]{1,0:T(8,128)(2,1)S(1)}, u32[]{:S(2)}, u32[]{:S(2)}) %collective-permute-start.23) | collective-permute-done | bytes 147488 | tf_op jit(solution)/shard_map/ppermute | solution.py:232
  53.3 3.0 %collective-permute-start.24 = (bf16[32,2304]{1,0:T(8,128)(2,1)S(1)}, bf16[32,2304]{1,0:T(8,128)(2,1)S(1)}, u32[]{:S(2)}, u32[]{:S(2)}) collective-permute-start(bf16[32,2304]{1,0:T(8,128)(2,1)S(1)} %fusion.12), channel_id=1, source_target_pairs={{0,12},{1,13},{2,14},{3,15},{4,8},{5,9},{6,10},{7,11},{8,4},{9,5},... | collective-permute-start | bytes 442376 | tf_op jit(solution)/shard_map/ppermute | solution.py:232
  56.5 0.9 %collective-permute-start.21 = (bf16[32,2304]{1,0:T(8,128)(2,1)S(1)}, bf16[32,2304]{1,0:T(8,128)(2,1)S(1)}, u32[]{:S(2)}, u32[]{:S(2)}) collective-permute-start(bf16[32,2304]{1,0:T(8,128)(2,1)S(1)} %add_convert_fusion.1), channel_id=1, source_target_pairs={{0,2},{1,3},{2,0},{3,1},{4,6},{5,7},{6,4},{7,5},{8,10},{9,11},{10,... | collective-permute-start | bytes 442376 | tf_op jit(solution)/shard_map/ppermute | solution.py:232
  57.4 0.9 %collective-permute-done.16.other = bf16[4,512,128]{2,1,0:T(8,128)(2,1)S(1)} collective-permute-done((bf16[4,512,128]{2,1,0:T(8,128)(2,1)S(1)}, bf16[4,512,128]{2,1,0:T(8,128)(2,1)S(1)}, u32[]{:S(2)}, u32[]{:S(2)}) %collective-permute-start.16) | collective-permute-done | bytes 524320 | tf_op jit(solution)/shard_map/ppermute | solution.py:232
  58.3 4.2 %finish.1 = (f32[2,16,128,128]{3,2,1,0:T(8,128)}, bf16[2,16,2048]{2,1,0:T(8,128)(2,1)}) custom-call(s32[2,2]{1,0:T(2,128)S(1)} %copy-done.10, s32[1]{0:T(128)} %bitcast.where_at, f32[2,16,128,128]{3,2,1,0:T(8,128)S(1)} %copy-done.2, bf16[4,512,128]{2,1,0:T(8,128)(2,1)S(1)} %get-tuple-element.72.mine, bf16[4,512,128]{2,1,0:T(8,128)(2,1)S(1)} %collective-permute-done.1.near, ...), custom_call_target="tpu_custom_call" | custom-call | tf_op jit(solution)/shard_map/finish/pallas_call | solution.py:420
  (90 shorter events, 6.9 us)
Async XLA Ops:
  0.6 30.9 %copy-start = (bf16[1,512,2304]{2,1,0:T(8,128)(2,1)S(1)}, bf16[1,512,2304]{2,1,0:T(8,128)(2,1)}, u32[]{:S(2)}) copy-start(bf16[1,512,2304]{2,1,0:T(8,128)(2,1)} %param.25) | copy-start | bytes 7077892
  2.5 12.7 %collective-permute-start = (bf16[32,2432]{1,0:T(8,128)(2,1)}, bf16[32,2432]{1,0:T(8,128)(2,1)S(1)}, u32[]{:S(2)}, u32[]{:S(2)}) collective-permute-start(bf16[32,2432]{1,0:T(8,128)(2,1)} %rows.1), channel_id=1, source_target_pairs={{0,12},{1,13},{2,14},{3,15},{4,8},{5,9},{6,10},{7,11},{8,4},{9,5},... | collective-permute-start | bytes 466952 | tf_op jit(solution)/shard_map/ppermute | solution.py:232
  7.5 10.8 %collective-permute-start.10 = (bf16[32,2432]{1,0:T(8,128)(2,1)}, bf16[32,2432]{1,0:T(8,128)(2,1)S(1)}, u32[]{:S(2)}, u32[]{:S(2)}) collective-permute-start(bf16[32,2432]{1,0:T(8,128)(2,1)} %rows.1), channel_id=1, source_target_pairs={{0,4},{1,5},{2,6},{3,7},{4,0},{5,1},{6,2},{7,3},{8,12},{9,13},{10,... | collective-permute-start | bytes 466952 | tf_op jit(solution)/shard_map/ppermute | solution.py:232
  7.5 5.7 %collective-permute-start.7 = (bf16[32,2432]{1,0:T(8,128)(2,1)}, bf16[32,2432]{1,0:T(8,128)(2,1)S(1)}, u32[]{:S(2)}, u32[]{:S(2)}) collective-permute-start(bf16[32,2432]{1,0:T(8,128)(2,1)} %rows.1), channel_id=1, source_target_pairs={{0,2},{1,3},{2,0},{3,1},{4,6},{5,7},{6,4},{7,5},{8,10},{9,11},{10,... | collective-permute-start | bytes 466952 | tf_op jit(solution)/shard_map/ppermute | solution.py:232
  12.1 3.0 %collective-permute-start.1 = (bf16[4,512,128]{2,1,0:T(8,128)(2,1)S(1)}, bf16[4,512,128]{2,1,0:T(8,128)(2,1)S(1)}, u32[]{:S(2)}, u32[]{:S(2)}) collective-permute-start(bf16[4,512,128]{2,1,0:T(8,128)(2,1)S(1)} %get-tuple-element.38), channel_id=1, source_target_pairs={{0,1},{1,0},{2,3},{3,2},{4,5},{5,4},{6,7},{7,6},{8,9},{9,8},{10,11... | collective-permute-start | bytes 1572872 | tf_op jit(solution)/shard_map/ppermute | solution.py:232
  12.2 6.2 %copy-start.7 = (bf16[2,16,2048]{2,1,0:T(8,128)(2,1)S(1)}, bf16[2,16,2048]{2,1,0:T(8,128)(2,1)}, u32[]{:S(2)}) copy-start(bf16[2,16,2048]{2,1,0:T(8,128)(2,1)} %refs_2_.1) | copy-start | bytes 393220
  13.2 19.2 %collective-permute-start.8 = (bf16[32,2432]{1,0:T(8,128)(2,1)S(1)}, bf16[32,2432]{1,0:T(8,128)(2,1)S(1)}, u32[]{:S(2)}, u32[]{:S(2)}) collective-permute-start(bf16[32,2432]{1,0:T(8,128)(2,1)S(1)} %collective-permute-done.7), channel_id=1, source_target_pairs={{0,4},{1,5},{2,6},{3,7},{4,0},{5,1},{6,2},{7,3},{8,12},{9,13},{10,... | collective-permute-start | bytes 466952 | tf_op jit(solution)/shard_map/ppermute | solution.py:232
  15.0 3.4 %copy-start.5 = (bf16[2,16,2048]{2,1,0:T(8,128)(2,1)S(1)}, bf16[2,16,2048]{2,1,0:T(8,128)(2,1)}, u32[]{:S(2)}) copy-start(bf16[2,16,2048]{2,1,0:T(8,128)(2,1)} %refs_0_.1) | copy-start | bytes 393220
  15.0 3.4 %copy-start.6 = (bf16[2,16,2048]{2,1,0:T(8,128)(2,1)S(1)}, bf16[2,16,2048]{2,1,0:T(8,128)(2,1)}, u32[]{:S(2)}) copy-start(bf16[2,16,2048]{2,1,0:T(8,128)(2,1)} %refs_1_.1) | copy-start | bytes 393220
  15.0 3.4 %copy-start.8 = (f32[2,16,16]{2,1,0:T(8,128)S(1)}, f32[2,16,16]{2,1,0:T(8,128)}, u32[]{:S(2)}) copy-start(f32[2,16,16]{2,1,0:T(8,128)} %refs_4_.1) | copy-start | bytes 6148
  15.0 3.4 %copy-start.11 = (s32[2]{0:T(128)S(1)}, s32[2]{0:T(128)}, u32[]{:S(2)}) copy-start(s32[2]{0:T(128)} %counts.1) | copy-start | bytes 28
  15.0 8.5 %copy-start.3 = (bf16[1,2304,1024]{2,1,0:T(8,128)(2,1)S(1)}, bf16[1,2304,1024]{2,1,0:T(8,128)(2,1)}, u32[]{:S(2)}) copy-start(bf16[1,2304,1024]{2,1,0:T(8,128)(2,1)} %param.24) | copy-start | bytes 14155780
  15.1 7.2 %collective-permute-start.4 = (bf16[32,2432]{1,0:T(8,128)(2,1)S(1)}, bf16[32,2432]{1,0:T(8,128)(2,1)S(1)}, u32[]{:S(2)}, u32[]{:S(2)}) collective-permute-start(bf16[32,2432]{1,0:T(8,128)(2,1)S(1)} %collective-permute-done), channel_id=1, source_target_pairs={{0,4},{1,5},{2,6},{3,7},{4,0},{5,1},{6,2},{7,3},{8,12},{9,13},{10,... | collective-permute-start | bytes 466952 | tf_op jit(solution)/shard_map/ppermute | solution.py:232
  16.2 7.3 %collective-permute-start.3 = (bf16[32,2432]{1,0:T(8,128)(2,1)S(1)}, bf16[32,2432]{1,0:T(8,128)(2,1)S(1)}, u32[]{:S(2)}, u32[]{:S(2)}) collective-permute-start(bf16[32,2432]{1,0:T(8,128)(2,1)S(1)} %collective-permute-done), channel_id=1, source_target_pairs={{0,2},{1,3},{2,0},{3,1},{4,6},{5,7},{6,4},{7,5},{8,10},{9,11},{10,... | collective-permute-start | bytes 466952 | tf_op jit(solution)/shard_map/ppermute | solution.py:232
  17.0 11.7 %collective-permute-start.2 = (bf16[2,512,128]{2,1,0:T(8,128)(2,1)S(1)}, bf16[2,512,128]{2,1,0:T(8,128)(2,1)S(1)}, u32[]{:S(2)}, u32[]{:S(2)}) collective-permute-start(bf16[2,512,128]{2,1,0:T(8,128)(2,1)S(1)} %slice.109), channel_id=1, source_target_pairs={{0,2},{1,3},{2,0},{3,1},{4,6},{5,7},{6,4},{7,5},{8,10},{9,11},{10,... | collective-permute-start | bytes 786440 | tf_op jit(solution)/shard_map/ppermute | solution.py:232
  22.3 10.1 %collective-permute-start.9 = (bf16[32,2432]{1,0:T(8,128)(2,1)S(1)}, bf16[32,2432]{1,0:T(8,128)(2,1)S(1)}, u32[]{:S(2)}, u32[]{:S(2)}) collective-permute-start(bf16[32,2432]{1,0:T(8,128)(2,1)S(1)} %collective-permute-done.4), channel_id=1, source_target_pairs={{0,2},{1,3},{2,0},{3,1},{4,6},{5,7},{6,4},{7,5},{8,10},{9,11},{10,... | collective-permute-start | bytes 466952 | tf_op jit(solution)/shard_map/ppermute | solution.py:232
  23.4 6.4 %collective-permute-start.11 = (bf16[128,2432]{1,0:T(8,128)(2,1)S(1)}, bf16[128,2432]{1,0:T(8,128)(2,1)S(1)}, u32[]{:S(2)}, u32[]{:S(2)}) collective-permute-start(bf16[128,2432]{1,0:T(8,128)(2,1)S(1)} %pad_maximum_fusion), channel_id=1, source_target_pairs={{0,1},{1,0},{2,3},{3,2},{4,5},{5,4},{6,7},{7,6},{8,9},{9,8},{10,11... | collective-permute-start | bytes 1867784 | tf_op jit(solution)/shard_map/ppermute | solution.py:232
  28.8 5.0 %collective-permute-start.5 = (bf16[1,512,128]{2,1,0:T(8,128)(2,1)S(1)}, bf16[1,512,128]{2,1,0:T(8,128)(2,1)S(1)}, u32[]{:S(2)}, u32[]{:S(2)}) collective-permute-start(bf16[1,512,128]{2,1,0:T(8,128)(2,1)S(1)} %slice.141), channel_id=1, source_target_pairs={{0,4},{1,5},{2,6},{3,7},{4,0},{5,1},{6,2},{7,3},{8,12},{9,13},{10,... | collective-permute-start | bytes 393224 | tf_op jit(solution)/shard_map/ppermute | solution.py:232
  32.5 2.5 %collective-permute-start.12 = (bf16[128,2432]{1,0:T(8,128)(2,1)S(1)}, bf16[128,2432]{1,0:T(8,128)(2,1)S(1)}, u32[]{:S(2)}, u32[]{:S(2)}) collective-permute-start(bf16[128,2432]{1,0:T(8,128)(2,1)S(1)} %pad_maximum_fusion.1), channel_id=1, source_target_pairs={{0,1},{1,0},{2,3},{3,2},{4,5},{5,4},{6,7},{7,6},{8,9},{9,8},{10,11... | collective-permute-start | bytes 1867784 | tf_op jit(solution)/shard_map/ppermute | solution.py:232
  33.9 8.3 %collective-permute-start.6 = (bf16[1,512,128]{2,1,0:T(8,128)(2,1)S(1)}, bf16[1,512,128]{2,1,0:T(8,128)(2,1)S(1)}, u32[]{:S(2)}, u32[]{:S(2)}) collective-permute-start(bf16[1,512,128]{2,1,0:T(8,128)(2,1)S(1)} %broadcast_select_fusion.5), channel_id=1, source_target_pairs={{0,12},{1,13},{2,14},{3,15},{4,8},{5,9},{6,10},{7,11},{8,4},{9,5},... | collective-permute-start | bytes 393224 | tf_op jit(solution)/shard_map/ppermute | solution.py:232
  34.9 3.3 %collective-permute-start.17 = (bf16[128,2304]{1,0:T(8,128)(2,1)S(1)}, bf16[128,2304]{1,0:T(8,128)(2,1)S(1)}, u32[]{:S(2)}, u32[]{:S(2)}) collective-permute-start(bf16[128,2304]{1,0:T(8,128)(2,1)S(1)} %slice.132), channel_id=1, source_target_pairs={{0,1},{1,0},{2,3},{3,2},{4,5},{5,4},{6,7},{7,6},{8,9},{9,8},{10,11... | collective-permute-start | bytes 1769480 | tf_op jit(solution)/shard_map/ppermute | solution.py:232
  37.6 2.2 %collective-permute-start.13 = (bf16[128,2304]{1,0:T(8,128)(2,1)S(1)}, bf16[128,2304]{1,0:T(8,128)(2,1)S(1)}, u32[]{:S(2)}, u32[]{:S(2)}) collective-permute-start(bf16[128,2304]{1,0:T(8,128)(2,1)S(1)} %slice.156), channel_id=1, source_target_pairs={{0,1},{1,0},{2,3},{3,2},{4,5},{5,4},{6,7},{7,6},{8,9},{9,8},{10,11... | collective-permute-start | bytes 1769480 | tf_op jit(solution)/shard_map/ppermute | solution.py:232
  38.4 24.2 %collective-permute-start.18 = (bf16[32,2304]{1,0:T(8,128)(2,1)S(1)}, bf16[32,2304]{1,0:T(8,128)(2,1)S(1)}, u32[]{:S(2)}, u32[]{:S(2)}) collective-permute-start(bf16[32,2304]{1,0:T(8,128)(2,1)S(1)} %slice.222), channel_id=1, source_target_pairs={{0,4},{1,5},{2,6},{3,7},{4,0},{5,1},{6,2},{7,3},{8,12},{9,13},{10,... | collective-permute-start | bytes 442376 | tf_op jit(solution)/shard_map/ppermute | solution.py:232
  40.0 6.7 %collective-permute-start.19 = (bf16[32,2304]{1,0:T(8,128)(2,1)S(1)}, bf16[32,2304]{1,0:T(8,128)(2,1)S(1)}, u32[]{:S(2)}, u32[]{:S(2)}) collective-permute-start(bf16[32,2304]{1,0:T(8,128)(2,1)S(1)} %get-tuple-element.70), channel_id=1, source_target_pairs={{0,2},{1,3},{2,0},{3,1},{4,6},{5,7},{6,4},{7,5},{8,10},{9,11},{10,... | collective-permute-start | bytes 442376 | tf_op jit(solution)/shard_map/ppermute | solution.py:232
  40.6 9.0 %collective-permute-start.22 = (bf16[32,2304]{1,0:T(8,128)(2,1)S(1)}, bf16[32,2304]{1,0:T(8,128)(2,1)S(1)}, u32[]{:S(2)}, u32[]{:S(2)}) collective-permute-start(bf16[32,2304]{1,0:T(8,128)(2,1)S(1)} %get-tuple-element.69), channel_id=1, source_target_pairs={{0,2},{1,3},{2,0},{3,1},{4,6},{5,7},{6,4},{7,5},{8,10},{9,11},{10,... | collective-permute-start | bytes 442376 | tf_op jit(solution)/shard_map/ppermute | solution.py:232
  42.2 5.4 %collective-permute-start.14 = (bf16[1,512,128]{2,1,0:T(8,128)(2,1)S(1)}, bf16[1,512,128]{2,1,0:T(8,128)(2,1)S(1)}, u32[]{:S(2)}, u32[]{:S(2)}) collective-permute-start(bf16[1,512,128]{2,1,0:T(8,128)(2,1)S(1)} %get-tuple-element.76), channel_id=1, source_target_pairs={{0,4},{1,5},{2,6},{3,7},{4,0},{5,1},{6,2},{7,3},{8,12},{9,13},{10,... | collective-permute-start | bytes 393224 | tf_op jit(solution)/shard_map/ppermute | solution.py:232
  46.8 6.4 %collective-permute-start.23 = (bf16[32,2304]{1,0:T(8,128)(2,1)S(1)}, bf16[32,2304]{1,0:T(8,128)(2,1)S(1)}, u32[]{:S(2)}, u32[]{:S(2)}) collective-permute-start(bf16[32,2304]{1,0:T(8,128)(2,1)S(1)} %fusion.10), channel_id=1, source_target_pairs={{0,4},{1,5},{2,6},{3,7},{4,0},{5,1},{6,2},{7,3},{8,12},{9,13},{10,... | collective-permute-start | bytes 442376 | tf_op jit(solution)/shard_map/ppermute | solution.py:232
  47.7 8.6 %collective-permute-start.15 = (bf16[2,512,128]{2,1,0:T(8,128)(2,1)S(1)}, bf16[2,512,128]{2,1,0:T(8,128)(2,1)S(1)}, u32[]{:S(2)}, u32[]{:S(2)}) collective-permute-start(bf16[2,512,128]{2,1,0:T(8,128)(2,1)S(1)} %get-tuple-element.74), channel_id=1, source_target_pairs={{0,2},{1,3},{2,0},{3,1},{4,6},{5,7},{6,4},{7,5},{8,10},{9,11},{10,... | collective-permute-start | bytes 786440 | tf_op jit(solution)/shard_map/ppermute | solution.py:232
  48.4 8.0 %collective-permute-start.20 = (bf16[32,2304]{1,0:T(8,128)(2,1)S(1)}, bf16[32,2304]{1,0:T(8,128)(2,1)S(1)}, u32[]{:S(2)}, u32[]{:S(2)}) collective-permute-start(bf16[32,2304]{1,0:T(8,128)(2,1)S(1)} %slice.137), channel_id=1, source_target_pairs={{0,4},{1,5},{2,6},{3,7},{4,0},{5,1},{6,2},{7,3},{8,12},{9,13},{10,... | collective-permute-start | bytes 442376 | tf_op jit(solution)/shard_map/ppermute | solution.py:232
  53.3 9.3 %collective-permute-start.24 = (bf16[32,2304]{1,0:T(8,128)(2,1)S(1)}, bf16[32,2304]{1,0:T(8,128)(2,1)S(1)}, u32[]{:S(2)}, u32[]{:S(2)}) collective-permute-start(bf16[32,2304]{1,0:T(8,128)(2,1)S(1)} %fusion.12), channel_id=1, source_target_pairs={{0,12},{1,13},{2,14},{3,15},{4,8},{5,9},{6,10},{7,11},{8,4},{9,5},... | collective-permute-start | bytes 442376 | tf_op jit(solution)/shard_map/ppermute | solution.py:232
  56.4 2.0 %collective-permute-start.16 = (bf16[4,512,128]{2,1,0:T(8,128)(2,1)S(1)}, bf16[4,512,128]{2,1,0:T(8,128)(2,1)S(1)}, u32[]{:S(2)}, u32[]{:S(2)}) collective-permute-start(bf16[4,512,128]{2,1,0:T(8,128)(2,1)S(1)} %get-tuple-element.71), channel_id=1, source_target_pairs={{0,1},{1,0},{2,3},{3,2},{4,5},{5,4},{6,7},{7,6},{8,9},{9,8},{10,11... | collective-permute-start | bytes 1572872 | tf_op jit(solution)/shard_map/ppermute | solution.py:232
  56.5 6.3 %collective-permute-start.21 = (bf16[32,2304]{1,0:T(8,128)(2,1)S(1)}, bf16[32,2304]{1,0:T(8,128)(2,1)S(1)}, u32[]{:S(2)}, u32[]{:S(2)}) collective-permute-start(bf16[32,2304]{1,0:T(8,128)(2,1)S(1)} %add_convert_fusion.1), channel_id=1, source_target_pairs={{0,2},{1,3},{2,0},{3,1},{4,6},{5,7},{6,4},{7,5},{8,10},{9,11},{10,... | collective-permute-start | bytes 442376 | tf_op jit(solution)/shard_map/ppermute | solution.py:232
  (6 other events, 10.8 us)

commit v6 on v5

--- a/solution.py
+++ b/solution.py
@@ -173,27 +173,29 @@
         kind = jnp.where(one == two, 1, kind)
         slot = position * slots + r
         source = jnp.where((swaps[p, 0] == slot) | (swaps[p, 1] == slot), kind, source)
-    for h in range(heads):
-        row = (first + h) * DK
-        block = jnp.bitwise_xor(lax.div(row, block_rows), chip)
-        at = pl.ds(pl.multiple_of(lax.rem(row, block_rows), DK), DK)
-        arrived = jnp.where(
-            source == 2, mine[block, at], jnp.where(source == 3, near[block, at], other[block, at])
-        )
-        state = jnp.where(source >= 2, arrived.astype(jnp.float32), states_ref[0, h])
-        both = jnp.dot(z_ref[r, first + h], state.astype(jnp.bfloat16), preferred_element_type=jnp.float32)
-        both = both[: 2 * T_MAX] + both[2 * T_MAX :]
-        writes = uo_ref[r, first + h, :T_MAX] - both[:T_MAX]
-        read = uo_ref[r, first + h, T_MAX:] + both[T_MAX:]
-        out_ref[0, :, h * DV : (h + 1) * DV] = read.astype(out_ref.dtype)
-        high, low = split(writes)
-        written = lax.dot_general(
-            key_ref[r, first + h],
-            jnp.concatenate([high, low, high], axis=0),
-            (((0,), (0,)), ((), ())),
-            preferred_element_type=jnp.float32,
-        )
-        new_ref[0, h] = jnp.transpose(kept_ref[r, first + h])[:, :1] * state + written
+    def steps(gathered):
+        for h in range(heads):
+            row = (first + h) * DK
+            block = jnp.bitwise_xor(lax.div(row, block_rows), chip)
+            at = pl.ds(pl.multiple_of(lax.rem(row, block_rows), DK), DK)
+            state = states_ref[0, h] if gathered is None else gathered[block, at].astype(jnp.float32)
+            both = jnp.dot(z_ref[r, first + h], state.astype(jnp.bfloat16), preferred_element_type=jnp.float32)
+            both = both[: 2 * T_MAX] + both[2 * T_MAX :]
+            writes = uo_ref[r, first + h, :T_MAX] - both[:T_MAX]
+            read = uo_ref[r, first + h, T_MAX:] + both[T_MAX:]
+            out_ref[0, :, h * DV : (h + 1) * DV] = read.astype(out_ref.dtype)
+            high, low = split(writes)
+            written = lax.dot_general(
+                key_ref[r, first + h],
+                jnp.concatenate([high, low, high], axis=0),
+                (((0,), (0,)), ((), ())),
+                preferred_element_type=jnp.float32,
+            )
+            new_ref[0, h] = jnp.transpose(kept_ref[r, first + h])[:, :1] * state + written
+
+    for kind, gathered in ((2, mine), (3, near), (4, other)):
+        pl.when(source == kind)(functools.partial(steps, gathered))
+    pl.when(source < 2)(functools.partial(steps, None))
 
 
 def per_device(
@@ -343,16 +345,6 @@
 
     counts = together(token_counts, across[1])[0]
     *prepared, first_weight = prepare(1, counts, gate_up_weight[0], prepared)
-    ways = [dict(dy=1)] + [dict(dz=mask) for mask in masks]
-    up = []
-    for level in range(levels):
-        n = held.shape[0] // 2
-        came = flip(held[n:], **ways[level])
-        if level == 0:
-            came, *prepared = together(came, *prepared)
-        up.append((held[:n], came))
-        held = choose(3 + 2 * level, held[:n], came)
-    needed = flip(held, **ways[levels])
     def feed(x):
         gate = x[:, D:].astype(f32)
         picked = (experts == position).astype(f32)
@@ -364,16 +356,27 @@
         produced = jnp.dot(activated, down_weight[0], preferred_element_type=f32)
         return (produced * weight[:, None]).astype(bf16)
 
-    def chip_feed(group):
-        return feed(jnp.concatenate([group, flip(group, ds=1)]))
-
+    far = jnp.concatenate(across)
+    near = jnp.concatenate(line)
+    near = feed(together(jnp.concatenate([near, flip(near, ds=1)]), far)[0])
+    far = jnp.concatenate([far, flip(far, ds=1)])
+    ways = [dict(dy=1)] + [dict(dz=mask) for mask in masks]
+    up = []
+    for level in range(levels):
+        n = held.shape[0] // 2
+        came = flip(held[n:], **ways[level])
+        if level == 0:
+            came, *prepared = together(came, *prepared)
+        elif level == 1:
+            came = together(came, near)[0]
+        up.append((held[:n], came))
+        held = choose(3 + 2 * level, held[:n], came)
+    needed = flip(held, **ways[levels])
     def chip_sum(fed):
         n = fed.shape[0] // 2
         return fed[:n].astype(f32) + flip(fed[n:], ds=1).astype(f32)
 
-    near = chip_feed(jnp.concatenate(line))
-    across[-1], near = together(across[-1], near)
-    far = chip_sum(chip_feed(jnp.concatenate(across))).astype(bf16)
+    far = chip_sum(feed(together(far, near)[0])).astype(bf16)
     near = chip_sum(near)
     needed = together(needed, far)[0]
 
@@ -403,7 +406,7 @@
     own_sum = near_sum + flip(far_sum.astype(bf16), dy=1).astype(f32)
     mirrored = flip(along(crossed).astype(bf16), dz=masks[-1])
 
-    heads = H // 2
+    heads = H
 
     def head_spec(n, m):
         return pl.BlockSpec((1, heads, n, m), lambda r, g, swaps, at: (r, g, 0, 0))

time: 63.7 us -> 63.3 us (level)
    ppermute x25, waiting for transfers between devices: 14.3 us -> 14.9 us  [flip(): return lax.ppermute(x, AXES, pairs)]
  transfers between devices with their start and end apart: 25 -> 25, of which waited for: 9 -> 10; matrix products, arithmetic and copies ran while one was open for 10% -> 10% of each run, Pallas kernels for 18% -> 18%
where the time goes in v6:
time: 63.3 us; the launch traced here: 63.1 us
  starting transfers between devices  24.8 us (39%)
  waiting for transfers between devices  14.9 us (24%)
  Pallas kernels  13 us (21%)
  matrix products  4.49 us (7%)
  local copies, waits for them, and re-layouts  2.86 us (5%)
  other arithmetic  1.89 us (3%)
  between operations  1.08 us (2%)
    ppermute x25, starting transfers between devices, flip(): return lax.ppermute(x, AXES, pairs)  24.8 us
    ppermute x25, waiting for transfers between devices, flip(): return lax.ppermute(x, AXES, pairs)  14.9 us
    pallas_call x2, Pallas kernels, prepare(): pl.pallas_call(functools.partial(fetch_and_prep_kernel if fetched else pr...  6.62 us
    pallas_call x1, Pallas kernels, per_device(): pl.pallas_call(functools.partial(finish_kernel, heads, block_rows, side_c...  3.82 us
    dot_general x2, matrix products, feed(): gate_up = jnp.dot(x[:, :D], first_weight, preferred_element_type=f32)  2.76 us
    unnamed x34, local copies, waits for them, and re-layouts  2.57 us
    pallas_call x1, Pallas kernels, per_device(): pl.pallas_call(functools.partial(rows_kernel, peer_count), out_shape=jax....  1.83 us
    dot_general x2, matrix products, feed(): produced = jnp.dot(activated, down_weight[0], preferred_element_type=f32)  1.73 us
  transfers between devices with their start and end apart: 25, of which 10 were waited for; matrix products, arithmetic and copies ran while one was open for 10% of the time, Pallas kernels for 18%

profile of v6, /device:TPU:0, one launch (start us, length us, event | category | flops | bytes accessed | tf_op | source)
XLA Modules:
  0.0 63.1 jit_solution(5302134076657465673)
XLA Ops:
  0.6 1.8 %rows.1 = bf16[32,2432]{1,0:T(8,128)(2,1)} custom-call(bf16[2,16,2304]{2,1,0:T(8,128)(2,1)} %hidden_ref.1, s32[2,8,16]{2,1,0:T(8,128)} %bitcast.29, f32[2,8,16]{2,1,0:T(8,128)} %bitcast.30), custom_call_target="tpu_custom_call" | custom-call | tf_op jit(solution)/shard_map/rows/pallas_call | solution.py:239
  2.5 5.0 %collective-permute-start = (bf16[32,2432]{1,0:T(8,128)(2,1)}, bf16[32,2432]{1,0:T(8,128)(2,1)S(1)}, u32[]{:S(2)}, u32[]{:S(2)}) collective-permute-start(bf16[32,2432]{1,0:T(8,128)(2,1)} %rows.1), channel_id=1, source_target_pairs={{0,12},{1,13},{2,14},{3,15},{4,8},{5,9},{6,10},{7,11},{8,4},{9,5},... | collective-permute-start | bytes 466952 | tf_op jit(solution)/shard_map/ppermute | solution.py:234
  7.5 1.5 %collective-permute-start.8 = (bf16[32,2432]{1,0:T(8,128)(2,1)}, bf16[32,2432]{1,0:T(8,128)(2,1)S(1)}, u32[]{:S(2)}, u32[]{:S(2)}) collective-permute-start(bf16[32,2432]{1,0:T(8,128)(2,1)} %rows.1), channel_id=1, source_target_pairs={{0,2},{1,3},{2,0},{3,1},{4,6},{5,7},{6,4},{7,5},{8,10},{9,11},{10,... | collective-permute-start | bytes 466952 | tf_op jit(solution)/shard_map/ppermute | solution.py:234
  9.1 1.6 %copy-done.1 = f32[2,16,128,128]{3,2,1,0:T(8,128)S(1)} copy-done((f32[2,16,128,128]{3,2,1,0:T(8,128)S(1)}, f32[2,16,128,128]{3,2,1,0:T(8,128)}, u32[]{:S(2)}) %copy-start.1) | copy-done | bytes 2097176
  11.3 0.8 %pack.1 = (bf16[4,512,128]{2,1,0:T(8,128)(2,1)S(1)}, bf16[4,512,128]{2,1,0:T(8,128)(2,1)S(1)}, bf16[16,128]{1,0:T(8,128)(2,1)S(1)}) custom-call(s32[2,2]{1,0:T(2,128)S(1)} %copy-done.9, s32[1]{0:T(128)} %bitcast.where_at, f32[2,4,512,128]{3,2,1,0:T(8,128)S(1)} %bitcast.25, f32[2,4,512,128]{3,2,1,0:T(8,128)S(1)} %bitcast.26), custom_call_target="tpu_custom_call" | custom-call | tf_op jit(solution)/shard_map/pack/pallas_call | solution.py:270
  12.3 0.9 %collective-permute-done.8 = bf16[32,2432]{1,0:T(8,128)(2,1)S(1)} collective-permute-done((bf16[32,2432]{1,0:T(8,128)(2,1)}, bf16[32,2432]{1,0:T(8,128)(2,1)S(1)}, u32[]{:S(2)}, u32[]{:S(2)}) %collective-permute-start.8) | collective-permute-done | bytes 155680 | tf_op jit(solution)/shard_map/ppermute | solution.py:234
  13.2 1.2 %collective-permute-start.9 = (bf16[32,2432]{1,0:T(8,128)(2,1)S(1)}, bf16[32,2432]{1,0:T(8,128)(2,1)S(1)}, u32[]{:S(2)}, u32[]{:S(2)}) collective-permute-start(bf16[32,2432]{1,0:T(8,128)(2,1)S(1)} %collective-permute-done.8), channel_id=1, source_target_pairs={{0,4},{1,5},{2,6},{3,7},{4,0},{5,1},{6,2},{7,3},{8,12},{9,13},{10,... | collective-permute-start | bytes 466952 | tf_op jit(solution)/shard_map/ppermute | solution.py:234
  14.5 1.7 %collective-permute-start.4 = (bf16[32,2432]{1,0:T(8,128)(2,1)S(1)}, bf16[32,2432]{1,0:T(8,128)(2,1)S(1)}, u32[]{:S(2)}, u32[]{:S(2)}) collective-permute-start(bf16[32,2432]{1,0:T(8,128)(2,1)S(1)} %collective-permute-done), channel_id=1, source_target_pairs={{0,4},{1,5},{2,6},{3,7},{4,0},{5,1},{6,2},{7,3},{8,12},{9,13},{10,... | collective-permute-start | bytes 466952 | tf_op jit(solution)/shard_map/ppermute | solution.py:234
  16.2 0.8 %collective-permute-start.3 = (bf16[32,2432]{1,0:T(8,128)(2,1)S(1)}, bf16[32,2432]{1,0:T(8,128)(2,1)S(1)}, u32[]{:S(2)}, u32[]{:S(2)}) collective-permute-start(bf16[32,2432]{1,0:T(8,128)(2,1)S(1)} %collective-permute-done), channel_id=1, source_target_pairs={{0,2},{1,3},{2,0},{3,1},{4,6},{5,7},{6,4},{7,5},{8,10},{9,11},{10,... | collective-permute-start | bytes 466952 | tf_op jit(solution)/shard_map/ppermute | solution.py:234
  17.0 1.3 %collective-permute-start.2 = (bf16[2,512,128]{2,1,0:T(8,128)(2,1)S(1)}, bf16[2,512,128]{2,1,0:T(8,128)(2,1)S(1)}, u32[]{:S(2)}, u32[]{:S(2)}) collective-permute-start(bf16[2,512,128]{2,1,0:T(8,128)(2,1)S(1)} %slice.109), channel_id=1, source_target_pairs={{0,2},{1,3},{2,0},{3,1},{4,6},{5,7},{6,4},{7,5},{8,10},{9,11},{10,... | collective-permute-start | bytes 786440 | tf_op jit(solution)/shard_map/ppermute | solution.py:234
  18.4 3.1 %prep0.1 = (bf16[2,16,64,128]{3,2,1,0:T(8,128)(2,1)S(1)}, f32[2,16,32,128]{3,2,1,0:T(8,128)S(1)}, bf16[2,16,48,128]{3,2,1,0:T(8,128)(2,1)S(1)}, f32[2,16,8,128]{3,2,1,0:T(8,128)S(1)}) custom-call(s32[2]{0:T(128)S(1)} %copy-done.11, bf16[2,16,2048]{2,1,0:T(8,128)(2,1)S(1)} %copy-done.5, bf16[2,16,2048]{2,1,0:T(8,128)(2,1)S(1)} %copy-done.6, ...), custom_call_target="tpu_custom_call" | custom-call | tf_op jit(solution)/shard_map/prep0/pallas_call | solution.py:295
  21.6 0.8 %collective-permute-done.4 = bf16[32,2432]{1,0:T(8,128)(2,1)S(1)} collective-permute-done((bf16[32,2432]{1,0:T(8,128)(2,1)S(1)}, bf16[32,2432]{1,0:T(8,128)(2,1)S(1)}, u32[]{:S(2)}, u32[]{:S(2)}) %collective-permute-start.4) | collective-permute-done | bytes 155680 | tf_op jit(solution)/shard_map/ppermute | solution.py:234
  22.3 1.1 %collective-permute-start.10 = (bf16[32,2432]{1,0:T(8,128)(2,1)S(1)}, bf16[32,2432]{1,0:T(8,128)(2,1)S(1)}, u32[]{:S(2)}, u32[]{:S(2)}) collective-permute-start(bf16[32,2432]{1,0:T(8,128)(2,1)S(1)} %collective-permute-done.4), channel_id=1, source_target_pairs={{0,2},{1,3},{2,0},{3,1},{4,6},{5,7},{6,4},{7,5},{8,10},{9,11},{10,... | collective-permute-start | bytes 466952 | tf_op jit(solution)/shard_map/ppermute | solution.py:234
  23.6 3.5 %prep1.1 = (bf16[2,16,64,128]{3,2,1,0:T(8,128)(2,1)S(1)}, f32[2,16,32,128]{3,2,1,0:T(8,128)S(1)}, bf16[2,16,48,128]{3,2,1,0:T(8,128)(2,1)S(1)}, f32[2,16,8,128]{3,2,1,0:T(8,128)S(1)}, bf16[2304,1024]{1,0:T(8,128)(2,1)S(1)}) custom-call(s32[2]{0:T(128)S(1)} %copy-done.11, ...), custom_call_target="tpu_custom_call", output_to_operand_aliasing={{0}: (7, {}), {1}: (8, {}), {2}: (9, {}), {3}: (10, {})} | custom-call | tf_op jit(solution)/shard_map/prep1/pallas_call | solution.py:295
  27.2 1.6 %collective-permute-done.2 = bf16[2,512,128]{2,1,0:T(8,128)(2,1)S(1)} collective-permute-done((bf16[2,512,128]{2,1,0:T(8,128)(2,1)S(1)}, bf16[2,512,128]{2,1,0:T(8,128)(2,1)S(1)}, u32[]{:S(2)}, u32[]{:S(2)}) %collective-permute-start.2) | collective-permute-done | bytes 262176 | tf_op jit(solution)/shard_map/ppermute | solution.py:234
  29.3 1.7 %collective-permute-done.10 = bf16[32,2432]{1,0:T(8,128)(2,1)S(1)} collective-permute-done((bf16[32,2432]{1,0:T(8,128)(2,1)S(1)}, bf16[32,2432]{1,0:T(8,128)(2,1)S(1)}, u32[]{:S(2)}, u32[]{:S(2)}) %collective-permute-start.10) | collective-permute-done | bytes 155680 | tf_op jit(solution)/shard_map/ppermute | solution.py:234
  31.2 1.4 %fusion.6 = f32[256,1024]{1,0:T(8,128)S(1)} fusion(bf16[2304,1024]{1,0:T(8,128)(2,1)S(1)} %get-tuple-element.59, bf16[256,2432]{1,0:T(8,128)(2,1)S(1)} %constant_dynamic-update-slice_fusion), kind=kOutput, calls=%fused_computation.10 | convolution fusion | flops 1207959552 | bytes 6946816 | tf_op jit(solution)/shard_map/dot_general | solution.py:354
  32.8 0.9 %fusion = bf16[256,2304]{1,0:T(8,128)(2,1)S(1)} fusion(bf16[1,512,2304]{2,1,0:T(8,128)(2,1)S(1)} %copy-done, f32[256]{0:T(256)S(1)} %fusion.23, f32[256,1024]{1,0:T(8,128)S(1)} %fusion.6), kind=kOutput, calls=%fused_computation.2 | convolution fusion | flops 605945856 | bytes 4588544 | tf_op jit(solution)/shard_map/dot_general | solution.py:356
  34.3 0.9 %collective-permute-start.11 = (bf16[1,512,128]{2,1,0:T(8,128)(2,1)S(1)}, bf16[1,512,128]{2,1,0:T(8,128)(2,1)S(1)}, u32[]{:S(2)}, u32[]{:S(2)}) collective-permute-start(bf16[1,512,128]{2,1,0:T(8,128)(2,1)S(1)} %broadcast_select_fusion.5), channel_id=1, source_target_pairs={{0,12},{1,13},{2,14},{3,15},{4,8},{5,9},{6,10},{7,11},{8,4},{9,5},... | collective-permute-start | bytes 393224 | tf_op jit(solution)/shard_map/ppermute | solution.py:234
  35.2 1.4 %fusion.4 = f32[256,1024]{1,0:T(8,128)S(1)} fusion(bf16[2304,1024]{1,0:T(8,128)(2,1)S(1)} %get-tuple-element.59, bf16[256,2432]{1,0:T(8,128)(2,1)S(1)} %constant_dynamic-update-slice_fusion.9), kind=kOutput, calls=%fused_computation.8 | convolution fusion | flops 1207959552 | bytes 6946816 | tf_op jit(solution)/shard_map/dot_general | solution.py:354
  36.8 0.9 %fusion.1 = bf16[256,2304]{1,0:T(8,128)(2,1)S(1)} fusion(bf16[1,512,2304]{2,1,0:T(8,128)(2,1)S(1)} %copy-done, f32[256]{0:T(256)S(1)} %fusion.21, f32[256,1024]{1,0:T(8,128)S(1)} %fusion.4), kind=kOutput, calls=%fused_computation.3 | convolution fusion | flops 605945856 | bytes 4588544 | tf_op jit(solution)/shard_map/dot_general | solution.py:356
  38.0 1.7 %collective-permute-done.13 = bf16[128,2304]{1,0:T(8,128)(2,1)S(1)} collective-permute-done((bf16[128,2304]{1,0:T(8,128)(2,1)S(1)}, bf16[128,2304]{1,0:T(8,128)(2,1)S(1)}, u32[]{:S(2)}, u32[]{:S(2)}) %collective-permute-start.13) | collective-permute-done | bytes 589856 | tf_op jit(solution)/shard_map/ppermute | solution.py:234
  40.0 1.6 %collective-permute-start.19 = (bf16[32,2304]{1,0:T(8,128)(2,1)S(1)}, bf16[32,2304]{1,0:T(8,128)(2,1)S(1)}, u32[]{:S(2)}, u32[]{:S(2)}) collective-permute-start(bf16[32,2304]{1,0:T(8,128)(2,1)S(1)} %get-tuple-element.72), channel_id=1, source_target_pairs={{0,2},{1,3},{2,0},{3,1},{4,6},{5,7},{6,4},{7,5},{8,10},{9,11},{10,... | collective-permute-start | bytes 442376 | tf_op jit(solution)/shard_map/ppermute | solution.py:234
  42.1 1.0 %collective-permute-start.14 = (bf16[1,512,128]{2,1,0:T(8,128)(2,1)S(1)}, bf16[1,512,128]{2,1,0:T(8,128)(2,1)S(1)}, u32[]{:S(2)}, u32[]{:S(2)}) collective-permute-start(bf16[1,512,128]{2,1,0:T(8,128)(2,1)S(1)} %get-tuple-element.86), channel_id=1, source_target_pairs={{0,4},{1,5},{2,6},{3,7},{4,0},{5,1},{6,2},{7,3},{8,12},{9,13},{10,... | collective-permute-start | bytes 393224 | tf_op jit(solution)/shard_map/ppermute | solution.py:234
  43.1 3.7 %collective-permute-done.19 = bf16[32,2304]{1,0:T(8,128)(2,1)S(1)} collective-permute-done((bf16[32,2304]{1,0:T(8,128)(2,1)S(1)}, bf16[32,2304]{1,0:T(8,128)(2,1)S(1)}, u32[]{:S(2)}, u32[]{:S(2)}) %collective-permute-start.19) | collective-permute-done | bytes 147488 | tf_op jit(solution)/shard_map/ppermute | solution.py:234
  47.7 1.1 %collective-permute-start.15 = (bf16[2,512,128]{2,1,0:T(8,128)(2,1)S(1)}, bf16[2,512,128]{2,1,0:T(8,128)(2,1)S(1)}, u32[]{:S(2)}, u32[]{:S(2)}) collective-permute-start(bf16[2,512,128]{2,1,0:T(8,128)(2,1)S(1)} %get-tuple-element.76), channel_id=1, source_target_pairs={{0,2},{1,3},{2,0},{3,1},{4,6},{5,7},{6,4},{7,5},{8,10},{9,11},{10,... | collective-permute-start | bytes 786440 | tf_op jit(solution)/shard_map/ppermute | solution.py:234
  48.8 1.8 %collective-permute-start.20 = (bf16[32,2304]{1,0:T(8,128)(2,1)S(1)}, bf16[32,2304]{1,0:T(8,128)(2,1)S(1)}, u32[]{:S(2)}, u32[]{:S(2)}) collective-permute-start(bf16[32,2304]{1,0:T(8,128)(2,1)S(1)} %slice.137), channel_id=1, source_target_pairs={{0,4},{1,5},{2,6},{3,7},{4,0},{5,1},{6,2},{7,3},{8,12},{9,13},{10,... | collective-permute-start | bytes 442376 | tf_op jit(solution)/shard_map/ppermute | solution.py:234
  50.6 2.4 %collective-permute-done.23 = bf16[32,2304]{1,0:T(8,128)(2,1)S(1)} collective-permute-done((bf16[32,2304]{1,0:T(8,128)(2,1)S(1)}, bf16[32,2304]{1,0:T(8,128)(2,1)S(1)}, u32[]{:S(2)}, u32[]{:S(2)}) %collective-permute-start.23) | collective-permute-done | bytes 147488 | tf_op jit(solution)/shard_map/ppermute | solution.py:234
  53.1 2.7 %collective-permute-start.24 = (bf16[32,2304]{1,0:T(8,128)(2,1)S(1)}, bf16[32,2304]{1,0:T(8,128)(2,1)S(1)}, u32[]{:S(2)}, u32[]{:S(2)}) collective-permute-start(bf16[32,2304]{1,0:T(8,128)(2,1)S(1)} %fusion.12), channel_id=1, source_target_pairs={{0,12},{1,13},{2,14},{3,15},{4,8},{5,9},{6,10},{7,11},{8,4},{9,5},... | collective-permute-start | bytes 442376 | tf_op jit(solution)/shard_map/ppermute | solution.py:234
  56.0 1.0 %collective-permute-start.21 = (bf16[32,2304]{1,0:T(8,128)(2,1)S(1)}, bf16[32,2304]{1,0:T(8,128)(2,1)S(1)}, u32[]{:S(2)}, u32[]{:S(2)}) collective-permute-start(bf16[32,2304]{1,0:T(8,128)(2,1)S(1)} %add_convert_fusion.1), channel_id=1, source_target_pairs={{0,2},{1,3},{2,0},{3,1},{4,6},{5,7},{6,4},{7,5},{8,10},{9,11},{10,... | collective-permute-start | bytes 442376 | tf_op jit(solution)/shard_map/ppermute | solution.py:234
  57.0 0.9 %collective-permute-done.16.other = bf16[4,512,128]{2,1,0:T(8,128)(2,1)S(1)} collective-permute-done((bf16[4,512,128]{2,1,0:T(8,128)(2,1)S(1)}, bf16[4,512,128]{2,1,0:T(8,128)(2,1)S(1)}, u32[]{:S(2)}, u32[]{:S(2)}) %collective-permute-start.16) | collective-permute-done | bytes 524320 | tf_op jit(solution)/shard_map/ppermute | solution.py:234
  57.9 3.8 %finish.1 = (f32[2,16,128,128]{3,2,1,0:T(8,128)}, bf16[2,16,2048]{2,1,0:T(8,128)(2,1)}) custom-call(s32[2,2]{1,0:T(2,128)S(1)} %copy-done.10, s32[1]{0:T(128)} %bitcast.where_at, f32[2,16,128,128]{3,2,1,0:T(8,128)S(1)} %copy-done.2, bf16[4,512,128]{2,1,0:T(8,128)(2,1)S(1)} %get-tuple-element.74.mine, bf16[4,512,128]{2,1,0:T(8,128)(2,1)S(1)} %collective-permute-done.1.near, ...), custom_call_target="tpu_custom_call" | custom-call | tf_op jit(solution)/shard_map/finish/pallas_call | solution.py:423
  (89 shorter events, 6.6 us)
Async XLA Ops:
  0.6 32.1 %copy-start = (bf16[1,512,2304]{2,1,0:T(8,128)(2,1)S(1)}, bf16[1,512,2304]{2,1,0:T(8,128)(2,1)}, u32[]{:S(2)}) copy-start(bf16[1,512,2304]{2,1,0:T(8,128)(2,1)} %param.25) | copy-start | bytes 7077892
  2.5 12.1 %collective-permute-start = (bf16[32,2432]{1,0:T(8,128)(2,1)}, bf16[32,2432]{1,0:T(8,128)(2,1)S(1)}, u32[]{:S(2)}, u32[]{:S(2)}) collective-permute-start(bf16[32,2432]{1,0:T(8,128)(2,1)} %rows.1), channel_id=1, source_target_pairs={{0,12},{1,13},{2,14},{3,15},{4,8},{5,9},{6,10},{7,11},{8,4},{9,5},... | collective-permute-start | bytes 466952 | tf_op jit(solution)/shard_map/ppermute | solution.py:234
  7.5 5.7 %collective-permute-start.8 = (bf16[32,2432]{1,0:T(8,128)(2,1)}, bf16[32,2432]{1,0:T(8,128)(2,1)S(1)}, u32[]{:S(2)}, u32[]{:S(2)}) collective-permute-start(bf16[32,2432]{1,0:T(8,128)(2,1)} %rows.1), channel_id=1, source_target_pairs={{0,2},{1,3},{2,0},{3,1},{4,6},{5,7},{6,4},{7,5},{8,10},{9,11},{10,... | collective-permute-start | bytes 466952 | tf_op jit(solution)/shard_map/ppermute | solution.py:234
  9.0 9.3 %collective-permute-start.6 = (bf16[32,2432]{1,0:T(8,128)(2,1)}, bf16[32,2432]{1,0:T(8,128)(2,1)S(1)}, u32[]{:S(2)}, u32[]{:S(2)}) collective-permute-start(bf16[32,2432]{1,0:T(8,128)(2,1)} %rows.1), channel_id=1, source_target_pairs={{0,4},{1,5},{2,6},{3,7},{4,0},{5,1},{6,2},{7,3},{8,12},{9,13},{10,... | collective-permute-start | bytes 466952 | tf_op jit(solution)/shard_map/ppermute | solution.py:234
  12.1 2.3 %collective-permute-start.1 = (bf16[4,512,128]{2,1,0:T(8,128)(2,1)S(1)}, bf16[4,512,128]{2,1,0:T(8,128)(2,1)S(1)}, u32[]{:S(2)}, u32[]{:S(2)}) collective-permute-start(bf16[4,512,128]{2,1,0:T(8,128)(2,1)S(1)} %get-tuple-element.39), channel_id=1, source_target_pairs={{0,1},{1,0},{2,3},{3,2},{4,5},{5,4},{6,7},{7,6},{8,9},{9,8},{10,11... | collective-permute-start | bytes 1572872 | tf_op jit(solution)/shard_map/ppermute | solution.py:234
  13.2 10.3 %collective-permute-start.9 = (bf16[32,2432]{1,0:T(8,128)(2,1)S(1)}, bf16[32,2432]{1,0:T(8,128)(2,1)S(1)}, u32[]{:S(2)}, u32[]{:S(2)}) collective-permute-start(bf16[32,2432]{1,0:T(8,128)(2,1)S(1)} %collective-permute-done.8), channel_id=1, source_target_pairs={{0,4},{1,5},{2,6},{3,7},{4,0},{5,1},{6,2},{7,3},{8,12},{9,13},{10,... | collective-permute-start | bytes 466952 | tf_op jit(solution)/shard_map/ppermute | solution.py:234
  14.4 4.0 %copy-start.5 = (bf16[2,16,2048]{2,1,0:T(8,128)(2,1)S(1)}, bf16[2,16,2048]{2,1,0:T(8,128)(2,1)}, u32[]{:S(2)}) copy-start(bf16[2,16,2048]{2,1,0:T(8,128)(2,1)} %refs_0_.1) | copy-start | bytes 393220
  14.4 4.0 %copy-start.6 = (bf16[2,16,2048]{2,1,0:T(8,128)(2,1)S(1)}, bf16[2,16,2048]{2,1,0:T(8,128)(2,1)}, u32[]{:S(2)}) copy-start(bf16[2,16,2048]{2,1,0:T(8,128)(2,1)} %refs_1_.1) | copy-start | bytes 393220
  14.4 4.0 %copy-start.7 = (bf16[2,16,2048]{2,1,0:T(8,128)(2,1)S(1)}, bf16[2,16,2048]{2,1,0:T(8,128)(2,1)}, u32[]{:S(2)}) copy-start(bf16[2,16,2048]{2,1,0:T(8,128)(2,1)} %refs_2_.1) | copy-start | bytes 393220
  14.4 4.0 %copy-start.8 = (f32[2,16,16]{2,1,0:T(8,128)S(1)}, f32[2,16,16]{2,1,0:T(8,128)}, u32[]{:S(2)}) copy-start(f32[2,16,16]{2,1,0:T(8,128)} %refs_4_.1) | copy-start | bytes 6148
  14.4 4.0 %copy-start.11 = (s32[2]{0:T(128)S(1)}, s32[2]{0:T(128)}, u32[]{:S(2)}) copy-start(s32[2]{0:T(128)} %counts.1) | copy-start | bytes 28
  14.5 9.2 %copy-start.3 = (bf16[1,2304,1024]{2,1,0:T(8,128)(2,1)S(1)}, bf16[1,2304,1024]{2,1,0:T(8,128)(2,1)}, u32[]{:S(2)}) copy-start(bf16[1,2304,1024]{2,1,0:T(8,128)(2,1)} %param.24) | copy-start | bytes 14155780
  14.5 7.8 %collective-permute-start.4 = (bf16[32,2432]{1,0:T(8,128)(2,1)S(1)}, bf16[32,2432]{1,0:T(8,128)(2,1)S(1)}, u32[]{:S(2)}, u32[]{:S(2)}) collective-permute-start(bf16[32,2432]{1,0:T(8,128)(2,1)S(1)} %collective-permute-done), channel_id=1, source_target_pairs={{0,4},{1,5},{2,6},{3,7},{4,0},{5,1},{6,2},{7,3},{8,12},{9,13},{10,... | collective-permute-start | bytes 466952 | tf_op jit(solution)/shard_map/ppermute | solution.py:234
  16.2 7.3 %collective-permute-start.3 = (bf16[32,2432]{1,0:T(8,128)(2,1)S(1)}, bf16[32,2432]{1,0:T(8,128)(2,1)S(1)}, u32[]{:S(2)}, u32[]{:S(2)}) collective-permute-start(bf16[32,2432]{1,0:T(8,128)(2,1)S(1)} %collective-permute-done), channel_id=1, source_target_pairs={{0,2},{1,3},{2,0},{3,1},{4,6},{5,7},{6,4},{7,5},{8,10},{9,11},{10,... | collective-permute-start | bytes 466952 | tf_op jit(solution)/shard_map/ppermute | solution.py:234
  17.0 11.7 %collective-permute-start.2 = (bf16[2,512,128]{2,1,0:T(8,128)(2,1)S(1)}, bf16[2,512,128]{2,1,0:T(8,128)(2,1)S(1)}, u32[]{:S(2)}, u32[]{:S(2)}) collective-permute-start(bf16[2,512,128]{2,1,0:T(8,128)(2,1)S(1)} %slice.109), channel_id=1, source_target_pairs={{0,2},{1,3},{2,0},{3,1},{4,6},{5,7},{6,4},{7,5},{8,10},{9,11},{10,... | collective-permute-start | bytes 786440 | tf_op jit(solution)/shard_map/ppermute | solution.py:234
  22.3 8.6 %collective-permute-start.10 = (bf16[32,2432]{1,0:T(8,128)(2,1)S(1)}, bf16[32,2432]{1,0:T(8,128)(2,1)S(1)}, u32[]{:S(2)}, u32[]{:S(2)}) collective-permute-start(bf16[32,2432]{1,0:T(8,128)(2,1)S(1)} %collective-permute-done.4), channel_id=1, source_target_pairs={{0,2},{1,3},{2,0},{3,1},{4,6},{5,7},{6,4},{7,5},{8,10},{9,11},{10,... | collective-permute-start | bytes 466952 | tf_op jit(solution)/shard_map/ppermute | solution.py:234
  23.4 7.6 %collective-permute-start.7 = (bf16[128,2432]{1,0:T(8,128)(2,1)S(1)}, bf16[128,2432]{1,0:T(8,128)(2,1)S(1)}, u32[]{:S(2)}, u32[]{:S(2)}) collective-permute-start(bf16[128,2432]{1,0:T(8,128)(2,1)S(1)} %pad_maximum_fusion), channel_id=1, source_target_pairs={{0,1},{1,0},{2,3},{3,2},{4,5},{5,4},{6,7},{7,6},{8,9},{9,8},{10,11... | collective-permute-start | bytes 1867784 | tf_op jit(solution)/shard_map/ppermute | solution.py:234
  28.8 5.4 %collective-permute-start.5 = (bf16[1,512,128]{2,1,0:T(8,128)(2,1)S(1)}, bf16[1,512,128]{2,1,0:T(8,128)(2,1)S(1)}, u32[]{:S(2)}, u32[]{:S(2)}) collective-permute-start(bf16[1,512,128]{2,1,0:T(8,128)(2,1)S(1)} %slice.141), channel_id=1, source_target_pairs={{0,4},{1,5},{2,6},{3,7},{4,0},{5,1},{6,2},{7,3},{8,12},{9,13},{10,... | collective-permute-start | bytes 393224 | tf_op jit(solution)/shard_map/ppermute | solution.py:234
  31.0 4.1 %collective-permute-start.12 = (bf16[128,2432]{1,0:T(8,128)(2,1)S(1)}, bf16[128,2432]{1,0:T(8,128)(2,1)S(1)}, u32[]{:S(2)}, u32[]{:S(2)}) collective-permute-start(bf16[128,2432]{1,0:T(8,128)(2,1)S(1)} %get-tuple-element.78), channel_id=1, source_target_pairs={{0,1},{1,0},{2,3},{3,2},{4,5},{5,4},{6,7},{7,6},{8,9},{9,8},{10,11... | collective-permute-start | bytes 1867784 | tf_op jit(solution)/shard_map/ppermute | solution.py:234
  33.7 4.1 %collective-permute-start.17 = (bf16[128,2304]{1,0:T(8,128)(2,1)S(1)}, bf16[128,2304]{1,0:T(8,128)(2,1)S(1)}, u32[]{:S(2)}, u32[]{:S(2)}) collective-permute-start(bf16[128,2304]{1,0:T(8,128)(2,1)S(1)} %slice.154), channel_id=1, source_target_pairs={{0,1},{1,0},{2,3},{3,2},{4,5},{5,4},{6,7},{7,6},{8,9},{9,8},{10,11... | collective-permute-start | bytes 1769480 | tf_op jit(solution)/shard_map/ppermute | solution.py:234
  34.3 7.8 %collective-permute-start.11 = (bf16[1,512,128]{2,1,0:T(8,128)(2,1)S(1)}, bf16[1,512,128]{2,1,0:T(8,128)(2,1)S(1)}, u32[]{:S(2)}, u32[]{:S(2)}) collective-permute-start(bf16[1,512,128]{2,1,0:T(8,128)(2,1)S(1)} %broadcast_select_fusion.5), channel_id=1, source_target_pairs={{0,12},{1,13},{2,14},{3,15},{4,8},{5,9},{6,10},{7,11},{8,4},{9,5},... | collective-permute-start | bytes 393224 | tf_op jit(solution)/shard_map/ppermute | solution.py:234
  37.7 2.1 %collective-permute-start.13 = (bf16[128,2304]{1,0:T(8,128)(2,1)S(1)}, bf16[128,2304]{1,0:T(8,128)(2,1)S(1)}, u32[]{:S(2)}, u32[]{:S(2)}) collective-permute-start(bf16[128,2304]{1,0:T(8,128)(2,1)S(1)} %slice.152), channel_id=1, source_target_pairs={{0,1},{1,0},{2,3},{3,2},{4,5},{5,4},{6,7},{7,6},{8,9},{9,8},{10,11... | collective-permute-start | bytes 1769480 | tf_op jit(solution)/shard_map/ppermute | solution.py:234
  37.9 23.8 %collective-permute-start.18 = (bf16[32,2304]{1,0:T(8,128)(2,1)S(1)}, bf16[32,2304]{1,0:T(8,128)(2,1)S(1)}, u32[]{:S(2)}, u32[]{:S(2)}) collective-permute-start(bf16[32,2304]{1,0:T(8,128)(2,1)S(1)} %slice.220), channel_id=1, source_target_pairs={{0,4},{1,5},{2,6},{3,7},{4,0},{5,1},{6,2},{7,3},{8,12},{9,13},{10,... | collective-permute-start | bytes 442376 | tf_op jit(solution)/shard_map/ppermute | solution.py:234
  40.0 6.8 %collective-permute-start.19 = (bf16[32,2304]{1,0:T(8,128)(2,1)S(1)}, bf16[32,2304]{1,0:T(8,128)(2,1)S(1)}, u32[]{:S(2)}, u32[]{:S(2)}) collective-permute-start(bf16[32,2304]{1,0:T(8,128)(2,1)S(1)} %get-tuple-element.72), channel_id=1, source_target_pairs={{0,2},{1,3},{2,0},{3,1},{4,6},{5,7},{6,4},{7,5},{8,10},{9,11},{10,... | collective-permute-start | bytes 442376 | tf_op jit(solution)/shard_map/ppermute | solution.py:234
  41.6 9.0 %collective-permute-start.22 = (bf16[32,2304]{1,0:T(8,128)(2,1)S(1)}, bf16[32,2304]{1,0:T(8,128)(2,1)S(1)}, u32[]{:S(2)}, u32[]{:S(2)}) collective-permute-start(bf16[32,2304]{1,0:T(8,128)(2,1)S(1)} %get-tuple-element.71), channel_id=1, source_target_pairs={{0,2},{1,3},{2,0},{3,1},{4,6},{5,7},{6,4},{7,5},{8,10},{9,11},{10,... | collective-permute-start | bytes 442376 | tf_op jit(solution)/shard_map/ppermute | solution.py:234
  42.1 5.5 %collective-permute-start.14 = (bf16[1,512,128]{2,1,0:T(8,128)(2,1)S(1)}, bf16[1,512,128]{2,1,0:T(8,128)(2,1)S(1)}, u32[]{:S(2)}, u32[]{:S(2)}) collective-permute-start(bf16[1,512,128]{2,1,0:T(8,128)(2,1)S(1)} %get-tuple-element.86), channel_id=1, source_target_pairs={{0,4},{1,5},{2,6},{3,7},{4,0},{5,1},{6,2},{7,3},{8,12},{9,13},{10,... | collective-permute-start | bytes 393224 | tf_op jit(solution)/shard_map/ppermute | solution.py:234
  46.8 6.3 %collective-permute-start.23 = (bf16[32,2304]{1,0:T(8,128)(2,1)S(1)}, bf16[32,2304]{1,0:T(8,128)(2,1)S(1)}, u32[]{:S(2)}, u32[]{:S(2)}) collective-permute-start(bf16[32,2304]{1,0:T(8,128)(2,1)S(1)} %fusion.10), channel_id=1, source_target_pairs={{0,4},{1,5},{2,6},{3,7},{4,0},{5,1},{6,2},{7,3},{8,12},{9,13},{10,... | collective-permute-start | bytes 442376 | tf_op jit(solution)/shard_map/ppermute | solution.py:234
  47.7 8.1 %collective-permute-start.15 = (bf16[2,512,128]{2,1,0:T(8,128)(2,1)S(1)}, bf16[2,512,128]{2,1,0:T(8,128)(2,1)S(1)}, u32[]{:S(2)}, u32[]{:S(2)}) collective-permute-start(bf16[2,512,128]{2,1,0:T(8,128)(2,1)S(1)} %get-tuple-element.76), channel_id=1, source_target_pairs={{0,2},{1,3},{2,0},{3,1},{4,6},{5,7},{6,4},{7,5},{8,10},{9,11},{10,... | collective-permute-start | bytes 786440 | tf_op jit(solution)/shard_map/ppermute | solution.py:234
  48.8 7.2 %collective-permute-start.20 = (bf16[32,2304]{1,0:T(8,128)(2,1)S(1)}, bf16[32,2304]{1,0:T(8,128)(2,1)S(1)}, u32[]{:S(2)}, u32[]{:S(2)}) collective-permute-start(bf16[32,2304]{1,0:T(8,128)(2,1)S(1)} %slice.137), channel_id=1, source_target_pairs={{0,4},{1,5},{2,6},{3,7},{4,0},{5,1},{6,2},{7,3},{8,12},{9,13},{10,... | collective-permute-start | bytes 442376 | tf_op jit(solution)/shard_map/ppermute | solution.py:234
  53.1 8.6 %collective-permute-start.24 = (bf16[32,2304]{1,0:T(8,128)(2,1)S(1)}, bf16[32,2304]{1,0:T(8,128)(2,1)S(1)}, u32[]{:S(2)}, u32[]{:S(2)}) collective-permute-start(bf16[32,2304]{1,0:T(8,128)(2,1)S(1)} %fusion.12), channel_id=1, source_target_pairs={{0,12},{1,13},{2,14},{3,15},{4,8},{5,9},{6,10},{7,11},{8,4},{9,5},... | collective-permute-start | bytes 442376 | tf_op jit(solution)/shard_map/ppermute | solution.py:234
  55.9 2.0 %collective-permute-start.16 = (bf16[4,512,128]{2,1,0:T(8,128)(2,1)S(1)}, bf16[4,512,128]{2,1,0:T(8,128)(2,1)S(1)}, u32[]{:S(2)}, u32[]{:S(2)}) collective-permute-start(bf16[4,512,128]{2,1,0:T(8,128)(2,1)S(1)} %get-tuple-element.73), channel_id=1, source_target_pairs={{0,1},{1,0},{2,3},{3,2},{4,5},{5,4},{6,7},{7,6},{8,9},{9,8},{10,11... | collective-permute-start | bytes 1572872 | tf_op jit(solution)/shard_map/ppermute | solution.py:234
  56.0 6.3 %collective-permute-start.21 = (bf16[32,2304]{1,0:T(8,128)(2,1)S(1)}, bf16[32,2304]{1,0:T(8,128)(2,1)S(1)}, u32[]{:S(2)}, u32[]{:S(2)}) collective-permute-start(bf16[32,2304]{1,0:T(8,128)(2,1)S(1)} %add_convert_fusion.1), channel_id=1, source_target_pairs={{0,2},{1,3},{2,0},{3,1},{4,6},{5,7},{6,4},{7,5},{8,10},{9,11},{10,... | collective-permute-start | bytes 442376 | tf_op jit(solution)/shard_map/ppermute | solution.py:234
  (6 other events, 11.4 us)

commit v7 on v6

--- a/solution.py
+++ b/solution.py
@@ -259,20 +259,19 @@
             pair = pair if own else 1 - pair
             one, two = swaps[pair, 0], swaps[pair, 1]
             held = jnp.where(lax.div(one, local_reqs) == at[0], one, two)
-            across_at = jnp.bitwise_and(lax.div(at[0], side_count), 1)
-            return (lax.rem(held, local_reqs), jnp.bitwise_xor(g, across_at), 0, 0)
-
-        return pl.BlockSpec((1, blocks // 2, block_rows, DV), index)
+            return (lax.rem(held, local_reqs), 0, 0, 0)
+
+        return pl.BlockSpec((1, blocks, block_rows, DV), index)
 
     packed = jax.ShapeDtypeStruct((blocks, block_rows, DV), bf16)
-    out_spec = pl.BlockSpec((blocks // 2, block_rows, DV), lambda g, swaps, at: (g, 0, 0))
+    out_spec = pl.BlockSpec((blocks, block_rows, DV), lambda g, swaps, at: (g, 0, 0))
     state_blocks = states.reshape(local_reqs, blocks, block_rows, DV)
     send, keep, plan = pl.pallas_call(
         functools.partial(pack_kernel, side_count, local_reqs, levels),
         out_shape=(packed, packed, jax.ShapeDtypeStruct((16, DV), bf16)),
         grid_spec=pltpu.PrefetchScalarGridSpec(
             num_scalar_prefetch=2,
-            grid=(2,),
+            grid=(1,),
             in_specs=[state_spec(False), state_spec(True)],
             out_specs=[out_spec, out_spec, pl.BlockSpec((16, DV), lambda g, swaps, at: (0, 0))],
         ),

time: 63.3 us -> 63.2 us (level)
  no operation moved by 1% of the time
where the time goes in v7:
time: 63.2 us; the launch traced here: 63 us
  starting transfers between devices  24.9 us (39%)
  waiting for transfers between devices  14.7 us (23%)
  Pallas kernels  12.9 us (20%)
  matrix products  4.48 us (7%)
  local copies, waits for them, and re-layouts  2.95 us (5%)
  other arithmetic  1.89 us (3%)
  between operations  1.08 us (2%)
    ppermute x25, starting transfers between devices, flip(): return lax.ppermute(x, AXES, pairs)  24.9 us
    ppermute x25, waiting for transfers between devices, flip(): return lax.ppermute(x, AXES, pairs)  14.7 us
    pallas_call x2, Pallas kernels, prepare(): pl.pallas_call(functools.partial(fetch_and_prep_kernel if fetched else pr...  6.81 us
    pallas_call x1, Pallas kernels, per_device(): pl.pallas_call(functools.partial(finish_kernel, heads, block_rows, side_c...  3.64 us
    dot_general x2, matrix products, feed(): gate_up = jnp.dot(x[:, :D], first_weight, preferred_element_type=f32)  2.76 us
    unnamed x34, local copies, waits for them, and re-layouts  2.66 us
    pallas_call x1, Pallas kernels, per_device(): pl.pallas_call(functools.partial(rows_kernel, peer_count), out_shape=jax....  1.83 us
    dot_general x2, matrix products, feed(): produced = jnp.dot(activated, down_weight[0], preferred_element_type=f32)  1.72 us
  transfers between devices with their start and end apart: 25, of which 10 were waited for; matrix products, arithmetic and copies ran while one was open for 10% of the time, Pallas kernels for 18%

profile of v7, /device:TPU:0, one launch (start us, length us, event | category | flops | bytes accessed | tf_op | source)
XLA Modules:
  0.0 63.0 jit_solution(3729990370183669064)
XLA Ops:
  0.6 1.8 %rows.1 = bf16[32,2432]{1,0:T(8,128)(2,1)} custom-call(bf16[2,16,2304]{2,1,0:T(8,128)(2,1)} %hidden_ref.1, s32[2,8,16]{2,1,0:T(8,128)} %bitcast.29, f32[2,8,16]{2,1,0:T(8,128)} %bitcast.30), custom_call_target="tpu_custom_call" | custom-call | tf_op jit(solution)/shard_map/rows/pallas_call | solution.py:239
  2.5 5.0 %collective-permute-start = (bf16[32,2432]{1,0:T(8,128)(2,1)}, bf16[32,2432]{1,0:T(8,128)(2,1)S(1)}, u32[]{:S(2)}, u32[]{:S(2)}) collective-permute-start(bf16[32,2432]{1,0:T(8,128)(2,1)} %rows.1), channel_id=1, source_target_pairs={{0,12},{1,13},{2,14},{3,15},{4,8},{5,9},{6,10},{7,11},{8,4},{9,5},... | collective-permute-start | bytes 466952 | tf_op jit(solution)/shard_map/ppermute | solution.py:234
  7.5 1.5 %collective-permute-start.8 = (bf16[32,2432]{1,0:T(8,128)(2,1)}, bf16[32,2432]{1,0:T(8,128)(2,1)S(1)}, u32[]{:S(2)}, u32[]{:S(2)}) collective-permute-start(bf16[32,2432]{1,0:T(8,128)(2,1)} %rows.1), channel_id=1, source_target_pairs={{0,2},{1,3},{2,0},{3,1},{4,6},{5,7},{6,4},{7,5},{8,10},{9,11},{10,... | collective-permute-start | bytes 466952 | tf_op jit(solution)/shard_map/ppermute | solution.py:234
  9.1 1.6 %copy-done.1 = f32[2,16,128,128]{3,2,1,0:T(8,128)S(1)} copy-done((f32[2,16,128,128]{3,2,1,0:T(8,128)S(1)}, f32[2,16,128,128]{3,2,1,0:T(8,128)}, u32[]{:S(2)}) %copy-start.1) | copy-done | bytes 2097176
  12.3 0.9 %collective-permute-done.8 = bf16[32,2432]{1,0:T(8,128)(2,1)S(1)} collective-permute-done((bf16[32,2432]{1,0:T(8,128)(2,1)}, bf16[32,2432]{1,0:T(8,128)(2,1)S(1)}, u32[]{:S(2)}, u32[]{:S(2)}) %collective-permute-start.8) | collective-permute-done | bytes 155680 | tf_op jit(solution)/shard_map/ppermute | solution.py:234
  13.2 1.2 %collective-permute-start.9 = (bf16[32,2432]{1,0:T(8,128)(2,1)S(1)}, bf16[32,2432]{1,0:T(8,128)(2,1)S(1)}, u32[]{:S(2)}, u32[]{:S(2)}) collective-permute-start(bf16[32,2432]{1,0:T(8,128)(2,1)S(1)} %collective-permute-done.8), channel_id=1, source_target_pairs={{0,4},{1,5},{2,6},{3,7},{4,0},{5,1},{6,2},{7,3},{8,12},{9,13},{10,... | collective-permute-start | bytes 466952 | tf_op jit(solution)/shard_map/ppermute | solution.py:234
  14.5 1.6 %collective-permute-start.4 = (bf16[32,2432]{1,0:T(8,128)(2,1)S(1)}, bf16[32,2432]{1,0:T(8,128)(2,1)S(1)}, u32[]{:S(2)}, u32[]{:S(2)}) collective-permute-start(bf16[32,2432]{1,0:T(8,128)(2,1)S(1)} %collective-permute-done), channel_id=1, source_target_pairs={{0,4},{1,5},{2,6},{3,7},{4,0},{5,1},{6,2},{7,3},{8,12},{9,13},{10,... | collective-permute-start | bytes 466952 | tf_op jit(solution)/shard_map/ppermute | solution.py:234
  16.1 0.9 %collective-permute-start.3 = (bf16[32,2432]{1,0:T(8,128)(2,1)S(1)}, bf16[32,2432]{1,0:T(8,128)(2,1)S(1)}, u32[]{:S(2)}, u32[]{:S(2)}) collective-permute-start(bf16[32,2432]{1,0:T(8,128)(2,1)S(1)} %collective-permute-done), channel_id=1, source_target_pairs={{0,2},{1,3},{2,0},{3,1},{4,6},{5,7},{6,4},{7,5},{8,10},{9,11},{10,... | collective-permute-start | bytes 466952 | tf_op jit(solution)/shard_map/ppermute | solution.py:234
  17.0 1.2 %collective-permute-start.2 = (bf16[2,512,128]{2,1,0:T(8,128)(2,1)S(1)}, bf16[2,512,128]{2,1,0:T(8,128)(2,1)S(1)}, u32[]{:S(2)}, u32[]{:S(2)}) collective-permute-start(bf16[2,512,128]{2,1,0:T(8,128)(2,1)S(1)} %slice.109), channel_id=1, source_target_pairs={{0,2},{1,3},{2,0},{3,1},{4,6},{5,7},{6,4},{7,5},{8,10},{9,11},{10,... | collective-permute-start | bytes 786440 | tf_op jit(solution)/shard_map/ppermute | solution.py:234
  18.4 3.1 %prep0.1 = (bf16[2,16,64,128]{3,2,1,0:T(8,128)(2,1)S(1)}, f32[2,16,32,128]{3,2,1,0:T(8,128)S(1)}, bf16[2,16,48,128]{3,2,1,0:T(8,128)(2,1)S(1)}, f32[2,16,8,128]{3,2,1,0:T(8,128)S(1)}) custom-call(s32[2]{0:T(128)S(1)} %copy-done.11, bf16[2,16,2048]{2,1,0:T(8,128)(2,1)S(1)} %copy-done.5, bf16[2,16,2048]{2,1,0:T(8,128)(2,1)S(1)} %copy-done.6, ...), custom_call_target="tpu_custom_call" | custom-call | tf_op jit(solution)/shard_map/prep0/pallas_call | solution.py:294
  21.5 0.8 %collective-permute-done.4 = bf16[32,2432]{1,0:T(8,128)(2,1)S(1)} collective-permute-done((bf16[32,2432]{1,0:T(8,128)(2,1)S(1)}, bf16[32,2432]{1,0:T(8,128)(2,1)S(1)}, u32[]{:S(2)}, u32[]{:S(2)}) %collective-permute-start.4) | collective-permute-done | bytes 155680 | tf_op jit(solution)/shard_map/ppermute | solution.py:234
  22.2 1.1 %collective-permute-start.10 = (bf16[32,2432]{1,0:T(8,128)(2,1)S(1)}, bf16[32,2432]{1,0:T(8,128)(2,1)S(1)}, u32[]{:S(2)}, u32[]{:S(2)}) collective-permute-start(bf16[32,2432]{1,0:T(8,128)(2,1)S(1)} %collective-permute-done.4), channel_id=1, source_target_pairs={{0,2},{1,3},{2,0},{3,1},{4,6},{5,7},{6,4},{7,5},{8,10},{9,11},{10,... | collective-permute-start | bytes 466952 | tf_op jit(solution)/shard_map/ppermute | solution.py:234
  23.6 3.7 %prep1.1 = (bf16[2,16,64,128]{3,2,1,0:T(8,128)(2,1)S(1)}, f32[2,16,32,128]{3,2,1,0:T(8,128)S(1)}, bf16[2,16,48,128]{3,2,1,0:T(8,128)(2,1)S(1)}, f32[2,16,8,128]{3,2,1,0:T(8,128)S(1)}, bf16[2304,1024]{1,0:T(8,128)(2,1)S(1)}) custom-call(s32[2]{0:T(128)S(1)} %copy-done.11, ...), custom_call_target="tpu_custom_call", output_to_operand_aliasing={{0}: (7, {}), {1}: (8, {}), {2}: (9, {}), {3}: (10, {})} | custom-call | tf_op jit(solution)/shard_map/prep1/pallas_call | solution.py:294
  27.3 1.3 %collective-permute-done.2 = bf16[2,512,128]{2,1,0:T(8,128)(2,1)S(1)} collective-permute-done((bf16[2,512,128]{2,1,0:T(8,128)(2,1)S(1)}, bf16[2,512,128]{2,1,0:T(8,128)(2,1)S(1)}, u32[]{:S(2)}, u32[]{:S(2)}) %collective-permute-start.2) | collective-permute-done | bytes 262176 | tf_op jit(solution)/shard_map/ppermute | solution.py:234
  29.3 1.6 %collective-permute-done.10 = bf16[32,2432]{1,0:T(8,128)(2,1)S(1)} collective-permute-done((bf16[32,2432]{1,0:T(8,128)(2,1)S(1)}, bf16[32,2432]{1,0:T(8,128)(2,1)S(1)}, u32[]{:S(2)}, u32[]{:S(2)}) %collective-permute-start.10) | collective-permute-done | bytes 155680 | tf_op jit(solution)/shard_map/ppermute | solution.py:234
  31.1 1.4 %fusion.6 = f32[256,1024]{1,0:T(8,128)S(1)} fusion(bf16[2304,1024]{1,0:T(8,128)(2,1)S(1)} %get-tuple-element.59, bf16[256,2432]{1,0:T(8,128)(2,1)S(1)} %constant_dynamic-update-slice_fusion), kind=kOutput, calls=%fused_computation.10 | convolution fusion | flops 1207959552 | bytes 6946816 | tf_op jit(solution)/shard_map/dot_general | solution.py:353
  32.7 0.9 %fusion = bf16[256,2304]{1,0:T(8,128)(2,1)S(1)} fusion(bf16[1,512,2304]{2,1,0:T(8,128)(2,1)S(1)} %copy-done, f32[256]{0:T(256)S(1)} %fusion.23, f32[256,1024]{1,0:T(8,128)S(1)} %fusion.6), kind=kOutput, calls=%fused_computation.2 | convolution fusion | flops 605945856 | bytes 4588544 | tf_op jit(solution)/shard_map/dot_general | solution.py:355
  34.2 1.1 %collective-permute-start.11 = (bf16[1,512,128]{2,1,0:T(8,128)(2,1)S(1)}, bf16[1,512,128]{2,1,0:T(8,128)(2,1)S(1)}, u32[]{:S(2)}, u32[]{:S(2)}) collective-permute-start(bf16[1,512,128]{2,1,0:T(8,128)(2,1)S(1)} %broadcast_select_fusion.5), channel_id=1, source_target_pairs={{0,12},{1,13},{2,14},{3,15},{4,8},{5,9},{6,10},{7,11},{8,4},{9,5},... | collective-permute-start | bytes 393224 | tf_op jit(solution)/shard_map/ppermute | solution.py:234
  35.4 1.4 %fusion.4 = f32[256,1024]{1,0:T(8,128)S(1)} fusion(bf16[2304,1024]{1,0:T(8,128)(2,1)S(1)} %get-tuple-element.59, bf16[256,2432]{1,0:T(8,128)(2,1)S(1)} %constant_dynamic-update-slice_fusion.9), kind=kOutput, calls=%fused_computation.8 | convolution fusion | flops 1207959552 | bytes 6946816 | tf_op jit(solution)/shard_map/dot_general | solution.py:353
  37.0 0.9 %fusion.1 = bf16[256,2304]{1,0:T(8,128)(2,1)S(1)} fusion(bf16[1,512,2304]{2,1,0:T(8,128)(2,1)S(1)} %copy-done, f32[256]{0:T(256)S(1)} %fusion.21, f32[256,1024]{1,0:T(8,128)S(1)} %fusion.4), kind=kOutput, calls=%fused_computation.3 | convolution fusion | flops 605945856 | bytes 4588544 | tf_op jit(solution)/shard_map/dot_general | solution.py:355
  38.2 1.7 %collective-permute-done.13 = bf16[128,2304]{1,0:T(8,128)(2,1)S(1)} collective-permute-done((bf16[128,2304]{1,0:T(8,128)(2,1)S(1)}, bf16[128,2304]{1,0:T(8,128)(2,1)S(1)}, u32[]{:S(2)}, u32[]{:S(2)}) %collective-permute-start.13) | collective-permute-done | bytes 589856 | tf_op jit(solution)/shard_map/ppermute | solution.py:234
  40.2 1.6 %collective-permute-start.19 = (bf16[32,2304]{1,0:T(8,128)(2,1)S(1)}, bf16[32,2304]{1,0:T(8,128)(2,1)S(1)}, u32[]{:S(2)}, u32[]{:S(2)}) collective-permute-start(bf16[32,2304]{1,0:T(8,128)(2,1)S(1)} %get-tuple-element.72), channel_id=1, source_target_pairs={{0,2},{1,3},{2,0},{3,1},{4,6},{5,7},{6,4},{7,5},{8,10},{9,11},{10,... | collective-permute-start | bytes 442376 | tf_op jit(solution)/shard_map/ppermute | solution.py:234
  43.0 3.9 %collective-permute-done.19 = bf16[32,2304]{1,0:T(8,128)(2,1)S(1)} collective-permute-done((bf16[32,2304]{1,0:T(8,128)(2,1)S(1)}, bf16[32,2304]{1,0:T(8,128)(2,1)S(1)}, u32[]{:S(2)}, u32[]{:S(2)}) %collective-permute-start.19) | collective-permute-done | bytes 147488 | tf_op jit(solution)/shard_map/ppermute | solution.py:234
  47.6 1.4 %collective-permute-start.15 = (bf16[2,512,128]{2,1,0:T(8,128)(2,1)S(1)}, bf16[2,512,128]{2,1,0:T(8,128)(2,1)S(1)}, u32[]{:S(2)}, u32[]{:S(2)}) collective-permute-start(bf16[2,512,128]{2,1,0:T(8,128)(2,1)S(1)} %get-tuple-element.76), channel_id=1, source_target_pairs={{0,2},{1,3},{2,0},{3,1},{4,6},{5,7},{6,4},{7,5},{8,10},{9,11},{10,... | collective-permute-start | bytes 786440 | tf_op jit(solution)/shard_map/ppermute | solution.py:234
  49.0 1.8 %collective-permute-start.20 = (bf16[32,2304]{1,0:T(8,128)(2,1)S(1)}, bf16[32,2304]{1,0:T(8,128)(2,1)S(1)}, u32[]{:S(2)}, u32[]{:S(2)}) collective-permute-start(bf16[32,2304]{1,0:T(8,128)(2,1)S(1)} %slice.137), channel_id=1, source_target_pairs={{0,4},{1,5},{2,6},{3,7},{4,0},{5,1},{6,2},{7,3},{8,12},{9,13},{10,... | collective-permute-start | bytes 442376 | tf_op jit(solution)/shard_map/ppermute | solution.py:234
  50.8 2.4 %collective-permute-done.23 = bf16[32,2304]{1,0:T(8,128)(2,1)S(1)} collective-permute-done((bf16[32,2304]{1,0:T(8,128)(2,1)S(1)}, bf16[32,2304]{1,0:T(8,128)(2,1)S(1)}, u32[]{:S(2)}, u32[]{:S(2)}) %collective-permute-start.23) | collective-permute-done | bytes 147488 | tf_op jit(solution)/shard_map/ppermute | solution.py:234
  53.3 2.4 %collective-permute-start.24 = (bf16[32,2304]{1,0:T(8,128)(2,1)S(1)}, bf16[32,2304]{1,0:T(8,128)(2,1)S(1)}, u32[]{:S(2)}, u32[]{:S(2)}) collective-permute-start(bf16[32,2304]{1,0:T(8,128)(2,1)S(1)} %fusion.12), channel_id=1, source_target_pairs={{0,12},{1,13},{2,14},{3,15},{4,8},{5,9},{6,10},{7,11},{8,4},{9,5},... | collective-permute-start | bytes 442376 | tf_op jit(solution)/shard_map/ppermute | solution.py:234
  56.0 1.0 %collective-permute-start.21 = (bf16[32,2304]{1,0:T(8,128)(2,1)S(1)}, bf16[32,2304]{1,0:T(8,128)(2,1)S(1)}, u32[]{:S(2)}, u32[]{:S(2)}) collective-permute-start(bf16[32,2304]{1,0:T(8,128)(2,1)S(1)} %add_convert_fusion.1), channel_id=1, source_target_pairs={{0,2},{1,3},{2,0},{3,1},{4,6},{5,7},{6,4},{7,5},{8,10},{9,11},{10,... | collective-permute-start | bytes 442376 | tf_op jit(solution)/shard_map/ppermute | solution.py:234
  56.9 0.9 %collective-permute-done.16.other = bf16[4,512,128]{2,1,0:T(8,128)(2,1)S(1)} collective-permute-done((bf16[4,512,128]{2,1,0:T(8,128)(2,1)S(1)}, bf16[4,512,128]{2,1,0:T(8,128)(2,1)S(1)}, u32[]{:S(2)}, u32[]{:S(2)}) %collective-permute-start.16) | collective-permute-done | bytes 524320 | tf_op jit(solution)/shard_map/ppermute | solution.py:234
  57.8 3.6 %finish.1 = (f32[2,16,128,128]{3,2,1,0:T(8,128)}, bf16[2,16,2048]{2,1,0:T(8,128)(2,1)}) custom-call(s32[2,2]{1,0:T(2,128)S(1)} %copy-done.10, s32[1]{0:T(128)} %bitcast.where_at, f32[2,16,128,128]{3,2,1,0:T(8,128)S(1)} %copy-done.2, bf16[4,512,128]{2,1,0:T(8,128)(2,1)S(1)} %get-tuple-element.74.mine, bf16[4,512,128]{2,1,0:T(8,128)(2,1)S(1)} %collective-permute-done.1.near, ...), custom_call_target="tpu_custom_call" | custom-call | tf_op jit(solution)/shard_map/finish/pallas_call | solution.py:422
  61.4 0.8 %collective-permute-done.21 = bf16[32,2304]{1,0:T(8,128)(2,1)S(1)} collective-permute-done((bf16[32,2304]{1,0:T(8,128)(2,1)S(1)}, bf16[32,2304]{1,0:T(8,128)(2,1)S(1)}, u32[]{:S(2)}, u32[]{:S(2)}) %collective-permute-start.21) | collective-permute-done | bytes 147488 | tf_op jit(solution)/shard_map/ppermute | solution.py:234
  62.3 0.7 %fusion.15 = bf16[32,2304]{1,0:T(8,128)(2,1)} fusion(f32[128,2304]{1,0:T(8,128)S(1)} %convert_add_fusion, bf16[32,2304]{1,0:T(8,128)(2,1)S(1)} %collective-permute-done.24, bf16[32,2304]{1,0:T(8,128)(2,1)S(1)} %collective-permute-done.21, bf16[32,2304]{1,0:T(8,128)(2,1)S(1)} %collective-permute-done.18), kind=kLoop, calls=%fused_computation.29 | loop fusion | flops 516096 | bytes 884736 | tf_op jit(solution)/shard_map/convert_element_type | solution.py:441
  (89 shorter events, 6.5 us)
Async XLA Ops:
  0.6 32.0 %copy-start = (bf16[1,512,2304]{2,1,0:T(8,128)(2,1)S(1)}, bf16[1,512,2304]{2,1,0:T(8,128)(2,1)}, u32[]{:S(2)}) copy-start(bf16[1,512,2304]{2,1,0:T(8,128)(2,1)} %param.25) | copy-start | bytes 7077892
  2.5 12.1 %collective-permute-start = (bf16[32,2432]{1,0:T(8,128)(2,1)}, bf16[32,2432]{1,0:T(8,128)(2,1)S(1)}, u32[]{:S(2)}, u32[]{:S(2)}) collective-permute-start(bf16[32,2432]{1,0:T(8,128)(2,1)} %rows.1), channel_id=1, source_target_pairs={{0,12},{1,13},{2,14},{3,15},{4,8},{5,9},{6,10},{7,11},{8,4},{9,5},... | collective-permute-start | bytes 466952 | tf_op jit(solution)/shard_map/ppermute | solution.py:234
  7.5 5.7 %collective-permute-start.8 = (bf16[32,2432]{1,0:T(8,128)(2,1)}, bf16[32,2432]{1,0:T(8,128)(2,1)S(1)}, u32[]{:S(2)}, u32[]{:S(2)}) collective-permute-start(bf16[32,2432]{1,0:T(8,128)(2,1)} %rows.1), channel_id=1, source_target_pairs={{0,2},{1,3},{2,0},{3,1},{4,6},{5,7},{6,4},{7,5},{8,10},{9,11},{10,... | collective-permute-start | bytes 466952 | tf_op jit(solution)/shard_map/ppermute | solution.py:234
  9.0 9.2 %collective-permute-start.6 = (bf16[32,2432]{1,0:T(8,128)(2,1)}, bf16[32,2432]{1,0:T(8,128)(2,1)S(1)}, u32[]{:S(2)}, u32[]{:S(2)}) collective-permute-start(bf16[32,2432]{1,0:T(8,128)(2,1)} %rows.1), channel_id=1, source_target_pairs={{0,4},{1,5},{2,6},{3,7},{4,0},{5,1},{6,2},{7,3},{8,12},{9,13},{10,... | collective-permute-start | bytes 466952 | tf_op jit(solution)/shard_map/ppermute | solution.py:234
  12.0 2.4 %collective-permute-start.1 = (bf16[4,512,128]{2,1,0:T(8,128)(2,1)S(1)}, bf16[4,512,128]{2,1,0:T(8,128)(2,1)S(1)}, u32[]{:S(2)}, u32[]{:S(2)}) collective-permute-start(bf16[4,512,128]{2,1,0:T(8,128)(2,1)S(1)} %get-tuple-element.39), channel_id=1, source_target_pairs={{0,1},{1,0},{2,3},{3,2},{4,5},{5,4},{6,7},{7,6},{8,9},{9,8},{10,11... | collective-permute-start | bytes 1572872 | tf_op jit(solution)/shard_map/ppermute | solution.py:234
  13.2 10.3 %collective-permute-start.9 = (bf16[32,2432]{1,0:T(8,128)(2,1)S(1)}, bf16[32,2432]{1,0:T(8,128)(2,1)S(1)}, u32[]{:S(2)}, u32[]{:S(2)}) collective-permute-start(bf16[32,2432]{1,0:T(8,128)(2,1)S(1)} %collective-permute-done.8), channel_id=1, source_target_pairs={{0,4},{1,5},{2,6},{3,7},{4,0},{5,1},{6,2},{7,3},{8,12},{9,13},{10,... | collective-permute-start | bytes 466952 | tf_op jit(solution)/shard_map/ppermute | solution.py:234
  14.4 3.9 %copy-start.5 = (bf16[2,16,2048]{2,1,0:T(8,128)(2,1)S(1)}, bf16[2,16,2048]{2,1,0:T(8,128)(2,1)}, u32[]{:S(2)}) copy-start(bf16[2,16,2048]{2,1,0:T(8,128)(2,1)} %refs_0_.1) | copy-start | bytes 393220
  14.4 3.9 %copy-start.6 = (bf16[2,16,2048]{2,1,0:T(8,128)(2,1)S(1)}, bf16[2,16,2048]{2,1,0:T(8,128)(2,1)}, u32[]{:S(2)}) copy-start(bf16[2,16,2048]{2,1,0:T(8,128)(2,1)} %refs_1_.1) | copy-start | bytes 393220
  14.4 3.9 %copy-start.7 = (bf16[2,16,2048]{2,1,0:T(8,128)(2,1)S(1)}, bf16[2,16,2048]{2,1,0:T(8,128)(2,1)}, u32[]{:S(2)}) copy-start(bf16[2,16,2048]{2,1,0:T(8,128)(2,1)} %refs_2_.1) | copy-start | bytes 393220
  14.4 3.9 %copy-start.8 = (f32[2,16,16]{2,1,0:T(8,128)S(1)}, f32[2,16,16]{2,1,0:T(8,128)}, u32[]{:S(2)}) copy-start(f32[2,16,16]{2,1,0:T(8,128)} %refs_4_.1) | copy-start | bytes 6148
  14.4 3.9 %copy-start.11 = (s32[2]{0:T(128)S(1)}, s32[2]{0:T(128)}, u32[]{:S(2)}) copy-start(s32[2]{0:T(128)} %counts.1) | copy-start | bytes 28
  14.5 9.2 %copy-start.3 = (bf16[1,2304,1024]{2,1,0:T(8,128)(2,1)S(1)}, bf16[1,2304,1024]{2,1,0:T(8,128)(2,1)}, u32[]{:S(2)}) copy-start(bf16[1,2304,1024]{2,1,0:T(8,128)(2,1)} %param.24) | copy-start | bytes 14155780
  14.5 7.7 %collective-permute-start.4 = (bf16[32,2432]{1,0:T(8,128)(2,1)S(1)}, bf16[32,2432]{1,0:T(8,128)(2,1)S(1)}, u32[]{:S(2)}, u32[]{:S(2)}) collective-permute-start(bf16[32,2432]{1,0:T(8,128)(2,1)S(1)} %collective-permute-done), channel_id=1, source_target_pairs={{0,4},{1,5},{2,6},{3,7},{4,0},{5,1},{6,2},{7,3},{8,12},{9,13},{10,... | collective-permute-start | bytes 466952 | tf_op jit(solution)/shard_map/ppermute | solution.py:234
  16.1 7.4 %collective-permute-start.3 = (bf16[32,2432]{1,0:T(8,128)(2,1)S(1)}, bf16[32,2432]{1,0:T(8,128)(2,1)S(1)}, u32[]{:S(2)}, u32[]{:S(2)}) collective-permute-start(bf16[32,2432]{1,0:T(8,128)(2,1)S(1)} %collective-permute-done), channel_id=1, source_target_pairs={{0,2},{1,3},{2,0},{3,1},{4,6},{5,7},{6,4},{7,5},{8,10},{9,11},{10,... | collective-permute-start | bytes 466952 | tf_op jit(solution)/shard_map/ppermute | solution.py:234
  17.0 11.6 %collective-permute-start.2 = (bf16[2,512,128]{2,1,0:T(8,128)(2,1)S(1)}, bf16[2,512,128]{2,1,0:T(8,128)(2,1)S(1)}, u32[]{:S(2)}, u32[]{:S(2)}) collective-permute-start(bf16[2,512,128]{2,1,0:T(8,128)(2,1)S(1)} %slice.109), channel_id=1, source_target_pairs={{0,2},{1,3},{2,0},{3,1},{4,6},{5,7},{6,4},{7,5},{8,10},{9,11},{10,... | collective-permute-start | bytes 786440 | tf_op jit(solution)/shard_map/ppermute | solution.py:234
  22.2 8.6 %collective-permute-start.10 = (bf16[32,2432]{1,0:T(8,128)(2,1)S(1)}, bf16[32,2432]{1,0:T(8,128)(2,1)S(1)}, u32[]{:S(2)}, u32[]{:S(2)}) collective-permute-start(bf16[32,2432]{1,0:T(8,128)(2,1)S(1)} %collective-permute-done.4), channel_id=1, source_target_pairs={{0,2},{1,3},{2,0},{3,1},{4,6},{5,7},{6,4},{7,5},{8,10},{9,11},{10,... | collective-permute-start | bytes 466952 | tf_op jit(solution)/shard_map/ppermute | solution.py:234
  23.4 7.5 %collective-permute-start.7 = (bf16[128,2432]{1,0:T(8,128)(2,1)S(1)}, bf16[128,2432]{1,0:T(8,128)(2,1)S(1)}, u32[]{:S(2)}, u32[]{:S(2)}) collective-permute-start(bf16[128,2432]{1,0:T(8,128)(2,1)S(1)} %pad_maximum_fusion), channel_id=1, source_target_pairs={{0,1},{1,0},{2,3},{3,2},{4,5},{5,4},{6,7},{7,6},{8,9},{9,8},{10,11... | collective-permute-start | bytes 1867784 | tf_op jit(solution)/shard_map/ppermute | solution.py:234
  28.7 5.4 %collective-permute-start.5 = (bf16[1,512,128]{2,1,0:T(8,128)(2,1)S(1)}, bf16[1,512,128]{2,1,0:T(8,128)(2,1)S(1)}, u32[]{:S(2)}, u32[]{:S(2)}) collective-permute-start(bf16[1,512,128]{2,1,0:T(8,128)(2,1)S(1)} %slice.141), channel_id=1, source_target_pairs={{0,4},{1,5},{2,6},{3,7},{4,0},{5,1},{6,2},{7,3},{8,12},{9,13},{10,... | collective-permute-start | bytes 393224 | tf_op jit(solution)/shard_map/ppermute | solution.py:234
  30.9 4.4 %collective-permute-start.12 = (bf16[128,2432]{1,0:T(8,128)(2,1)S(1)}, bf16[128,2432]{1,0:T(8,128)(2,1)S(1)}, u32[]{:S(2)}, u32[]{:S(2)}) collective-permute-start(bf16[128,2432]{1,0:T(8,128)(2,1)S(1)} %get-tuple-element.78), channel_id=1, source_target_pairs={{0,1},{1,0},{2,3},{3,2},{4,5},{5,4},{6,7},{7,6},{8,9},{9,8},{10,11... | collective-permute-start | bytes 1867784 | tf_op jit(solution)/shard_map/ppermute | solution.py:234
  33.6 4.4 %collective-permute-start.17 = (bf16[128,2304]{1,0:T(8,128)(2,1)S(1)}, bf16[128,2304]{1,0:T(8,128)(2,1)S(1)}, u32[]{:S(2)}, u32[]{:S(2)}) collective-permute-start(bf16[128,2304]{1,0:T(8,128)(2,1)S(1)} %slice.154), channel_id=1, source_target_pairs={{0,1},{1,0},{2,3},{3,2},{4,5},{5,4},{6,7},{7,6},{8,9},{9,8},{10,11... | collective-permute-start | bytes 1769480 | tf_op jit(solution)/shard_map/ppermute | solution.py:234
  34.2 8.1 %collective-permute-start.11 = (bf16[1,512,128]{2,1,0:T(8,128)(2,1)S(1)}, bf16[1,512,128]{2,1,0:T(8,128)(2,1)S(1)}, u32[]{:S(2)}, u32[]{:S(2)}) collective-permute-start(bf16[1,512,128]{2,1,0:T(8,128)(2,1)S(1)} %broadcast_select_fusion.5), channel_id=1, source_target_pairs={{0,12},{1,13},{2,14},{3,15},{4,8},{5,9},{6,10},{7,11},{8,4},{9,5},... | collective-permute-start | bytes 393224 | tf_op jit(solution)/shard_map/ppermute | solution.py:234
  37.9 2.1 %collective-permute-start.13 = (bf16[128,2304]{1,0:T(8,128)(2,1)S(1)}, bf16[128,2304]{1,0:T(8,128)(2,1)S(1)}, u32[]{:S(2)}, u32[]{:S(2)}) collective-permute-start(bf16[128,2304]{1,0:T(8,128)(2,1)S(1)} %slice.152), channel_id=1, source_target_pairs={{0,1},{1,0},{2,3},{3,2},{4,5},{5,4},{6,7},{7,6},{8,9},{9,8},{10,11... | collective-permute-start | bytes 1769480 | tf_op jit(solution)/shard_map/ppermute | solution.py:234
  38.1 23.3 %collective-permute-start.18 = (bf16[32,2304]{1,0:T(8,128)(2,1)S(1)}, bf16[32,2304]{1,0:T(8,128)(2,1)S(1)}, u32[]{:S(2)}, u32[]{:S(2)}) collective-permute-start(bf16[32,2304]{1,0:T(8,128)(2,1)S(1)} %slice.220), channel_id=1, source_target_pairs={{0,4},{1,5},{2,6},{3,7},{4,0},{5,1},{6,2},{7,3},{8,12},{9,13},{10,... | collective-permute-start | bytes 442376 | tf_op jit(solution)/shard_map/ppermute | solution.py:234
  40.2 6.8 %collective-permute-start.19 = (bf16[32,2304]{1,0:T(8,128)(2,1)S(1)}, bf16[32,2304]{1,0:T(8,128)(2,1)S(1)}, u32[]{:S(2)}, u32[]{:S(2)}) collective-permute-start(bf16[32,2304]{1,0:T(8,128)(2,1)S(1)} %get-tuple-element.72), channel_id=1, source_target_pairs={{0,2},{1,3},{2,0},{3,1},{4,6},{5,7},{6,4},{7,5},{8,10},{9,11},{10,... | collective-permute-start | bytes 442376 | tf_op jit(solution)/shard_map/ppermute | solution.py:234
  41.8 9.0 %collective-permute-start.22 = (bf16[32,2304]{1,0:T(8,128)(2,1)S(1)}, bf16[32,2304]{1,0:T(8,128)(2,1)S(1)}, u32[]{:S(2)}, u32[]{:S(2)}) collective-permute-start(bf16[32,2304]{1,0:T(8,128)(2,1)S(1)} %get-tuple-element.71), channel_id=1, source_target_pairs={{0,2},{1,3},{2,0},{3,1},{4,6},{5,7},{6,4},{7,5},{8,10},{9,11},{10,... | collective-permute-start | bytes 442376 | tf_op jit(solution)/shard_map/ppermute | solution.py:234
  42.3 5.2 %collective-permute-start.14 = (bf16[1,512,128]{2,1,0:T(8,128)(2,1)S(1)}, bf16[1,512,128]{2,1,0:T(8,128)(2,1)S(1)}, u32[]{:S(2)}, u32[]{:S(2)}) collective-permute-start(bf16[1,512,128]{2,1,0:T(8,128)(2,1)S(1)} %get-tuple-element.86), channel_id=1, source_target_pairs={{0,4},{1,5},{2,6},{3,7},{4,0},{5,1},{6,2},{7,3},{8,12},{9,13},{10,... | collective-permute-start | bytes 393224 | tf_op jit(solution)/shard_map/ppermute | solution.py:234
  47.0 6.3 %collective-permute-start.23 = (bf16[32,2304]{1,0:T(8,128)(2,1)S(1)}, bf16[32,2304]{1,0:T(8,128)(2,1)S(1)}, u32[]{:S(2)}, u32[]{:S(2)}) collective-permute-start(bf16[32,2304]{1,0:T(8,128)(2,1)S(1)} %fusion.10), channel_id=1, source_target_pairs={{0,4},{1,5},{2,6},{3,7},{4,0},{5,1},{6,2},{7,3},{8,12},{9,13},{10,... | collective-permute-start | bytes 442376 | tf_op jit(solution)/shard_map/ppermute | solution.py:234
  47.6 8.1 %collective-permute-start.15 = (bf16[2,512,128]{2,1,0:T(8,128)(2,1)S(1)}, bf16[2,512,128]{2,1,0:T(8,128)(2,1)S(1)}, u32[]{:S(2)}, u32[]{:S(2)}) collective-permute-start(bf16[2,512,128]{2,1,0:T(8,128)(2,1)S(1)} %get-tuple-element.76), channel_id=1, source_target_pairs={{0,2},{1,3},{2,0},{3,1},{4,6},{5,7},{6,4},{7,5},{8,10},{9,11},{10,... | collective-permute-start | bytes 786440 | tf_op jit(solution)/shard_map/ppermute | solution.py:234
  49.0 6.9 %collective-permute-start.20 = (bf16[32,2304]{1,0:T(8,128)(2,1)S(1)}, bf16[32,2304]{1,0:T(8,128)(2,1)S(1)}, u32[]{:S(2)}, u32[]{:S(2)}) collective-permute-start(bf16[32,2304]{1,0:T(8,128)(2,1)S(1)} %slice.137), channel_id=1, source_target_pairs={{0,4},{1,5},{2,6},{3,7},{4,0},{5,1},{6,2},{7,3},{8,12},{9,13},{10,... | collective-permute-start | bytes 442376 | tf_op jit(solution)/shard_map/ppermute | solution.py:234
  53.3 8.1 %collective-permute-start.24 = (bf16[32,2304]{1,0:T(8,128)(2,1)S(1)}, bf16[32,2304]{1,0:T(8,128)(2,1)S(1)}, u32[]{:S(2)}, u32[]{:S(2)}) collective-permute-start(bf16[32,2304]{1,0:T(8,128)(2,1)S(1)} %fusion.12), channel_id=1, source_target_pairs={{0,12},{1,13},{2,14},{3,15},{4,8},{5,9},{6,10},{7,11},{8,4},{9,5},... | collective-permute-start | bytes 442376 | tf_op jit(solution)/shard_map/ppermute | solution.py:234
  55.8 2.0 %collective-permute-start.16 = (bf16[4,512,128]{2,1,0:T(8,128)(2,1)S(1)}, bf16[4,512,128]{2,1,0:T(8,128)(2,1)S(1)}, u32[]{:S(2)}, u32[]{:S(2)}) collective-permute-start(bf16[4,512,128]{2,1,0:T(8,128)(2,1)S(1)} %get-tuple-element.73), channel_id=1, source_target_pairs={{0,1},{1,0},{2,3},{3,2},{4,5},{5,4},{6,7},{7,6},{8,9},{9,8},{10,11... | collective-permute-start | bytes 1572872 | tf_op jit(solution)/shard_map/ppermute | solution.py:234
  56.0 6.3 %collective-permute-start.21 = (bf16[32,2304]{1,0:T(8,128)(2,1)S(1)}, bf16[32,2304]{1,0:T(8,128)(2,1)S(1)}, u32[]{:S(2)}, u32[]{:S(2)}) collective-permute-start(bf16[32,2304]{1,0:T(8,128)(2,1)S(1)} %add_convert_fusion.1), channel_id=1, source_target_pairs={{0,2},{1,3},{2,0},{3,1},{4,6},{5,7},{6,4},{7,5},{8,10},{9,11},{10,... | collective-permute-start | bytes 442376 | tf_op jit(solution)/shard_map/ppermute | solution.py:234
  (6 other events, 11.3 us)
